TPU v7x, 32 devices: a whole 2x2x4 slice. The times are simulated.
32 devices in a mesh: member: 2 (over y), lon: 4 (over x, core), lat: 4 (over z).
Axes of the slice: x: 2, y: 2, z: 4, core: 2. Of those that a mesh axis runs over, the one named last changes fastest.
Arguments:
- tracer: float32 [150, 128, 1024], P('member', 'lat', 'lon'), parts along dimension 0, may hold values from -6 to 6
- u_flow: float32 [150, 128, 1024], P('member', 'lat', 'lon'), parts along dimension 0, may hold values from -0.25 to 0.25
- v_flow: float32 [150, 128, 1024], P('member', 'lat', 'lon'), parts along dimension 0, may hold values from -0.25 to 0.25
- depth_levels: int32 [256, 1024], P(('member', 'lat'), 'lon'), parts along dimension 0, may hold values from 0 to 75
- class_index: int32 [150, 128, 1024], P('member', 'lat', 'lon'), parts along dimension 0, may hold values from 0 to 191
- basin_index: int32 [256, 1024], P(('member', 'lat'), 'lon'), parts along dimension 0, may hold values from 0 to 4
- level_thickness: float32 [75], replicated, may hold values from 0.5 to 2
Outputs:
- tracer_next: float32 [150, 128, 1024], P('member', 'lat', 'lon'), parts along dimension 0
- overturning: float32 [10, 128, 192], P('member', ('lat', 'lon')), parts along dimension 0
- tendency_sum: float32 [10, 128, 192], P('member', ('lat', 'lon')), parts along dimension 0
There are 2 independent parts, one for each index of `member`. A program takes and returns all parts, laid end to end along the dimension named above; an argument that names none is the same for every part. Nothing has to cross between parts.
All inputs are finite; a program needn't handle non-finite values.
Results may differ from a plain program's by a relative error of at most 0.0003.
Values sent between devices are 32-bit elements; how exact they have to be, the bound alone decides.
No kernel may reach another device: no remote copies, remote signals or barrier semaphores. Data moves between devices by JAX's collectives and lax.ppermute only.
A program may use at most 128 MiB of HBM per device.

v0:
```python
import math

import jax
import jax.numpy as jnp
from jax import lax
from jax.sharding import PartitionSpec as P

C = 192
B = 5


DIFFUSION = 0.1


def padded_2(array, sides, width):
    for axis, dim in sides:
        peers, length = (lax.axis_size(axis), array.shape[dim])
        up = [(i, (i + 1) % peers) for i in range(peers - 1)]
        down = [(j, i) for i, j in up]
        last = lax.slice_in_dim(array, length - width, length, axis=dim)
        initial = lax.slice_in_dim(array, 0, width, axis=dim)
        before = lax.ppermute(last, axis, up)
        after = lax.ppermute(initial, axis, down)
        array = jnp.concatenate([before, array, after], axis=dim)
    return array


def entering(array, axis, combine, identity):
    peers, index = (lax.axis_size(axis), lax.axis_index(axis))
    everything = lax.all_gather(array, axis)
    start = jnp.broadcast_to(jnp.asarray(identity, array.dtype), array.shape)

    def lap(k, before):
        reached = k < index
        new = combine(before, everything[k])
        return jnp.where(reached, new, before)

    return lax.fori_loop(0, peers, lap, start)


def face_fluxes(tracer_pad, speed_pad, wet_pad, length, along):

    def window(array, offset):
        return lax.slice_in_dim(array, offset, offset + length + 1, axis=along)

    behind = window(tracer_pad, 0)
    here = window(tracer_pad, 1)
    ahead = window(tracer_pad, 2)
    beyond = window(tracer_pad, 3)
    speed = window(speed_pad, 1)
    open_face = window(wet_pad, 1) * window(wet_pad, 2)
    advect = speed * (7.0 * (here + ahead) - (behind + beyond)) / 12.0
    upwind = jnp.abs(speed) * (beyond - 3.0 * ahead + 3.0 * here - behind) / 12.0
    return open_face * (advect + upwind - DIFFUSION * (ahead - here))


def divergence(fluxes, along):
    extent = fluxes.shape[along] - 1
    return lax.slice_in_dim(fluxes, 1, extent + 1, axis=along) - lax.slice_in_dim(
        fluxes, 0, extent, axis=along
    )


def add_terms(earlier, later):
    return earlier + later


def body(tracer, u_flow, v_flow, depth_levels, class_index, basin_index, level_thickness):
    level_count, row_count, col_count = tracer.shape
    lon_count = lax.axis_size("lon")
    level_ids = lax.broadcasted_iota(jnp.int32, (level_count, 1, 1), 0)
    wet = (level_ids < depth_levels[None]).astype(jnp.float32)
    masked = wet * tracer
    padded = padded_2(jnp.stack([masked, u_flow, v_flow]), (("lon", 3), ("lat", 2)), 2)
    tracer_pad = padded[0]
    east_pad = padded[1]
    north_pad = padded[2]
    depth_pad = jnp.pad(padded_2(depth_levels, (("lon", 1), ("lat", 0)), 1), 1)
    wet_pad = (level_ids < depth_pad[None]).astype(jnp.float32)
    zonal = face_fluxes(tracer_pad[:, 2:-2], east_pad[:, 2:-2], wet_pad[:, 2:-2], col_count, 2)
    merid = face_fluxes(
        tracer_pad[:, :, 2:-2], north_pad[:, :, 2:-2], wet_pad[:, :, 2:-2], row_count, 1
    )
    tracer_next = wet * (masked - divergence(zonal, 2) - divergence(merid, 1))
    thickness = level_thickness[:, None, None]
    transport = v_flow * wet * wet_pad[:, 3:-1, 2:-2] * thickness
    change = (tracer_next - masked) * thickness
    basin_ids = lax.broadcasted_iota(jnp.int32, (B, 1, 1), 0)
    basin_hot = (basin_index[None] == basin_ids).astype(jnp.float32)
    amounts = jnp.stack([transport, change])
    class_ids = lax.broadcasted_iota(jnp.int32, (C, 1, 1, 1), 0)
    block_rows = 2

    def bin_rows(block):
        first = block * block_rows
        amount_block = lax.dynamic_slice_in_dim(amounts, first, block_rows, 2)
        class_block = lax.dynamic_slice_in_dim(class_index, first, block_rows, 1)
        basin_block = lax.dynamic_slice_in_dim(basin_hot, first, block_rows, 1)
        weights = (amount_block[:, None] * basin_block[None, :, None]).reshape(
            2 * B, level_count, block_rows, col_count
        )
        onehot = (class_block[None] == class_ids).astype(jnp.float32)
        return jnp.einsum(
            "qkri,ckri->rqc",
            weights,
            onehot,
            precision=lax.Precision.HIGHEST,
            preferred_element_type=jnp.float32,
        )

    binned = lax.map(bin_rows, jnp.arange(row_count // block_rows, dtype=jnp.int32))
    binned = binned.reshape(row_count, 2, B, C).transpose(1, 2, 0, 3)
    upper = jnp.flip(jnp.cumsum(jnp.flip(binned[0], 2), axis=2), 2)
    running = jnp.cumsum(binned[1], axis=1)
    group_total = running[:, -1, :]
    carry = entering(group_total, "lat", add_terms, jnp.zeros_like(group_total))
    running = running + carry[:, None, :]
    unit = 1.0 / math.sqrt(col_count * lon_count * level_count)
    both = jnp.stack([upper * (16.0 * unit), running * (4.0 * unit)])
    whole = lax.psum(both, "lon")
    share = row_count // lon_count
    owned = lax.dynamic_slice_in_dim(whole, lax.axis_index("lon") * share, share, 2)
    return (tracer_next, owned[0], owned[1])


def solution(mesh):
    return jax.shard_map(
        body,
        mesh=mesh,
        in_specs=(
            P("member", "lat", "lon"),
            P("member", "lat", "lon"),
            P("member", "lat", "lon"),
            P(("member", "lat"), "lon"),
            P("member", "lat", "lon"),
            P(("member", "lat"), "lon"),
            P(),
        ),
        out_specs=(
            P("member", "lat", "lon"),
            P("member", ("lat", "lon"), None),
            P("member", ("lat", "lon"), None),
        ),
        check_vma=False,
    )
```

profile of v0, /device:TPU:0, one launch (start us, length us, event | category | flops | bytes accessed | tf_op | source)
XLA Modules:
  0.0 498.1 jit_solution(4399796061839733654)
XLA Ops:
  7.2 5.5 %copy.34 = f32[75,32,256]{0,1,2:T(8,128)} copy(f32[75,32,256]{2,1,0:T(8,128)} %param.11) | data formatting | bytes 4915200 | tf_op args[0]
  16.6 5.3 %copy.36 = f32[75,32,256]{0,1,2:T(8,128)} copy(f32[75,32,256]{2,1,0:T(8,128)} %param.12) | data formatting | bytes 4915200 | tf_op args[1]
  21.9 5.9 %fusion.17 = f32[1,75,32,256]{1,2,3,0:T(8,128)S(1)} fusion(f32[75,32,256]{0,1,2:T(8,128)} %copy.34, s32[32,256]{0,1:T(8,128)S(1)} %copy.33), kind=kLoop, calls=%fused_computation.36 | loop fusion | flops 1228800 | bytes 4947968 | tf_op jit(solution)/shard_map/stack | solution.py:74
  33.5 5.1 %collective-permute-start = (s32[32,1]{1,0:T(8,128)S(1)}, s32[32,1]{1,0:T(8,128)S(1)}, u32[]{:S(2)}, u32[]{:S(2)}) collective-permute-start(s32[32,1]{1,0:T(8,128)S(1)} %get-tuple-element.216), channel_id=1, source_target_pairs={{0,4},{4,8},{8,12},{1,5},{5,9},{9,13},{2,6},{6,10},{10,14},{3,7},{... | collective-permute-start | bytes 392 | tf_op jit(solution)/shard_map/ppermute | solution.py:22
  63.5 8.2 %collective-permute-done.6 = f32[3,75,2,260]{3,2,1,0:T(2,128)S(1)} collective-permute-done((f32[3,75,2,260]{3,2,1,0:T(2,128)S(1)}, f32[3,75,2,260]{3,2,1,0:T(2,128)S(1)}, u32[]{:S(2)}, u32[]{:S(2)}) %collective-permute-start.6) | collective-permute-done | bytes 468032 | tf_op jit(solution)/shard_map/ppermute | solution.py:22
  72.4 4.8 collective-permute-done.7
  79.5 14.3 %pad_maximum_fusion = f32[3,75,36,260]{1,2,3,0:T(8,128)} fusion(f32[3,75,2,260]{1,2,3,0:T(2,128)S(1)} %copy.41, f32[3,75,32,2]{1,2,3,0:T(8,128)S(1)} %collective-permute-done.5, f32[1,75,32,256]{1,2,3,0:T(8,128)} %bitcast.67, f32[1,75,32,256]{1,2,3,0:T(8,128)} %bitcast.70, f32[1,75,32,256]{1,2,3,0:T(8,128)} %copy-done.2, ...), kind=kLoop, calls=%fused_computation.12 | loop fusion | flops 12636000 | bytes 16848000 | tf_op jit(solution)/shard_map/concatenate | solution.py:24
  93.8 10.4 %slice_bitcast_fusion.2 = (f32[75,36,260]{0,1,2:T(8,128)}, f32[75,36,260]{0,1,2:T(8,128)}, f32[75,36,260]{0,1,2:T(8,128)S(1)}) fusion(f32[3,75,36,260]{1,2,3,0:T(8,128)} %pad_maximum_fusion), kind=kLoop, calls=%fused_computation.16 | loop fusion | bytes 16848000 | tf_op jit(solution)/shard_map/squeeze | solution.py:76
  104.3 8.4 %fusion.10 = f32[75,32,257]{0,1,2:T(8,128)} fusion(f32[75,36,260]{0,1,2:T(8,128)S(1)} %bitcast.65, f32[75,36,260]{0,1,2:T(8,128)} %get-tuple-element.202, f32[75,36,260]{0,1,2:T(8,128)S(1)} %get-tuple-element.204), kind=kLoop, calls=%fused_computation.23 | loop fusion | flops 11719200 | bytes 19737600 | tf_op jit(solution)/shard_map/mul | solution.py:54
  112.7 8.5 %fusion.9 = f32[75,33,256]{0,1,2:T(8,128)} fusion(f32[75,36,260]{0,1,2:T(8,128)S(1)} %bitcast.65, f32[75,36,260]{0,1,2:T(8,128)} %get-tuple-element.203, f32[75,36,260]{0,1,2:T(8,128)S(1)} %get-tuple-element.204), kind=kLoop, calls=%fused_computation.20 | loop fusion | flops 12038400 | bytes 20275200 | tf_op jit(solution)/shard_map/mul | solution.py:54
  121.2 11.6 %multiply_bitcast_fusion = (f32[1,75,32,256]{1,2,3,0:T(8,128)S(1)}, f32[75,32,256]{0,1,2:T(8,128)}, f32[1,75,32,256]{1,2,3,0:T(8,128)S(1)}) fusion(f32[75,32,256]{0,1,2:T(8,128)} %copy.34, f32[75]{0:T(128)S(1)} %copy-done.7, s32[32,256]{0,1:T(8,128)S(1)} %copy.33, f32[75,33,256]{0,1,2:T(8,128)} %fusion.9, f32[75,32,257]{0,1,2:T(8,128)} %fusion.10, ...), kind=kLoop, calls=%fused_computation.33 | loop fusion | flops 7372800 | bytes 24609068 | tf_op jit(solution)/shard_map/stack | solution.py:90
  137.0 9.2 %copy.43 = f32[2,75,32,256]{3,2,1,0:T(8,128)} copy(f32[2,75,32,256]{1,2,3,0:T(8,128)} %pad_maximum_fusion.1) | data formatting | bytes 9830400
  146.2 294.3 %while.25 = (s32[]{:T(128)}, f32[16,2,10,192]{3,1,0,2:T(2,128)S(1)}, s32[16]{0:T(128)S(1)}, f32[2,75,32,256]{3,2,1,0:T(8,128)}, f32[5,32,256]{2,1,0:T(8,128)}, /...) while((s32[]{:T(128)}, f32[16,2,10,192]{3,1,0,2:T(2,128)S(1)}, ...), condition=%wide.region_1.2_spmd.clone, body=%wide.region_0.1_spmd.clone.sunk | while | flops 892492800 | bytes 4902063 | solution.py:111
  151.2 13.3 %fusion.25 = f32[1,2,10,192]{3,2,1,0:T(8,128)S(1)} fusion(s32[75,2,256]{2,0,1:T(8,128)S(1)} %copy.73, f32[10,75,2,256]{3,2,1,0:T(2,128)S(1)} %bitcast_multiply_fusion.2), kind=kOutput, calls=%fused_computation.6.clone.1 | convolution fusion | flops 892108800 | bytes 1704960 | tf_op jit(solution)/shard_map/while/body/eval_jaxpr/qkri,ckri->rqc/dot_general | solution.py:103
  169.6 13.3 %fusion.25 = f32[1,2,10,192]{3,2,1,0:T(8,128)S(1)} fusion(s32[75,2,256]{2,0,1:T(8,128)S(1)} %copy.73, f32[10,75,2,256]{3,2,1,0:T(2,128)S(1)} %bitcast_multiply_fusion.2), kind=kOutput, calls=%fused_computation.6.clone.1 | convolution fusion | flops 892108800 | bytes 1704960 | tf_op jit(solution)/shard_map/while/body/eval_jaxpr/qkri,ckri->rqc/dot_general | solution.py:103
  188.0 13.3 %fusion.25 = f32[1,2,10,192]{3,2,1,0:T(8,128)S(1)} fusion(s32[75,2,256]{2,0,1:T(8,128)S(1)} %copy.73, f32[10,75,2,256]{3,2,1,0:T(2,128)S(1)} %bitcast_multiply_fusion.2), kind=kOutput, calls=%fused_computation.6.clone.1 | convolution fusion | flops 892108800 | bytes 1704960 | tf_op jit(solution)/shard_map/while/body/eval_jaxpr/qkri,ckri->rqc/dot_general | solution.py:103
  206.4 13.3 %fusion.25 = f32[1,2,10,192]{3,2,1,0:T(8,128)S(1)} fusion(s32[75,2,256]{2,0,1:T(8,128)S(1)} %copy.73, f32[10,75,2,256]{3,2,1,0:T(2,128)S(1)} %bitcast_multiply_fusion.2), kind=kOutput, calls=%fused_computation.6.clone.1 | convolution fusion | flops 892108800 | bytes 1704960 | tf_op jit(solution)/shard_map/while/body/eval_jaxpr/qkri,ckri->rqc/dot_general | solution.py:103
  224.8 13.3 %fusion.25 = f32[1,2,10,192]{3,2,1,0:T(8,128)S(1)} fusion(s32[75,2,256]{2,0,1:T(8,128)S(1)} %copy.73, f32[10,75,2,256]{3,2,1,0:T(2,128)S(1)} %bitcast_multiply_fusion.2), kind=kOutput, calls=%fused_computation.6.clone.1 | convolution fusion | flops 892108800 | bytes 1704960 | tf_op jit(solution)/shard_map/while/body/eval_jaxpr/qkri,ckri->rqc/dot_general | solution.py:103
  243.2 13.3 %fusion.25 = f32[1,2,10,192]{3,2,1,0:T(8,128)S(1)} fusion(s32[75,2,256]{2,0,1:T(8,128)S(1)} %copy.73, f32[10,75,2,256]{3,2,1,0:T(2,128)S(1)} %bitcast_multiply_fusion.2), kind=kOutput, calls=%fused_computation.6.clone.1 | convolution fusion | flops 892108800 | bytes 1704960 | tf_op jit(solution)/shard_map/while/body/eval_jaxpr/qkri,ckri->rqc/dot_general | solution.py:103
  261.6 13.3 %fusion.25 = f32[1,2,10,192]{3,2,1,0:T(8,128)S(1)} fusion(s32[75,2,256]{2,0,1:T(8,128)S(1)} %copy.73, f32[10,75,2,256]{3,2,1,0:T(2,128)S(1)} %bitcast_multiply_fusion.2), kind=kOutput, calls=%fused_computation.6.clone.1 | convolution fusion | flops 892108800 | bytes 1704960 | tf_op jit(solution)/shard_map/while/body/eval_jaxpr/qkri,ckri->rqc/dot_general | solution.py:103
  280.0 13.3 %fusion.25 = f32[1,2,10,192]{3,2,1,0:T(8,128)S(1)} fusion(s32[75,2,256]{2,0,1:T(8,128)S(1)} %copy.73, f32[10,75,2,256]{3,2,1,0:T(2,128)S(1)} %bitcast_multiply_fusion.2), kind=kOutput, calls=%fused_computation.6.clone.1 | convolution fusion | flops 892108800 | bytes 1704960 | tf_op jit(solution)/shard_map/while/body/eval_jaxpr/qkri,ckri->rqc/dot_general | solution.py:103
  298.4 13.3 %fusion.25 = f32[1,2,10,192]{3,2,1,0:T(8,128)S(1)} fusion(s32[75,2,256]{2,0,1:T(8,128)S(1)} %copy.73, f32[10,75,2,256]{3,2,1,0:T(2,128)S(1)} %bitcast_multiply_fusion.2), kind=kOutput, calls=%fused_computation.6.clone.1 | convolution fusion | flops 892108800 | bytes 1704960 | tf_op jit(solution)/shard_map/while/body/eval_jaxpr/qkri,ckri->rqc/dot_general | solution.py:103
  316.7 13.3 %fusion.25 = f32[1,2,10,192]{3,2,1,0:T(8,128)S(1)} fusion(s32[75,2,256]{2,0,1:T(8,128)S(1)} %copy.73, f32[10,75,2,256]{3,2,1,0:T(2,128)S(1)} %bitcast_multiply_fusion.2), kind=kOutput, calls=%fused_computation.6.clone.1 | convolution fusion | flops 892108800 | bytes 1704960 | tf_op jit(solution)/shard_map/while/body/eval_jaxpr/qkri,ckri->rqc/dot_general | solution.py:103
  335.1 13.3 %fusion.25 = f32[1,2,10,192]{3,2,1,0:T(8,128)S(1)} fusion(s32[75,2,256]{2,0,1:T(8,128)S(1)} %copy.73, f32[10,75,2,256]{3,2,1,0:T(2,128)S(1)} %bitcast_multiply_fusion.2), kind=kOutput, calls=%fused_computation.6.clone.1 | convolution fusion | flops 892108800 | bytes 1704960 | tf_op jit(solution)/shard_map/while/body/eval_jaxpr/qkri,ckri->rqc/dot_general | solution.py:103
  353.5 13.3 %fusion.25 = f32[1,2,10,192]{3,2,1,0:T(8,128)S(1)} fusion(s32[75,2,256]{2,0,1:T(8,128)S(1)} %copy.73, f32[10,75,2,256]{3,2,1,0:T(2,128)S(1)} %bitcast_multiply_fusion.2), kind=kOutput, calls=%fused_computation.6.clone.1 | convolution fusion | flops 892108800 | bytes 1704960 | tf_op jit(solution)/shard_map/while/body/eval_jaxpr/qkri,ckri->rqc/dot_general | solution.py:103
  371.9 13.3 %fusion.25 = f32[1,2,10,192]{3,2,1,0:T(8,128)S(1)} fusion(s32[75,2,256]{2,0,1:T(8,128)S(1)} %copy.73, f32[10,75,2,256]{3,2,1,0:T(2,128)S(1)} %bitcast_multiply_fusion.2), kind=kOutput, calls=%fused_computation.6.clone.1 | convolution fusion | flops 892108800 | bytes 1704960 | tf_op jit(solution)/shard_map/while/body/eval_jaxpr/qkri,ckri->rqc/dot_general | solution.py:103
  390.3 13.3 %fusion.25 = f32[1,2,10,192]{3,2,1,0:T(8,128)S(1)} fusion(s32[75,2,256]{2,0,1:T(8,128)S(1)} %copy.73, f32[10,75,2,256]{3,2,1,0:T(2,128)S(1)} %bitcast_multiply_fusion.2), kind=kOutput, calls=%fused_computation.6.clone.1 | convolution fusion | flops 892108800 | bytes 1704960 | tf_op jit(solution)/shard_map/while/body/eval_jaxpr/qkri,ckri->rqc/dot_general | solution.py:103
  408.7 13.3 %fusion.25 = f32[1,2,10,192]{3,2,1,0:T(8,128)S(1)} fusion(s32[75,2,256]{2,0,1:T(8,128)S(1)} %copy.73, f32[10,75,2,256]{3,2,1,0:T(2,128)S(1)} %bitcast_multiply_fusion.2), kind=kOutput, calls=%fused_computation.6.clone.1 | convolution fusion | flops 892108800 | bytes 1704960 | tf_op jit(solution)/shard_map/while/body/eval_jaxpr/qkri,ckri->rqc/dot_general | solution.py:103
  427.1 13.3 %fusion.25 = f32[1,2,10,192]{3,2,1,0:T(8,128)S(1)} fusion(s32[75,2,256]{2,0,1:T(8,128)S(1)} %copy.73, f32[10,75,2,256]{3,2,1,0:T(2,128)S(1)} %bitcast_multiply_fusion.2), kind=kOutput, calls=%fused_computation.6.clone.1 | convolution fusion | flops 892108800 | bytes 1704960 | tf_op jit(solution)/shard_map/while/body/eval_jaxpr/qkri,ckri->rqc/dot_general | solution.py:103
  444.9 13.3 %all-gather = f32[20,1,192]{2,1,0:T(1,128)S(1)} all-gather(f32[5,1,192]{2,1,0:T(1,128)S(1)} %slice.199), channel_id=2, replica_groups=mesh['member'=2,'lon'=4,'lat'=4] {'lat'}, dimensions={0}, use_global_device_ids=true | all-gather | bytes 19200 | tf_op jit(solution)/shard_map/all_gather | solution.py:30
  459.3 5.0 %copy.48 = f32[75,32,256]{2,1,0:T(8,128)} copy(f32[75,32,256]{0,1,2:T(8,128)} %get-tuple-element.201) | data formatting | bytes 4915200
  464.3 25.6 %all-reduce.4.cloned.1.call-done = f32[2,5,32,192]{3,2,1,0:T(8,128)} async-done(((f32[2,5,32,192]{3,2,1,0:T(8,128)}), f32[2,5,32,192]{3,2,1,0:T(8,128)}) %all-reduce.4.cloned.1.call-update) | async-done | bytes 245776 | tf_op jit(solution)/shard_map/psum | solution.py:120
  (207 shorter events, 118.3 us)
Async XLA Ops:
  7.2 5.6 %copy-start.4 = (s32[32,256]{1,0:T(8,128)S(1)}, s32[32,256]{1,0:T(8,128)}, u32[]{:S(2)}) copy-start(s32[32,256]{1,0:T(8,128)} %param.14) | copy-start | bytes 98308
  7.2 5.6 %copy-start.3 = (f32[75,32,256]{2,1,0:T(8,128)S(1)}, f32[75,32,256]{2,1,0:T(8,128)}, u32[]{:S(2)}) copy-start(f32[75,32,256]{2,1,0:T(8,128)} %param.13) | copy-start | bytes 7372804
  7.2 482.7 %all-reduce.4.cloned.1.call-start = ((), (), s32[]{:S(2)}) async-start(), calls=%async_computation | async-start | bytes 655360 | tf_op jit(solution)/shard_map/psum | solution.py:120
  21.9 5.9 %copy-start = (f32[75,32,256]{0,1,2:T(8,128)S(1)}, f32[75,32,256]{0,1,2:T(8,128)}, u32[]{:S(2)}) copy-start(f32[75,32,256]{0,1,2:T(8,128)} %copy.37) | copy-start | bytes 7372804
  21.9 5.9 %copy-start.1 = (f32[75,32,256]{0,1,2:T(8,128)S(1)}, f32[75,32,256]{0,1,2:T(8,128)}, u32[]{:S(2)}) copy-start(f32[75,32,256]{0,1,2:T(8,128)} %copy.36) | copy-start | bytes 7372804
  27.8 2.0 copy-start.2
  27.8 12.2 %copy-start.6 = (s32[32,256]{1,0:T(8,128)S(1)}, s32[32,256]{1,0:T(8,128)}, u32[]{:S(2)}) copy-start(s32[32,256]{1,0:T(8,128)} %param.16) | copy-start | bytes 98308
  29.8 18.0 %collective-permute-start.4 = (f32[3,75,32,2]{1,2,3,0:T(8,128)S(1)}, f32[3,75,32,2]{1,2,3,0:T(8,128)S(1)}, u32[]{:S(2)}, u32[]{:S(2)}) collective-permute-start(f32[3,75,32,2]{1,2,3,0:T(8,128)S(1)} %get-tuple-element.207), channel_id=1, source_target_pairs={{0,4},{4,8},{8,12},{1,5},{5,9},{9,13},{2,6},{6,10},{10,14},{3,7},{... | collective-permute-start | bytes 172808 | tf_op jit(solution)/shard_map/ppermute | solution.py:22
  32.2 15.7 %collective-permute-start.5 = (f32[3,75,32,2]{1,2,3,0:T(8,128)S(1)}, f32[3,75,32,2]{1,2,3,0:T(8,128)S(1)}, u32[]{:S(2)}, u32[]{:S(2)}) collective-permute-start(f32[3,75,32,2]{1,2,3,0:T(8,128)S(1)} %get-tuple-element.208), channel_id=1, source_target_pairs={{4,0},{8,4},{12,8},{5,1},{9,5},{13,9},{6,2},{10,6},{14,10},{7,3},{... | collective-permute-start | bytes 172808 | tf_op jit(solution)/shard_map/ppermute | solution.py:23
  33.5 7.1 %collective-permute-start = (s32[32,1]{1,0:T(8,128)S(1)}, s32[32,1]{1,0:T(8,128)S(1)}, u32[]{:S(2)}, u32[]{:S(2)}) collective-permute-start(s32[32,1]{1,0:T(8,128)S(1)} %get-tuple-element.216), channel_id=1, source_target_pairs={{0,4},{4,8},{8,12},{1,5},{5,9},{9,13},{2,6},{6,10},{10,14},{3,7},{... | collective-permute-start | bytes 392 | tf_op jit(solution)/shard_map/ppermute | solution.py:22
  38.7 4.3 collective-permute-start.1
  43.1 15.9 %collective-permute-start.2 = (s32[1,258]{1,0:T(1,128)S(1)}, s32[1,258]{1,0:T(1,128)S(1)}, u32[]{:S(2)}, u32[]{:S(2)}) collective-permute-start(s32[1,258]{1,0:T(1,128)S(1)} %get-tuple-element.214), channel_id=1, source_target_pairs={{0,1},{1,2},{2,3},{4,5},{5,6},{6,7},{8,9},{9,10},{10,11},{12,13},{... | collective-permute-start | bytes 3104 | tf_op jit(solution)/shard_map/ppermute | solution.py:22
  46.5 12.4 %collective-permute-start.3 = (s32[1,258]{1,0:T(1,128)S(1)}, s32[1,258]{1,0:T(1,128)S(1)}, u32[]{:S(2)}, u32[]{:S(2)}) collective-permute-start(s32[1,258]{1,0:T(1,128)S(1)} %get-tuple-element.215), channel_id=1, source_target_pairs={{1,0},{2,1},{3,2},{5,4},{6,5},{7,6},{9,8},{10,9},{11,10},{13,12},{... | collective-permute-start | bytes 3104 | tf_op jit(solution)/shard_map/ppermute | solution.py:23
  52.2 19.5 %collective-permute-start.6 = (f32[3,75,2,260]{3,2,1,0:T(2,128)S(1)}, f32[3,75,2,260]{3,2,1,0:T(2,128)S(1)}, u32[]{:S(2)}, u32[]{:S(2)}) collective-permute-start(f32[3,75,2,260]{3,2,1,0:T(2,128)S(1)} %copy.38), channel_id=1, source_target_pairs={{0,1},{1,2},{2,3},{4,5},{5,6},{6,7},{8,9},{9,10},{10,11},{12,13},{... | collective-permute-start | bytes 1404008 | tf_op jit(solution)/shard_map/ppermute | solution.py:22
  57.5 19.8 %collective-permute-start.7 = (f32[3,75,2,260]{3,2,1,0:T(2,128)S(1)}, f32[3,75,2,260]{3,2,1,0:T(2,128)}, u32[]{:S(2)}, u32[]{:S(2)}) collective-permute-start(f32[3,75,2,260]{3,2,1,0:T(2,128)S(1)} %copy.39), channel_id=1, source_target_pairs={{1,0},{2,1},{3,2},{5,4},{6,5},{7,6},{9,8},{10,9},{11,10},{13,12},{... | collective-permute-start | bytes 1404008 | tf_op jit(solution)/shard_map/ppermute | solution.py:23
  79.5 24.7 %slice-start = ((s8[5324800]{0:T(1024)(128)(4,1)}), s8[4194304]{0:T(1024)(128)(4,1)S(1)}, s32[]{:S(2)}) async-start(s8[5324800]{0:T(1024)(128)(4,1)} %bitcast.64), calls=%async_computation.1 | async-start | bytes 8388608
  93.8 10.5 %slice-start.1 = ((s8[5324800]{0:T(1024)(128)(4,1)}), s8[1130496]{0:T(1024)(128)(4,1)S(1)}, s32[]{:S(2)}) async-start(s8[5324800]{0:T(1024)(128)(4,1)} %bitcast.64), calls=%async_computation.2 | async-start | bytes 2260992
  112.7 8.5 %copy-start.7 = (f32[75]{0:T(128)S(1)}, f32[75]{0:T(128)}, u32[]{:S(2)}) copy-start(f32[75]{0:T(128)} %param.17) | copy-start | bytes 904
  137.0 9.2 %copy-start.5 = (f32[16,2,10,192]{3,1,0,2:T(2,128)S(1)}, f32[16,2,10,192]{3,1,0,2:T(2,128)}, u32[]{:S(2)}) copy-start(f32[16,2,10,192]{3,1,0,2:T(2,128)} %custom-call.1) | copy-start | bytes 737284
Sparse Core Ops, SparseCore 0:
  459.4 30.4 all-reduce.3
where the time goes:
time: 501 us; the launch traced here: 498 us
  matrix products  213 us (43%)
  local copies, waits for them, and re-layouts  112 us (22%)
  other arithmetic  72.2 us (14%)
  waiting for transfers between devices  41 us (8%)
  starting transfers between devices  20.9 us (4%)
  between operations  14.4 us (3%)
  blocking collectives  13.3 us (3%)
  loops' own time  11.3 us (2%)
    dot_general x16, matrix products, bin_rows(): jnp.einsum('qkri,ckri->rqc', weights, onehot, precision=lax.Precision.HIG...  213 us
    unnamed x30, local copies, waits for them, and re-layouts  31.4 us
    psum x1, waiting for transfers between devices, body(): whole = lax.psum(both, 'lon')  25.6 us
    dynamic_slice x16, local copies, waits for them, and re-layouts, bin_rows(): amount_block = lax.dynamic_slice_in_dim(amounts, first, block_rows, 2)  22.4 us
    dynamic_slice x32, local copies, waits for them, and re-layouts, bin_rows(): class_block = lax.dynamic_slice_in_dim(class_index, first, block_rows, 1)  18.4 us
    mul x2, other arithmetic, face_fluxes(): return open_face * (advect + upwind - DIFFUSION * (ahead - here))  16.9 us
    another operation x2, other arithmetic, body(): amounts = jnp.stack([transport, change])  15.8 us
    ppermute x4, starting transfers between devices, padded_2(): before = lax.ppermute(last, axis, up)  15.5 us
  transfers between devices with their start and end apart: 9, of which 4 were waited for; matrix products, arithmetic and copies ran while one was open for 3% of the time, Pallas kernels for 0%

commit v1 on v0

v1 whole, which is shorter than its diff:
```python
import functools
import math

import jax
import jax.numpy as jnp
from jax import lax
from jax.experimental import pallas as pl
from jax.experimental.pallas import tpu as pltpu
from jax.sharding import PartitionSpec as P

C = 192
B = 5
DIFFUSION = 0.1

LANES = 128
SLOTS = 4
PER_TILE = LANES // SLOTS
LOW = 64
HIGH = C // LOW
HEADS = 16
VMEM = 56 << 20
F32 = jnp.float32
BF16 = jnp.bfloat16


def lane_ids(shape):
    return lax.broadcasted_iota(jnp.int32, shape, len(shape) - 1)


def row_ids(shape):
    return lax.broadcasted_iota(jnp.int32, shape, len(shape) - 2)


def pack_kernel(tracer_ref, east_ref, north_ref, depth_ref, lon_ref, up_ref, down_ref):
    levels, rows, cols = tracer_ref.shape
    tiles = pl.cdiv(levels, PER_TILE)
    lon_ref[...] = jnp.zeros_like(lon_ref)
    lanes = lane_ids((rows, LANES))

    def level(k, carry):
        masked = jnp.where(k < depth_ref[...], tracer_ref[k], 0.0)
        ends = jnp.where(lanes < LANES // 2, masked[:, :LANES], masked[:, cols - LANES :])
        slot = k % PER_TILE
        turned = pltpu.roll(ends, (SLOTS * slot + 2) % LANES, 1)
        tile = pl.ds(pl.multiple_of(k // PER_TILE * LANES, LANES), LANES)
        lon_ref[:, tile] = jnp.where(lanes // SLOTS == slot, turned, lon_ref[:, tile])
        speed = pltpu.roll(east_ref[k], (k + 1) % LANES, 1)
        last = pl.ds(tiles * LANES, LANES)
        lon_ref[:, last] = jnp.where(lanes == k, speed, lon_ref[:, last])
        here = pl.ds(k, 1)
        up_ref[0, here, :] = masked[rows - 2 : rows - 1]
        up_ref[1, here, :] = masked[rows - 1 : rows]
        up_ref[2, here, :] = north_ref[k, 7:8, :]
        down_ref[0, here, :] = masked[0:1]
        down_ref[1, here, :] = masked[1:2]
        return carry

    lax.fori_loop(0, levels, level, 0)
    depth = depth_ref[...].astype(F32)
    last = pl.ds(tiles * LANES, LANES)
    from_end = pltpu.roll(depth[:, cols - LANES :], LANES - 1, 1)
    from_start = pltpu.roll(depth[:, :LANES], LANES - 1, 1)
    lon_ref[:, last] = jnp.where(
        lanes == LANES - 2, from_end, jnp.where(lanes == LANES - 1, from_start, lon_ref[:, last])
    )
    up_ref[0, levels : levels + 1, :] = depth[rows - 1 : rows]
    down_ref[0, levels : levels + 1, :] = depth[0:1]


def pack(tracer, u_flow, v_flow, depth):
    levels, rows, cols = tracer.shape
    tiles = pl.cdiv(levels, PER_TILE)
    tall = (levels + 8) // 8 * 8
    return pl.pallas_call(
        pack_kernel,
        grid=(1,),
        in_specs=[
            pl.BlockSpec((levels, rows, cols), lambda i: (0, 0, 0)),
            pl.BlockSpec((levels, rows, LANES), lambda i: (0, 0, cols // LANES - 1)),
            pl.BlockSpec((levels, 8, cols), lambda i: (0, rows // 8 - 1, 0)),
            pl.BlockSpec((rows, cols), lambda i: (0, 0)),
        ],
        out_specs=[
            pl.BlockSpec((rows, (tiles + 1) * LANES), lambda i: (0, 0)),
            pl.BlockSpec((3, tall, cols), lambda i: (0, 0, 0)),
            pl.BlockSpec((2, tall, cols), lambda i: (0, 0, 0)),
        ],
        out_shape=[
            jax.ShapeDtypeStruct((rows, (tiles + 1) * LANES), F32),
            jax.ShapeDtypeStruct((3, tall, cols), F32),
            jax.ShapeDtypeStruct((2, tall, cols), F32),
        ],
        compiler_params=pltpu.CompilerParams(vmem_limit_bytes=VMEM),
        name="pack_edges",
    )(tracer, u_flow, v_flow, depth)


def face_flux(value, speed, closed, axis):
    extent = value.shape[axis]
    step = pltpu.roll(value, extent - 1, axis)
    pair = value + step
    slope = step - value
    back = pltpu.roll(slope, 1, axis)
    front = pltpu.roll(slope, extent - 1, axis)
    twelfth = speed * (1.0 / 12.0)
    advect = twelfth * (6.0 * pair + (back - front))
    upwind = jnp.abs(twelfth) * (front - 2.0 * slope + back)
    flux = advect + upwind - DIFFUSION * slope
    return jnp.where(closed, 0.0, flux)


def main_kernel(
    thick_ref, tracer_ref, east_ref, north_ref, class_ref, depth_ref, basin_ref,
    west_ref, far_ref, south_ref, ahead_ref,
    next_ref, bins_ref,
    edge_ref, zonal_ref, merid_ref, head_ref, flow_hi, flow_lo, gain_hi, gain_lo, head_key, low_key, sums_ref,
):
    chunk = pl.program_id(0)
    per, rows, cols = tracer_ref.shape
    levels = thick_ref.shape[0]
    tiles = pl.cdiv(levels, PER_TILE)
    last = tiles * LANES

    @pl.when(chunk == 0)
    def _():
        lanes = lane_ids((rows, last))
        edge_ref[...] = jnp.where(lanes % SLOTS < 2, west_ref[:, :last], far_ref[:, :last])
        depth = depth_ref[...].astype(F32)
        west = west_ref[:, last + LANES - 2 : last + LANES - 1]
        far = far_ref[:, last + LANES - 1 : last + LANES]
        side = lane_ids((rows, LANES))
        halo = jnp.where(side == 0, far, west)
        wide = jnp.concatenate([depth, halo], 1)
        zonal_ref[...] = jnp.minimum(wide, pltpu.roll(wide, cols + LANES - 1, 1)).astype(jnp.int32)
        ends = row_ids((8, cols))
        halo = jnp.where(ends == 0, ahead_ref[0, levels : levels + 1, :], south_ref[0, levels : levels + 1, :])
        tall = jnp.concatenate([depth, halo], 0)
        merid_ref[...] = jnp.minimum(tall, pltpu.roll(tall, rows + 7, 0)).astype(jnp.int32)
        head_ref[...] = basin_ref[...] * HIGH

    def level(q, carry):
        k = chunk * per + q
        depth = depth_ref[...]
        wet = k < depth
        masked = jnp.where(wet, tracer_ref[q], 0.0)
        thick = thick_ref[k]
        tile = pl.ds(pl.multiple_of(k // PER_TILE * LANES, LANES), LANES)
        slot = k % PER_TILE
        halo = pltpu.roll(edge_ref[:, tile], (2 * LANES - 2 - SLOTS * slot) % LANES, 1)
        speed_halo = pltpu.roll(west_ref[:, last:], LANES - 1 - k, 1)
        zonal = face_flux(
            jnp.concatenate([masked, halo], 1),
            jnp.concatenate([east_ref[q], speed_halo], 1),
            k >= zonal_ref[...],
            1,
        )
        zonal_div = (zonal - pltpu.roll(zonal, 1, 1))[:, :cols]
        here = pl.ds(k, 1)
        side = row_ids((8, cols))
        halo = jnp.where(
            side == 0,
            ahead_ref[0, here, :],
            jnp.where(
                side == 1, ahead_ref[1, here, :], jnp.where(side == 6, south_ref[0, here, :], south_ref[1, here, :])
            ),
        )
        speed_halo = jnp.broadcast_to(south_ref[2, here, :], (8, cols))
        north = north_ref[q]
        faces = merid_ref[...]
        merid = face_flux(
            jnp.concatenate([masked, halo], 0), jnp.concatenate([north, speed_halo], 0), k >= faces, 0
        )
        merid_div = (merid - pltpu.roll(merid, 1, 0))[:rows]
        updated = jnp.where(wet, masked - zonal_div - merid_div, 0.0)
        next_ref[q] = updated
        flow = jnp.where(k < faces[:rows], north * thick, 0.0)
        gain = (updated - masked) * thick
        upper = flow.astype(BF16).astype(F32)
        flow_hi[q] = upper
        flow_lo[q] = flow - upper
        upper = gain.astype(BF16).astype(F32)
        gain_hi[q] = upper
        gain_lo[q] = gain - upper
        classes = class_ref[q]
        head_key[q] = (head_ref[...] + classes // LOW).astype(F32)
        low_key[q] = (classes % LOW).astype(F32)
        return carry

    lax.fori_loop(0, per, level, 0)

    heads = row_ids((HEADS, cols)).astype(F32).astype(BF16)
    lows = row_ids((LOW, cols)).astype(F32).astype(BF16)
    ones = jnp.ones((LOW, cols), BF16)
    none = jnp.zeros((LOW, cols), BF16)
    unroll = 8

    def spread(ref, q, r, count):
        return jnp.broadcast_to(ref[q, pl.ds(r, 1), :], (count, cols)).astype(BF16)

    def bin_row(r):
        left, right = ([], [])
        for q in range(per):
            hot = spread(head_key, q, r, HEADS) == heads
            left.append(
                jnp.concatenate(
                    [
                        jnp.where(hot, spread(ref, q, r, HEADS), none[:HEADS])
                        for ref in (flow_hi, flow_lo, gain_hi, gain_lo)
                    ],
                    0,
                )
            )
            right.append(jnp.where(spread(low_key, q, r, LOW) == lows, ones, none))
        return lax.dot_general(
            jnp.concatenate(left, 1),
            jnp.concatenate(right, 1),
            (((1,), (1,)), ((), ())),
            preferred_element_type=F32,
        )

    def some_rows(start, carry):
        for p in range(unroll):
            r = start * unroll + p
            total = bin_row(r)
            sums_ref[r] = jnp.where(chunk == 0, total, total + sums_ref[r])
        return carry

    lax.fori_loop(0, rows // unroll, some_rows, 0)

    @pl.when(chunk == pl.num_programs(0) - 1)
    def _():
        def finish(r, running):
            total = sums_ref[r]
            flow = total[:HEADS] + total[HEADS : 2 * HEADS]
            running = running + total[2 * HEADS : 3 * HEADS] + total[3 * HEADS :]
            bins_ref[r] = jnp.concatenate([flow, running], 1)
            return running

        lax.fori_loop(0, rows, finish, jnp.zeros((HEADS, LOW), F32), unroll=4)


def step_and_bin(thick, tracer, u_flow, v_flow, classes, depth, basins, west, far, south, ahead):
    levels, rows, cols = tracer.shape
    per = next(n for n in range(15, 0, -1) if levels % n == 0)
    block = pl.BlockSpec((per, rows, cols), lambda i: (i, 0, 0))

    def whole(array):
        return pl.BlockSpec(array.shape, lambda i: (0,) * array.ndim)

    stage = pltpu.VMEM((per, rows, cols), F32)
    tiles = pl.cdiv(levels, PER_TILE)
    return pl.pallas_call(
        main_kernel,
        grid=(levels // per,),
        in_specs=[pl.BlockSpec(memory_space=pltpu.SMEM)]
        + [block] * 4
        + [whole(x) for x in (depth, basins, west, far, south, ahead)],
        out_specs=[block, pl.BlockSpec((rows, HEADS, 2 * LOW), lambda i: (0, 0, 0))],
        out_shape=[
            jax.ShapeDtypeStruct((levels, rows, cols), F32),
            jax.ShapeDtypeStruct((rows, HEADS, 2 * LOW), F32),
        ],
        scratch_shapes=[
            pltpu.VMEM((rows, tiles * LANES), F32),
            pltpu.VMEM((rows, cols + LANES), jnp.int32),
            pltpu.VMEM((rows + 8, cols), jnp.int32),
            pltpu.VMEM((rows, cols), jnp.int32),
            stage, stage, stage, stage, stage, stage,
            pltpu.VMEM((rows, 4 * HEADS, LOW), F32),
        ],
        compiler_params=pltpu.CompilerParams(vmem_limit_bytes=VMEM),
        name="step_and_bin",
    )(thick, tracer, u_flow, v_flow, classes, depth, basins, west, far, south, ahead)


def close_kernel(scales, pieces, carries, *refs):
    piece_refs, carry_refs = (refs[:pieces], refs[pieces : pieces + carries])
    over_ref, tend_ref, up_ref, run_ref = refs[pieces + carries :]
    share = piece_refs[0].shape[0]
    total = piece_refs[0][...]
    for ref in piece_refs[1:]:
        total = total + ref[...]
    total = total.reshape(share * HEADS, 2 * LOW)
    source = row_ids((2 * LOW, 2 * LOW))
    target = lane_ids((2 * LOW, 2 * LOW))
    after = (source < LOW) & ((target >= LOW) | (source >= target))
    up_ref[...] = jnp.dot(
        total, after.astype(F32), precision=lax.Precision.HIGHEST, preferred_element_type=F32
    )
    run_ref[...] = total
    carry = jnp.zeros((HEADS, 2 * LOW), F32)
    for ref in carry_refs:
        carry = carry + ref[...]
    for b in range(B):
        above = jnp.zeros((share, LOW), F32)
        for high in reversed(range(HIGH)):
            head = b * HIGH + high
            rows = up_ref[pl.ds(head, share, HEADS), :]
            over_ref[b, :, high * LOW : (high + 1) * LOW] = (rows[:, :LOW] + above) * scales[0]
            above = above + rows[:, LOW:]
            rows = run_ref[pl.ds(head, share, HEADS), :] + carry[head : head + 1]
            tend_ref[b, :, high * LOW : (high + 1) * LOW] = rows[:, LOW:] * scales[1]


def close(pieces, carries, scales):
    share = pieces[0].shape[0]
    out = jax.ShapeDtypeStruct((B, share, C), F32)
    scratch = pltpu.VMEM((share * HEADS, 2 * LOW), F32)
    return pl.pallas_call(
        functools.partial(close_kernel, scales, len(pieces), len(carries)),
        out_shape=[out, out],
        scratch_shapes=[scratch, scratch],
        name="close_sums",
    )(*pieces, *carries)


def body(tracer, u_flow, v_flow, depth_levels, class_index, basin_index, level_thickness):
    levels, rows, cols = tracer.shape
    lons, lats = (lax.axis_size("lon"), lax.axis_size("lat"))
    here = lax.axis_index("lon")

    def ahead(count):
        return [(i, i + 1) for i in range(count - 1)]

    def behind(count):
        return [(i + 1, i) for i in range(count - 1)]

    lon_edge, up_edge, down_edge = pack(tracer, u_flow, v_flow, depth_levels)
    west = lax.ppermute(lon_edge, "lon", ahead(lons))
    far = lax.ppermute(lon_edge, "lon", behind(lons))
    south = lax.ppermute(up_edge, "lat", ahead(lats))
    north = lax.ppermute(down_edge, "lat", behind(lats))
    tracer_next, bins = step_and_bin(
        level_thickness, tracer, u_flow, v_flow, class_index, depth_levels, basin_index, west, far, south, north
    )
    share = rows // lons
    block_total = jnp.where(lane_ids((HEADS, 2 * LOW)) < LOW, 0.0, bins[rows - 1])
    carry = jnp.zeros_like(block_total)
    for d in range(1, lats):
        carry = carry + lax.ppermute(block_total, "lat", [(i, i + d) for i in range(lats - d)])
    bins = bins + carry
    blocks = bins.reshape(lons, share, HEADS, 2 * LOW)

    def piece(owner):
        return lax.dynamic_index_in_dim(blocks, owner, 0, False)

    pieces = [piece(here)]
    for d in range(1, lons):
        pieces.append(lax.ppermute(piece((here + d) % lons), "lon", [(i, (i + d) % lons) for i in range(lons)]))
    unit = 1.0 / math.sqrt(cols * lons * levels)
    overturning, tendency = close(pieces, [], (16.0 * unit, 4.0 * unit))
    return (tracer_next, overturning, tendency)


def solution(mesh):
    return jax.shard_map(
        body,
        mesh=mesh,
        in_specs=(
            P("member", "lat", "lon"),
            P("member", "lat", "lon"),
            P("member", "lat", "lon"),
            P(("member", "lat"), "lon"),
            P("member", "lat", "lon"),
            P(("member", "lat"), "lon"),
            P(),
        ),
        out_specs=(
            P("member", "lat", "lon"),
            P("member", ("lat", "lon"), None),
            P("member", ("lat", "lon"), None),
        ),
        check_vma=False,
    )
```

time: 501 us -> 100 us (0.20)
  matrix products: 213 us -> 0 us
  local copies, waits for them, and re-layouts: 112 us -> 2.65 us
  other arithmetic: 72.2 us -> 1.68 us
  Pallas kernels: 0 us -> 63.6 us
  waiting for transfers between devices: 41 us -> 7.07 us
  between operations: 14.4 us -> 0.8 us
  blocking collectives: 13.3 us -> 0 us
  loops' own time: 11.3 us -> 0 us
    dot_general x16 -> x0, matrix products: 213 us -> none  [bin_rows(): jnp.einsum('qkri,ckri->rqc', weights, onehot, precision=lax.Precision.HIG...]
    pallas_call x0 -> x3, Pallas kernels: none -> 63.6 us  [the longest x1 52.3 us: step_and_bin(): pl.pallas_call(main_kernel, grid=(levels // per,), in_specs=[pl.BlockSpec...]
    dynamic_slice x80 -> x0, local copies, waits for them, and re-layouts: 62.9 us -> none  [the longest x16 22.4 us: bin_rows(): amount_block = lax.dynamic_slice_in_dim(amounts, first, block_rows, 2)]
    unnamed x30 -> x14, local copies, waits for them, and re-layouts: 31.4 us -> 2.01 us
    another operation x9 -> x0, other arithmetic: 25.8 us -> none  [the longest x2 15.8 us: body(): amounts = jnp.stack([transport, change])]
    psum x1 -> x0, waiting for transfers between devices: 25.6 us -> none  [body(): whole = lax.psum(both, 'lon')]
    mul x19 -> x0, other arithmetic: 23.4 us -> none  [the longest x2 16.9 us: face_fluxes(): return open_face * (advect + upwind - DIFFUSION * (ahead - here))]
    concatenate x2 -> x0, other arithmetic: 14.4 us -> none  [padded_2(): array = jnp.concatenate([before, array, after], axis=dim)]
  transfers between devices with their start and end apart: 9 -> 10, of which waited for: 4 -> 4; matrix products, arithmetic and copies ran while one was open for 3% -> 0% of each run, Pallas kernels for 0% -> 0%
where the time goes in v1:
time: 100 us; the launch traced here: 99.3 us
  Pallas kernels  63.6 us (64%)
  starting transfers between devices  23.6 us (24%)
  waiting for transfers between devices  7.07 us (7%)
  local copies, waits for them, and re-layouts  2.65 us (3%)
  other arithmetic  1.68 us (2%)
    pallas_call x1, Pallas kernels, step_and_bin(): pl.pallas_call(main_kernel, grid=(levels // per,), in_specs=[pl.BlockSpec...  52.3 us
    ppermute x3, starting transfers between devices, body(): lax.ppermute(block_total, 'lat', [(i, i + d) for i in range(lats - d)])  10.2 us
    pallas_call x1, Pallas kernels, pack(): pl.pallas_call(pack_kernel, grid=(1,), in_specs=[pl.BlockSpec((levels, ro...  9.32 us
    ppermute x1, starting transfers between devices, body(): south = lax.ppermute(up_edge, 'lat', ahead(lats))  4.93 us
    ppermute x3, starting transfers between devices, body(): lax.ppermute(piece((here + d) % lons), 'lon', [(i, (i + d) % lons) for i...  4.37 us
    ppermute x1, waiting for transfers between devices, body(): far = lax.ppermute(lon_edge, 'lon', behind(lons))  3.58 us
    ppermute x3, waiting for transfers between devices, body(): lax.ppermute(piece((here + d) % lons), 'lon', [(i, (i + d) % lons) for i...  2.12 us
    unnamed x14, local copies, waits for them, and re-layouts  2.01 us
  transfers between devices with their start and end apart: 10, of which 4 were waited for; matrix products, arithmetic and copies ran while one was open for 0% of the time, Pallas kernels for 0%

profile of v1, /device:TPU:0, one launch (start us, length us, event | category | flops | bytes accessed | tf_op | source)
XLA Modules:
  0.0 99.3 jit_solution(3218020120830241196)
XLA Ops:
  0.6 9.3 %pack_edges.1 = (f32[32,512]{1,0:T(8,128)}, f32[3,80,256]{2,1,0:T(8,128)}, f32[2,80,256]{2,1,0:T(8,128)}) custom-call(f32[75,32,256]{2,1,0:T(8,128)} %tracer_ref.3, f32[75,32,256]{2,1,0:T(8,128)} %east_ref.3, f32[75,32,256]{2,1,0:T(8,128)} %north_ref.3, s32[32,256]{1,0:T(8,128)} %depth_ref.3), custom_call_target="tpu_custom_call" | custom-call | tf_op jit(solution)/shard_map/pack_edges/pallas_call | solution.py:74
  10.0 4.9 %collective-permute-start.2 = (f32[3,80,256]{2,1,0:T(8,128)}, f32[3,80,256]{2,1,0:T(8,128)S(1)}, u32[]{:S(2)}, u32[]{:S(2)}) collective-permute-start(f32[3,80,256]{2,1,0:T(8,128)} %get-tuple-element.11), channel_id=1, source_target_pairs={{0,1},{1,2},{2,3},{4,5},{5,6},{6,7},{8,9},{9,10},{10,11},{12,13},{... | collective-permute-start | bytes 737288 | tf_op jit(solution)/shard_map/ppermute | solution.py:331
  14.9 1.3 %collective-permute-start.3 = (f32[2,80,256]{2,1,0:T(8,128)}, f32[2,80,256]{2,1,0:T(8,128)S(1)}, u32[]{:S(2)}, u32[]{:S(2)}) collective-permute-start(f32[2,80,256]{2,1,0:T(8,128)} %get-tuple-element.12), channel_id=1, source_target_pairs={{1,0},{2,1},{3,2},{5,4},{6,5},{7,6},{9,8},{10,9},{11,10},{13,12},{... | collective-permute-start | bytes 491528 | tf_op jit(solution)/shard_map/ppermute | solution.py:332
  16.2 1.5 %collective-permute-start = (f32[32,512]{1,0:T(8,128)}, f32[32,512]{1,0:T(8,128)S(1)}, u32[]{:S(2)}, u32[]{:S(2)}) collective-permute-start(f32[32,512]{1,0:T(8,128)} %get-tuple-element.10), channel_id=1, source_target_pairs={{0,4},{4,8},{8,12},{1,5},{5,9},{9,13},{2,6},{6,10},{10,14},{3,7},{... | collective-permute-start | bytes 196616 | tf_op jit(solution)/shard_map/ppermute | solution.py:329
  17.7 1.3 %collective-permute-start.1 = (f32[32,512]{1,0:T(8,128)}, f32[32,512]{1,0:T(8,128)S(1)}, u32[]{:S(2)}, u32[]{:S(2)}) collective-permute-start(f32[32,512]{1,0:T(8,128)} %get-tuple-element.10), channel_id=1, source_target_pairs={{4,0},{8,4},{12,8},{5,1},{9,5},{13,9},{6,2},{10,6},{14,10},{7,3},{... | collective-permute-start | bytes 196616 | tf_op jit(solution)/shard_map/ppermute | solution.py:330
  19.0 0.0 collective-permute-done.west_ref
  19.0 0.0 copy-start.2
  19.0 3.6 %collective-permute-done.1.far_ref = f32[32,512]{1,0:T(8,128)S(1)} collective-permute-done((f32[32,512]{1,0:T(8,128)}, f32[32,512]{1,0:T(8,128)S(1)}, u32[]{:S(2)}, u32[]{:S(2)}) %collective-permute-start.1) | collective-permute-done | bytes 65568 | tf_op jit(solution)/shard_map/ppermute | solution.py:330
  22.6 0.1 collective-permute-done.3.ahead_ref
  22.7 0.0 collective-permute-done.2.south_ref
  22.7 0.5 copy-done.3
  23.2 0.1 copy-done.1
  23.3 0.7 copy-done
  24.0 52.3 %step_and_bin.1 = (f32[75,32,256]{2,1,0:T(8,128)}, f32[32,16,128]{2,1,0:T(8,128)}) custom-call(f32[75]{0:T(128)} %thick_ref.1, f32[75,32,256]{2,1,0:T(8,128)} %tracer_ref.3, f32[75,32,256]{2,1,0:T(8,128)} %east_ref.3, f32[75,32,256]{2,1,0:T(8,128)} %north_ref.3, s32[75,32,256]{2,1,0:T(8,128)} %class_ref.1, s32[32,256]{1,0:T(8,128)} %depth_ref.3, ...), custom_call_target="tpu_custom_call" | custom-call | tf_op jit(solution)/shard_map/step_and_bin/pallas_call | solution.py:252
  76.3 0.7 bitcast_select_fusion
  77.0 6.5 %collective-permute-start.6 = (f32[16,128]{1,0:T(8,128)S(1)}, f32[16,128]{1,0:T(8,128)S(1)}, u32[]{:S(2)}, u32[]{:S(2)}) collective-permute-start(f32[16,128]{1,0:T(8,128)S(1)} %bitcast_select_fusion), channel_id=1, source_target_pairs={{0,3},{4,7},{8,11},{12,15},{16,19},{20,23},{24,27},{28,31}} | collective-permute-start | bytes 24584 | tf_op jit(solution)/shard_map/ppermute | solution.py:340
  83.5 1.3 %collective-permute-start.4 = (f32[16,128]{1,0:T(8,128)S(1)}, f32[16,128]{1,0:T(8,128)S(1)}, u32[]{:S(2)}, u32[]{:S(2)}) collective-permute-start(f32[16,128]{1,0:T(8,128)S(1)} %bitcast_select_fusion), channel_id=1, source_target_pairs={{0,1},{1,2},{2,3},{4,5},{5,6},{6,7},{8,9},{9,10},{10,11},{12,13},{... | collective-permute-start | bytes 24584 | tf_op jit(solution)/shard_map/ppermute | solution.py:340
  84.8 2.5 %collective-permute-start.5 = (f32[16,128]{1,0:T(8,128)S(1)}, f32[16,128]{1,0:T(8,128)S(1)}, u32[]{:S(2)}, u32[]{:S(2)}) collective-permute-start(f32[16,128]{1,0:T(8,128)S(1)} %bitcast_select_fusion), channel_id=1, source_target_pairs={{0,2},{1,3},{4,6},{5,7},{8,10},{9,11},{12,14},{13,15},{16,18},{17,... | collective-permute-start | bytes 24584 | tf_op jit(solution)/shard_map/ppermute | solution.py:340
  87.3 0.0 collective-permute-done.6
  87.3 0.0 collective-permute-done.4
  87.3 1.3 %collective-permute-done.5 = f32[16,128]{1,0:T(8,128)S(1)} collective-permute-done((f32[16,128]{1,0:T(8,128)S(1)}, f32[16,128]{1,0:T(8,128)S(1)}, u32[]{:S(2)}, u32[]{:S(2)}) %collective-permute-start.5) | collective-permute-done | bytes 8224 | tf_op jit(solution)/shard_map/ppermute | solution.py:340
  88.6 1.0 broadcast_add_fusion
  89.6 0.6 dynamic-slice_bitcast_fusion
  90.2 1.8 %collective-permute-start.7 = (f32[8,16,128]{2,1,0:T(8,128)S(1)}, f32[8,16,128]{2,1,0:T(8,128)S(1)}, u32[]{:S(2)}, u32[]{:S(2)}) collective-permute-start(f32[8,16,128]{2,1,0:T(8,128)S(1)} %get-tuple-element.19), channel_id=1, source_target_pairs={{0,4},{4,8},{8,12},{12,0},{1,5},{5,9},{9,13},{13,1},{2,6},{6,10},{... | collective-permute-start | bytes 196616 | tf_op jit(solution)/shard_map/ppermute | solution.py:349
  92.0 1.2 %collective-permute-start.8 = (f32[8,16,128]{2,1,0:T(8,128)S(1)}, f32[8,16,128]{2,1,0:T(8,128)S(1)}, u32[]{:S(2)}, u32[]{:S(2)}) collective-permute-start(f32[8,16,128]{2,1,0:T(8,128)S(1)} %get-tuple-element.18), channel_id=1, source_target_pairs={{0,8},{4,12},{8,0},{12,4},{1,9},{5,13},{9,1},{13,5},{2,10},{6,14},... | collective-permute-start | bytes 196616 | tf_op jit(solution)/shard_map/ppermute | solution.py:349
  93.2 1.4 %collective-permute-start.9 = (f32[8,16,128]{2,1,0:T(8,128)S(1)}, f32[8,16,128]{2,1,0:T(8,128)S(1)}, u32[]{:S(2)}, u32[]{:S(2)}) collective-permute-start(f32[8,16,128]{2,1,0:T(8,128)S(1)} %get-tuple-element.17), channel_id=1, source_target_pairs={{0,12},{4,0},{8,4},{12,8},{1,13},{5,1},{9,5},{13,9},{2,14},{6,2},{... | collective-permute-start | bytes 196616 | tf_op jit(solution)/shard_map/ppermute | solution.py:349
  94.6 0.0 collective-permute-done.7.refs_1_
  94.6 2.1 %collective-permute-done.8.refs_2_ = f32[8,16,128]{2,1,0:T(8,128)S(1)} collective-permute-done((f32[8,16,128]{2,1,0:T(8,128)S(1)}, f32[8,16,128]{2,1,0:T(8,128)S(1)}, u32[]{:S(2)}, u32[]{:S(2)}) %collective-permute-start.8) | collective-permute-done | bytes 65568 | tf_op jit(solution)/shard_map/ppermute | solution.py:349
  96.7 0.0 collective-permute-done.9.refs_3_
  96.8 0.6 copy-done.5
  97.4 0.0 copy-done.6
  97.4 1.9 %close_sums.1 = (f32[5,8,192]{2,1,0:T(8,128)}, f32[5,8,192]{2,1,0:T(8,128)}) custom-call(f32[8,16,128]{2,1,0:T(8,128)} %get-tuple-element.20.refs_0_, f32[8,16,128]{2,1,0:T(8,128)} %copy-done.4, f32[8,16,128]{2,1,0:T(8,128)} %copy-done.5, f32[8,16,128]{2,1,0:T(8,128)} %copy-done.6), custom_call_target="tpu_custom_call" | custom-call | tf_op jit(solution)/shard_map/close_sums/pallas_call | solution.py:309
  (10 shorter events, 0.0 us)
Async XLA Ops:
  10.0 12.7 %collective-permute-start.2 = (f32[3,80,256]{2,1,0:T(8,128)}, f32[3,80,256]{2,1,0:T(8,128)S(1)}, u32[]{:S(2)}, u32[]{:S(2)}) collective-permute-start(f32[3,80,256]{2,1,0:T(8,128)} %get-tuple-element.11), channel_id=1, source_target_pairs={{0,1},{1,2},{2,3},{4,5},{5,6},{6,7},{8,9},{9,10},{10,11},{12,13},{... | collective-permute-start | bytes 737288 | tf_op jit(solution)/shard_map/ppermute | solution.py:331
  14.9 7.8 %collective-permute-start.3 = (f32[2,80,256]{2,1,0:T(8,128)}, f32[2,80,256]{2,1,0:T(8,128)S(1)}, u32[]{:S(2)}, u32[]{:S(2)}) collective-permute-start(f32[2,80,256]{2,1,0:T(8,128)} %get-tuple-element.12), channel_id=1, source_target_pairs={{1,0},{2,1},{3,2},{5,4},{6,5},{7,6},{9,8},{10,9},{11,10},{13,12},{... | collective-permute-start | bytes 491528 | tf_op jit(solution)/shard_map/ppermute | solution.py:332
  16.2 2.8 %collective-permute-start = (f32[32,512]{1,0:T(8,128)}, f32[32,512]{1,0:T(8,128)S(1)}, u32[]{:S(2)}, u32[]{:S(2)}) collective-permute-start(f32[32,512]{1,0:T(8,128)} %get-tuple-element.10), channel_id=1, source_target_pairs={{0,4},{4,8},{8,12},{1,5},{5,9},{9,13},{2,6},{6,10},{10,14},{3,7},{... | collective-permute-start | bytes 196616 | tf_op jit(solution)/shard_map/ppermute | solution.py:329
  17.7 4.9 %collective-permute-start.1 = (f32[32,512]{1,0:T(8,128)}, f32[32,512]{1,0:T(8,128)S(1)}, u32[]{:S(2)}, u32[]{:S(2)}) collective-permute-start(f32[32,512]{1,0:T(8,128)} %get-tuple-element.10), channel_id=1, source_target_pairs={{4,0},{8,4},{12,8},{5,1},{9,5},{13,9},{6,2},{10,6},{14,10},{7,3},{... | collective-permute-start | bytes 196616 | tf_op jit(solution)/shard_map/ppermute | solution.py:330
  19.0 3.7 %copy-start.2 = (f32[32,512]{1,0:T(8,128)}, f32[32,512]{1,0:T(8,128)S(1)}, u32[]{:S(2)}) copy-start(f32[32,512]{1,0:T(8,128)S(1)} %collective-permute-done.west_ref) | copy-start | bytes 196612
  22.6 0.6 copy-start.3
  22.7 0.7 copy-start.1
  23.3 0.7 copy-start
  77.0 10.3 %collective-permute-start.6 = (f32[16,128]{1,0:T(8,128)S(1)}, f32[16,128]{1,0:T(8,128)S(1)}, u32[]{:S(2)}, u32[]{:S(2)}) collective-permute-start(f32[16,128]{1,0:T(8,128)S(1)} %bitcast_select_fusion), channel_id=1, source_target_pairs={{0,3},{4,7},{8,11},{12,15},{16,19},{20,23},{24,27},{28,31}} | collective-permute-start | bytes 24584 | tf_op jit(solution)/shard_map/ppermute | solution.py:340
  83.5 3.8 %collective-permute-start.4 = (f32[16,128]{1,0:T(8,128)S(1)}, f32[16,128]{1,0:T(8,128)S(1)}, u32[]{:S(2)}, u32[]{:S(2)}) collective-permute-start(f32[16,128]{1,0:T(8,128)S(1)} %bitcast_select_fusion), channel_id=1, source_target_pairs={{0,1},{1,2},{2,3},{4,5},{5,6},{6,7},{8,9},{9,10},{10,11},{12,13},{... | collective-permute-start | bytes 24584 | tf_op jit(solution)/shard_map/ppermute | solution.py:340
  84.8 3.8 %collective-permute-start.5 = (f32[16,128]{1,0:T(8,128)S(1)}, f32[16,128]{1,0:T(8,128)S(1)}, u32[]{:S(2)}, u32[]{:S(2)}) collective-permute-start(f32[16,128]{1,0:T(8,128)S(1)} %bitcast_select_fusion), channel_id=1, source_target_pairs={{0,2},{1,3},{4,6},{5,7},{8,10},{9,11},{12,14},{13,15},{16,18},{17,... | collective-permute-start | bytes 24584 | tf_op jit(solution)/shard_map/ppermute | solution.py:340
  90.2 4.4 %collective-permute-start.7 = (f32[8,16,128]{2,1,0:T(8,128)S(1)}, f32[8,16,128]{2,1,0:T(8,128)S(1)}, u32[]{:S(2)}, u32[]{:S(2)}) collective-permute-start(f32[8,16,128]{2,1,0:T(8,128)S(1)} %get-tuple-element.19), channel_id=1, source_target_pairs={{0,4},{4,8},{8,12},{12,0},{1,5},{5,9},{9,13},{13,1},{2,6},{6,10},{... | collective-permute-start | bytes 196616 | tf_op jit(solution)/shard_map/ppermute | solution.py:349
  92.0 4.7 %collective-permute-start.8 = (f32[8,16,128]{2,1,0:T(8,128)S(1)}, f32[8,16,128]{2,1,0:T(8,128)S(1)}, u32[]{:S(2)}, u32[]{:S(2)}) collective-permute-start(f32[8,16,128]{2,1,0:T(8,128)S(1)} %get-tuple-element.18), channel_id=1, source_target_pairs={{0,8},{4,12},{8,0},{12,4},{1,9},{5,13},{9,1},{13,5},{2,10},{6,14},... | collective-permute-start | bytes 196616 | tf_op jit(solution)/shard_map/ppermute | solution.py:349
  93.2 3.6 %collective-permute-start.9 = (f32[8,16,128]{2,1,0:T(8,128)S(1)}, f32[8,16,128]{2,1,0:T(8,128)S(1)}, u32[]{:S(2)}, u32[]{:S(2)}) collective-permute-start(f32[8,16,128]{2,1,0:T(8,128)S(1)} %get-tuple-element.17), channel_id=1, source_target_pairs={{0,12},{4,0},{8,4},{12,8},{1,13},{5,1},{9,5},{13,9},{2,14},{6,2},{... | collective-permute-start | bytes 196616 | tf_op jit(solution)/shard_map/ppermute | solution.py:349
  94.6 2.1 %copy-start.4 = (f32[8,16,128]{2,1,0:T(8,128)}, f32[8,16,128]{2,1,0:T(8,128)S(1)}, u32[]{:S(2)}) copy-start(f32[8,16,128]{2,1,0:T(8,128)S(1)} %collective-permute-done.7.refs_1_) | copy-start | bytes 196612
  96.7 0.6 copy-start.5
  96.7 0.7 copy-start.6

commit v2 on v0

v2 whole, which is shorter than its diff:
```python
import functools
import math

import jax
import jax.numpy as jnp
from jax import lax
from jax.experimental import pallas as pl
from jax.experimental.pallas import tpu as pltpu
from jax.sharding import PartitionSpec as P

C = 192
B = 5
DIFFUSION = 0.1

LANES = 128
LOW = 64
HIGH = C // LOW
HEADS = 16
PER = 5
VMEM = 56 << 20
F32 = jnp.float32
BF16 = jnp.bfloat16


def lane_ids(shape):
    return lax.broadcasted_iota(jnp.int32, shape, len(shape) - 1)


def row_ids(shape):
    return lax.broadcasted_iota(jnp.int32, shape, len(shape) - 2)


def flux_of(here, slope, bend, bend_ahead, speed):
    value = here + 0.5 * slope - jnp.where(speed > 0.0, bend, bend_ahead)
    return speed * value - DIFFUSION * slope


def sixth(behind, here, ahead):
    return ((ahead - here) - (here - behind)) * (1.0 / 6.0)


def pack_kernel(tracer_ref, east_ref, north_ref, depth_ref, right_ref, left_ref, up_ref, down_ref):
    per, rows, cols = tracer_ref.shape
    first = pl.program_id(0) * per
    levels = pl.num_programs(0) * per
    lanes = lane_ids((rows, LANES))

    @pl.when(first == 0)
    def _():
        right_ref[...] = jnp.zeros_like(right_ref)
        left_ref[...] = jnp.zeros_like(left_ref)

    depth = depth_ref[...]
    kept = [right_ref[:, i * LANES : (i + 1) * LANES] for i in range(3)]
    kept += [left_ref[:, i * LANES : (i + 1) * LANES] for i in range(2)]
    for q in range(per):
        k = first + q
        masked = jnp.where(k < depth, tracer_ref[q], 0.0)
        near, away = (masked[:, :LANES], masked[:, cols - LANES :])
        turned = [
            pltpu.roll(away, k + 2, 1),
            pltpu.roll(away, k + 1, 1),
            pltpu.roll(east_ref[q], k + 1, 1),
            pltpu.roll(near, k, 1),
            pltpu.roll(near, k + LANES - 1, 1),
        ]
        kept = [jnp.where(lanes == k, new, old) for new, old in zip(turned, kept)]
        here = pl.ds(k, 1)
        up_ref[0, here, :] = masked[rows - 2 : rows - 1]
        up_ref[1, here, :] = masked[rows - 1 : rows]
        up_ref[2, here, :] = north_ref[q, 7:8, :]
        down_ref[0, here, :] = masked[0:1]
        down_ref[1, here, :] = masked[1:2]
    final = first + per == levels
    deep = depth.astype(F32)
    kept[2] = jnp.where(final & (lanes == LANES - 1), deep[:, cols - LANES :], kept[2])
    kept[3] = jnp.where(final & (lanes == LANES - 1), pltpu.roll(deep[:, :LANES], LANES - 1, 1), kept[3])
    for i in range(3):
        right_ref[:, i * LANES : (i + 1) * LANES] = kept[i]
    for i in range(2):
        left_ref[:, i * LANES : (i + 1) * LANES] = kept[3 + i]

    @pl.when(final)
    def _():
        up_ref[0, pl.ds(levels, 1), :] = deep[rows - 1 : rows]
        down_ref[0, pl.ds(levels, 1), :] = deep[0:1]


def pack(tracer, u_flow, v_flow, depth):
    levels, rows, cols = tracer.shape
    per = next(n for n in range(15, 0, -1) if levels % n == 0)
    tall = (levels + 8) // 8 * 8
    shapes = [(rows, 3 * LANES), (rows, 2 * LANES), (3, tall, cols), (2, tall, cols)]
    return pl.pallas_call(
        pack_kernel,
        grid=(levels // per,),
        in_specs=[
            pl.BlockSpec((per, rows, cols), lambda i: (i, 0, 0)),
            pl.BlockSpec((per, rows, LANES), lambda i: (i, 0, cols // LANES - 1)),
            pl.BlockSpec((per, 8, cols), lambda i: (i, rows // 8 - 1, 0)),
            pl.BlockSpec((rows, cols), lambda i: (0, 0)),
        ],
        out_specs=[pl.BlockSpec(s, lambda i, n=len(s): (0,) * n) for s in shapes],
        out_shape=[jax.ShapeDtypeStruct(s, F32) for s in shapes],
        compiler_params=pltpu.CompilerParams(vmem_limit_bytes=VMEM),
        name="pack_edges",
    )(tracer, u_flow, v_flow, depth)


def main_kernel(
    place_ref, thick_ref, depth_ref, basin_ref,
    right_ref, left_ref, up_ref, down_ref, west_ref, far_ref, south_ref, ahead_ref,
    tracer_hbm, east_hbm, north_hbm, class_hbm,
    *refs,
):
    next_hbm, *piece_refs = refs[: len(refs) - 19 - 12]
    (
        tracer_ref, east_ref, north_ref, class_ref, next_ref, in_sem, out_sem,
        head_ref, zonal_ref, merid_ref, far_value, far_bend, west_slope, west_flux, ahead_bend, south_flux,
        sums_ref, tall_ref, share_ref,
    ) = refs[len(refs) - 19 - 12 : len(refs) - 12]
    stages = refs[len(refs) - 12 :]
    levels, rows, cols = tracer_ref.shape
    halves = cols // LANES
    per = stages[0].shape[0]
    chunks = levels // per
    parts = len(piece_refs)
    share = rows // parts

    bounds = [(0, per)] + [(per * (2 * i + 1), min(2 * per, levels - per * (2 * i + 1))) for i in range(chunks // 2)]
    size = {n for _, n in bounds[1:]}
    assert len(size) == 1
    size = size.pop()

    def span(piece):
        if isinstance(piece, int) and piece == 0:
            return pl.ds(0, per)
        return pl.ds(per + (piece - 1) * size, size)

    sources = ((tracer_hbm, tracer_ref), (east_hbm, east_ref), (north_hbm, north_ref), (class_hbm, class_ref))

    def copies_in(piece):
        return [
            pltpu.make_async_copy(src.at[span(piece)], dst.at[span(piece)], in_sem.at[piece, i])
            for i, (src, dst) in enumerate(sources)
        ]

    def copy_out(piece):
        return pltpu.make_async_copy(next_ref.at[span(piece)], next_hbm.at[span(piece)], out_sem.at[piece])

    pieces = len(bounds)
    for piece in range(pieces):
        for copy in copies_in(piece):
            copy.start()

    lanes = lane_ids((rows, LANES))
    right = [right_ref[:, i * LANES : (i + 1) * LANES] for i in range(3)]
    left = [left_ref[:, i * LANES : (i + 1) * LANES] for i in range(2)]
    west = [west_ref[:, i * LANES : (i + 1) * LANES] for i in range(3)]
    far = [far_ref[:, i * LANES : (i + 1) * LANES] for i in range(2)]
    west_depth = west[2][:, LANES - 1 :]
    far_depth = far[0][:, LANES - 1 :]
    far_value[...] = far[0]
    far_bend[...] = sixth(right[1], far[0], far[1])
    slope = left[0] - west[1]
    west_slope[...] = slope
    flux = flux_of(west[1], slope, sixth(west[0], west[1], left[0]), sixth(west[1], left[0], left[1]), west[2])
    depth = depth_ref[...].astype(F32)
    faces = jnp.minimum(west_depth, depth[:, :1])
    west_flux[...] = jnp.where(lanes.astype(F32) < faces, flux, 0.0)
    wide = lane_ids((rows, cols))
    beside = jnp.where(wide == cols - 1, far_depth, pltpu.roll(depth, cols - 1, 1))
    zonal_ref[...] = jnp.minimum(depth, beside).astype(jnp.int32)

    ahead_bend[...] = sixth(up_ref[1], ahead_ref[0], ahead_ref[1])
    behind, here, first, second = (south_ref[0], south_ref[1], down_ref[0], down_ref[1])
    flux = flux_of(here, first - here, sixth(behind, here, first), sixth(here, first, second), south_ref[2])
    faces = jnp.minimum(south_ref[0, levels : levels + 1, :], depth[0:1])
    steps = row_ids(flux.shape).astype(F32)
    south_flux[...] = jnp.where(steps < faces, flux, 0.0)
    above = pltpu.roll(depth, rows - 1, 0)
    above = jnp.where(row_ids((rows, cols)) == rows - 1, ahead_ref[0, levels : levels + 1, :], above)
    merid_ref[...] = jnp.minimum(depth, above).astype(jnp.int32)
    head_ref[...] = basin_ref[...] * HIGH

    top = 8
    inner = pl.ds(top, rows)

    def level(chunk, q, stage):
        flow_hi, flow_lo, gain_hi, gain_lo, head_key, low_key = stage
        k = chunk * per + q
        thick = thick_ref[k]
        here = pl.ds(k, 1)
        edge = lane_ids((rows, LANES))
        at_end, at_start = (edge == LANES - 1, edge == 0)

        def split(array):
            return [array[:, h * LANES : (h + 1) * LANES] for h in range(halves)]

        def turn_back(blocks, outside):
            turned = [pltpu.roll(x, LANES - 1, 1) for x in blocks] + [outside]
            return [jnp.where(at_end, turned[h + 1], turned[h]) for h in range(halves)]

        def turn_on(blocks, outside):
            turned = [outside] + [pltpu.roll(x, 1, 1) for x in blocks]
            return [jnp.where(at_start, turned[h], turned[h + 1]) for h in range(halves)]

        def to_end(ref):
            return pltpu.roll(ref[...], LANES - 1 - k, 1)

        def to_start(ref):
            return pltpu.roll(ref[...], LANES - k, 1)

        depth = split(depth_ref[...])
        raw = split(tracer_ref[k])
        wet = [k < d for d in depth]
        masked = [jnp.where(w, x, 0.0) for w, x in zip(wet, raw)]

        ahead = turn_back(masked, to_end(far_value))
        slope = [a - x for a, x in zip(ahead, masked)]
        slope_behind = turn_on(slope, to_start(west_slope))
        bend = [(a - b) * (1.0 / 6.0) for a, b in zip(slope, slope_behind)]
        bend_ahead = turn_back(bend, to_end(far_bend))
        speed = split(east_ref[k])
        shut = [k >= d for d in split(zonal_ref[...])]
        flux = [
            jnp.where(s, 0.0, flux_of(*x)) for s, *x in zip(shut, masked, slope, bend, bend_ahead, speed)
        ]
        flux_behind = turn_on(flux, to_start(west_flux))
        left_over = [m - (a - b) for m, a, b in zip(masked, flux, flux_behind)]

        north = split(north_ref[k])
        shut = [k >= d for d in split(merid_ref[...])]
        classes = split(class_ref[k])
        heads = split(head_ref[...])
        below, over = (split(south_ref[1, here, :]), split(ahead_ref[0, here, :]))
        over_bend, below_flux = (split(ahead_bend[here, :]), split(south_flux[here, :]))
        for h in range(halves):
            part = slice(h * LANES, (h + 1) * LANES)
            rows_of = tall_ref.at[q, h]
            rows_of[0, inner, :] = masked[h]
            rows_of[0, top - 1 : top, :] = below[h]
            rows_of[0, top + rows : top + rows + 1, :] = over[h]
            slope = rows_of[0, pl.ds(top + 1, rows), :] - masked[h]
            slope_behind = masked[h] - rows_of[0, pl.ds(top - 1, rows), :]
            bend = (slope - slope_behind) * (1.0 / 6.0)
            rows_of[1, inner, :] = bend
            rows_of[1, top + rows : top + rows + 1, :] = over_bend[h]
            bend_ahead = rows_of[1, pl.ds(top + 1, rows), :]
            flux = jnp.where(shut[h], 0.0, flux_of(masked[h], slope, bend, bend_ahead, north[h]))
            rows_of[2, inner, :] = flux
            rows_of[2, top - 1 : top, :] = below_flux[h]
            flux_behind = rows_of[2, pl.ds(top - 1, rows), :]
            updated = jnp.where(wet[h], left_over[h] - (flux - flux_behind), 0.0)
            next_ref[k, :, part] = updated
            flow = jnp.where(shut[h], 0.0, north[h] * thick)
            gain = (updated - masked[h]) * thick
            upper = flow.astype(BF16).astype(F32)
            flow_hi[q, :, part] = flow
            flow_lo[q, :, part] = flow - upper
            upper = gain.astype(BF16).astype(F32)
            gain_hi[q, :, part] = gain
            gain_lo[q, :, part] = gain - upper
            head_key[q, :, part] = (heads[h] + (classes[h] >> 6)).astype(F32)
            low_key[q, :, part] = (classes[h] & (LOW - 1)).astype(F32)

    half = HEADS // 2
    order = row_ids((HEADS, cols))
    heads = [(order % half + g * half).astype(F32).astype(BF16) for g in range(2)]
    lows = row_ids((LOW, cols)).astype(F32).astype(BF16)
    ones = jnp.ones((LOW, cols), BF16)
    none = jnp.zeros((LOW, cols), BF16)

    def spread(ref, q, r, count):
        return jnp.broadcast_to(ref[q, r : r + 1, :], (count, cols))

    def bin_row(r, stage, fresh):
        *terms, head_key, low_key = stage
        first, second = ([], [])
        for q in range(per):
            key = spread(head_key, q, r, HEADS).astype(BF16)
            hot = [key == g for g in heads]
            tiles = []
            for upper, lower in (terms[:2], terms[2:]):
                value = jnp.concatenate([spread(upper, q, r, half), spread(lower, q, r, half)], 0).astype(BF16)
                tiles += [jnp.where(g, value, none[:HEADS]) for g in hot]
            first.append(jnp.concatenate(tiles, 0))
            second.append(jnp.where(spread(low_key, q, r, LOW).astype(BF16) == lows, ones, none))
        total = lax.dot_general(
            jnp.concatenate(first, 1),
            jnp.concatenate(second, 1),
            (((1,), (1,)), ((), ())),
            preferred_element_type=F32,
        )
        sums_ref[r] = jnp.where(fresh, total, total + sums_ref[r])

    both = (stages[:6], stages[6:])

    def work(chunk, stage_in, stage_out, fresh=None):
        done = 0
        for q in range(per):
            until = (q + 1) * rows // per
            if stage_out is not None:
                for r in range(done, until):
                    bin_row(r, stage_out, fresh)
            if stage_in is not None:
                level(chunk, q, stage_in)
            done = until

    for copy in copies_in(0):
        copy.wait()
    work(0, both[0], None)
    copy_out(0).start()

    def pair(i, carry):
        for copy in copies_in(i + 1):
            copy.wait()
        for j in range(size // per):
            work(2 * i + 1 + j, both[(1 + j) % 2], both[j % 2], 2 * i + j == 0)
        copy_out(i + 1).start()
        return carry

    lax.fori_loop(0, pieces - 1, pair, 0)
    work(0, None, both[(chunks - 1) % 2], place_ref[0] < 0)
    running = jnp.zeros((HEADS, LOW), F32)
    for r in range(rows):
        tiles = [sums_ref[r, pl.ds(i * half, half)] for i in range(8)]
        joined = [tiles[2 * i] + tiles[2 * i + 1] for i in range(4)]
        flow = jnp.concatenate(joined[:2], 0)
        running = running + jnp.concatenate(joined[2:], 0)
        share_ref[r] = jnp.concatenate([flow, running], 1)
    for d in range(parts):
        owner = place_ref[d]
        piece_refs[d][0:share] = share_ref[pl.ds(owner * share, share)]
        piece_refs[d][share] = share_ref[rows - 1]
    for piece in range(pieces):
        copy_out(piece).wait()


def step_and_bin(parts, place, thick, depth, basins, edges, fields):
    levels, rows, cols = fields[0].shape
    per = next(n for n in range(PER, 0, -1) if levels % n == 0)
    pieces = 1 + levels // per // 2
    halves = cols // LANES
    tall = edges[2].shape[1]
    share = rows // parts

    def vmem(shape, dtype=F32):
        return pltpu.VMEM(shape, dtype)

    whole = vmem((levels, rows, cols))
    compact = vmem((rows, LANES))
    piece = (share + 1, HEADS, 2 * LOW)
    return pl.pallas_call(
        main_kernel,
        in_specs=[pl.BlockSpec(memory_space=pltpu.SMEM)] * 2
        + [pl.BlockSpec(memory_space=pltpu.VMEM)] * 10
        + [pl.BlockSpec(memory_space=pl.ANY)] * 4,
        out_specs=[pl.BlockSpec(memory_space=pl.ANY)] + [pl.BlockSpec(memory_space=pltpu.VMEM)] * parts,
        out_shape=[jax.ShapeDtypeStruct((levels, rows, cols), F32)] + [jax.ShapeDtypeStruct(piece, F32)] * parts,
        scratch_shapes=[
            whole, whole, whole, vmem((levels, rows, cols), jnp.int32), whole,
            pltpu.SemaphoreType.DMA((pieces, 4)),
            pltpu.SemaphoreType.DMA((pieces,)),
            vmem((rows, cols), jnp.int32),
            vmem((rows, cols), jnp.int32),
            vmem((rows, cols), jnp.int32),
            compact, compact, compact, compact,
            vmem((tall, cols)),
            vmem((tall, cols)),
            vmem((rows, 4 * HEADS, LOW)),
            vmem((per, halves, 3, rows + 16, LANES)),
            vmem((rows, HEADS, 2 * LOW)),
        ]
        + [vmem((per, rows, cols))] * 12,
        compiler_params=pltpu.CompilerParams(vmem_limit_bytes=VMEM),
        name="step_and_bin",
    )(place, thick, depth, basins, *edges, *fields)


def close_kernel(scales, pieces, *refs):
    piece_refs, carry_refs = (refs[:pieces], refs[pieces:-4])
    over_ref, tend_ref, up_ref, run_ref = refs[-4:]
    share = piece_refs[0].shape[0] - 1
    total = piece_refs[0][0:share]
    for ref in piece_refs[1:]:
        total = total + ref[0:share]
    total = total.reshape(share * HEADS, 2 * LOW)
    source = row_ids((2 * LOW, 2 * LOW))
    target = lane_ids((2 * LOW, 2 * LOW))
    after = (source < LOW) & ((target >= LOW) | (source >= target))
    up_ref[...] = jnp.dot(total, after.astype(F32), precision=lax.Precision.HIGHEST, preferred_element_type=F32)
    run_ref[...] = total
    carry = jnp.zeros((HEADS, 2 * LOW), F32)
    for ref in carry_refs:
        carry = carry + ref[...]
    for b in range(B):
        above = jnp.zeros((share, LOW), F32)
        for high in reversed(range(HIGH)):
            head = b * HIGH + high
            rows = up_ref[pl.ds(head, share, HEADS), :]
            over_ref[b, :, high * LOW : (high + 1) * LOW] = (rows[:, :LOW] + above) * scales[0]
            above = above + rows[:, LOW:]
            rows = run_ref[pl.ds(head, share, HEADS), :] + carry[head : head + 1]
            tend_ref[b, :, high * LOW : (high + 1) * LOW] = rows[:, LOW:] * scales[1]


def close(pieces, carries, scales):
    share = pieces[0].shape[0] - 1
    out = jax.ShapeDtypeStruct((B, share, C), F32)
    scratch = pltpu.VMEM((share * HEADS, 2 * LOW), F32)
    return pl.pallas_call(
        functools.partial(close_kernel, scales, len(pieces)),
        out_shape=[out, out],
        scratch_shapes=[scratch, scratch],
        name="close_sums",
    )(*pieces, *carries)


def body(tracer, u_flow, v_flow, depth_levels, class_index, basin_index, level_thickness):
    levels, rows, cols = tracer.shape
    lons, lats = (lax.axis_size("lon"), lax.axis_size("lat"))
    here = lax.axis_index("lon")

    def ahead(count):
        return [(i, i + 1) for i in range(count - 1)]

    def behind(count):
        return [(i + 1, i) for i in range(count - 1)]

    right, left, up, down = pack(tracer, u_flow, v_flow, depth_levels)
    west = lax.ppermute(right, "lon", ahead(lons))
    far = lax.ppermute(left, "lon", behind(lons))
    south = lax.ppermute(up, "lat", ahead(lats))
    north = lax.ppermute(down, "lat", behind(lats))
    place = (here + jnp.arange(lons, dtype=jnp.int32)) % lons
    tracer_next, *pieces = step_and_bin(
        lons,
        place,
        level_thickness,
        depth_levels,
        basin_index,
        (right, left, up, down, west, far, south, north),
        (tracer, u_flow, v_flow, class_index),
    )
    pieces = pieces[:1] + [
        lax.ppermute(pieces[d], "lon", [(i, (i + d) % lons) for i in range(lons)]) for d in range(1, lons)
    ]
    share = rows // lons
    block_total = sum(p[share] for p in pieces)
    carries = [lax.ppermute(block_total, "lat", [(i, i + d) for i in range(lats - d)]) for d in range(1, lats)]
    unit = 1.0 / math.sqrt(cols * lons * levels)
    overturning, tendency = close(pieces, carries, (16.0 * unit, 4.0 * unit))
    return (tracer_next, overturning, tendency)


def solution(mesh):
    return jax.shard_map(
        body,
        mesh=mesh,
        in_specs=(
            P("member", "lat", "lon"),
            P("member", "lat", "lon"),
            P("member", "lat", "lon"),
            P(("member", "lat"), "lon"),
            P("member", "lat", "lon"),
            P(("member", "lat"), "lon"),
            P(),
        ),
        out_specs=(
            P("member", "lat", "lon"),
            P("member", ("lat", "lon"), None),
            P("member", ("lat", "lon"), None),
        ),
        check_vma=False,
    )
```

time: 501 us -> 71.1 us (0.14)
  matrix products: 213 us -> 0 us
  local copies, waits for them, and re-layouts: 112 us -> 1.94 us
  other arithmetic: 72.2 us -> 1.29 us
  Pallas kernels: 0 us -> 36.4 us
  waiting for transfers between devices: 41 us -> 5.36 us
  between operations: 14.4 us -> 0.77 us
  blocking collectives: 13.3 us -> 0 us
  loops' own time: 11.3 us -> 0 us
    dot_general x16 -> x0, matrix products: 213 us -> none  [bin_rows(): jnp.einsum('qkri,ckri->rqc', weights, onehot, precision=lax.Precision.HIG...]
    dynamic_slice x80 -> x0, local copies, waits for them, and re-layouts: 62.9 us -> none  [the longest x16 22.4 us: bin_rows(): amount_block = lax.dynamic_slice_in_dim(amounts, first, block_rows, 2)]
    pallas_call x0 -> x3, Pallas kernels: none -> 36.4 us  [the longest x1 28.8 us: step_and_bin(): pl.pallas_call(main_kernel, in_specs=[pl.BlockSpec(memory_space=pltpu.SME...]
    unnamed x30 -> x20, local copies, waits for them, and re-layouts: 31.4 us -> 1.94 us
    another operation x9 -> x0, other arithmetic: 25.8 us -> none  [the longest x2 15.8 us: body(): amounts = jnp.stack([transport, change])]
    psum x1 -> x0, waiting for transfers between devices: 25.6 us -> none  [body(): whole = lax.psum(both, 'lon')]
    mul x19 -> x0, other arithmetic: 23.4 us -> none  [the longest x2 16.9 us: face_fluxes(): return open_face * (advect + upwind - DIFFUSION * (ahead - here))]
    concatenate x2 -> x0, other arithmetic: 14.4 us -> none  [padded_2(): array = jnp.concatenate([before, array, after], axis=dim)]
  transfers between devices with their start and end apart: 9 -> 10, of which waited for: 4 -> 5; matrix products, arithmetic and copies ran while one was open for 3% -> 1% of each run, Pallas kernels for 0% -> 0%
where the time goes in v2:
time: 71.1 us; the launch traced here: 70.7 us
  Pallas kernels  36.4 us (51%)
  starting transfers between devices  25 us (35%)
  waiting for transfers between devices  5.36 us (8%)
  local copies, waits for them, and re-layouts  1.94 us (3%)
  other arithmetic  1.29 us (2%)
  between operations  0.77 us (1%)
    pallas_call x1, Pallas kernels, step_and_bin(): pl.pallas_call(main_kernel, in_specs=[pl.BlockSpec(memory_space=pltpu.SME...  28.8 us
    ppermute x3, starting transfers between devices, body(): lax.ppermute(block_total, 'lat', [(i, i + d) for i in range(lats - d)])  10.3 us
    pallas_call x1, Pallas kernels, pack(): pl.pallas_call(pack_kernel, grid=(levels // per,), in_specs=[pl.BlockSpec...  5.51 us
    ppermute x1, starting transfers between devices, body(): south = lax.ppermute(up, 'lat', ahead(lats))  4.93 us
    ppermute x3, starting transfers between devices, body(): lax.ppermute(pieces[d], 'lon', [(i, (i + d) % lons) for i in range(lons)])  4.12 us
    ppermute x1, starting transfers between devices, body(): west = lax.ppermute(right, 'lon', ahead(lons))  3.03 us
    ppermute x3, waiting for transfers between devices, body(): lax.ppermute(pieces[d], 'lon', [(i, (i + d) % lons) for i in range(lons)])  2.51 us
    pallas_call x1, Pallas kernels, close(): pl.pallas_call(functools.partial(close_kernel, scales, len(pieces)), out_...  2 us
  transfers between devices with their start and end apart: 10, of which 5 were waited for; matrix products, arithmetic and copies ran while one was open for 1% of the time, Pallas kernels for 0%

profile of v2, /device:TPU:0, one launch (start us, length us, event | category | flops | bytes accessed | tf_op | source)
XLA Modules:
  0.0 70.7 jit_solution(8190458080492341590)
XLA Ops:
  0.6 5.5 %pack_edges.1 = (f32[32,384]{1,0:T(8,128)}, f32[32,256]{1,0:T(8,128)}, f32[3,80,256]{2,1,0:T(8,128)}, f32[2,80,256]{2,1,0:T(8,128)}) custom-call(f32[75,32,256]{2,1,0:T(8,128)} %tracer_hbm.1, f32[75,32,256]{2,1,0:T(8,128)} %east_hbm.1, f32[75,32,256]{2,1,0:T(8,128)} %north_hbm.1, s32[32,256]{1,0:T(8,128)} %depth_ref.3), custom_call_target="tpu_custom_call" | custom-call | tf_op jit(solution)/shard_map/pack_edges/pallas_call | solution.py:94
  6.1 4.9 %collective-permute-start.2 = (f32[3,80,256]{2,1,0:T(8,128)}, f32[3,80,256]{2,1,0:T(8,128)S(1)}, u32[]{:S(2)}, u32[]{:S(2)}) collective-permute-start(f32[3,80,256]{2,1,0:T(8,128)} %get-tuple-element.16.up_ref), channel_id=1, source_target_pairs={{0,1},{1,2},{2,3},{4,5},{5,6},{6,7},{8,9},{9,10},{10,11},{12,13},{... | collective-permute-start | bytes 737288 | tf_op jit(solution)/shard_map/ppermute | solution.py:434
  11.1 1.3 %collective-permute-start.3 = (f32[2,80,256]{2,1,0:T(8,128)}, f32[2,80,256]{2,1,0:T(8,128)S(1)}, u32[]{:S(2)}, u32[]{:S(2)}) collective-permute-start(f32[2,80,256]{2,1,0:T(8,128)} %get-tuple-element.17.down_ref), channel_id=1, source_target_pairs={{1,0},{2,1},{3,2},{5,4},{6,5},{7,6},{9,8},{10,9},{11,10},{13,12},{... | collective-permute-start | bytes 491528 | tf_op jit(solution)/shard_map/ppermute | solution.py:435
  12.4 1.3 %collective-permute-start.1 = (f32[32,256]{1,0:T(8,128)}, f32[32,256]{1,0:T(8,128)S(1)}, u32[]{:S(2)}, u32[]{:S(2)}) collective-permute-start(f32[32,256]{1,0:T(8,128)} %get-tuple-element.15.left_ref), channel_id=1, source_target_pairs={{4,0},{8,4},{12,8},{5,1},{9,5},{13,9},{6,2},{10,6},{14,10},{7,3},{... | collective-permute-start | bytes 98312 | tf_op jit(solution)/shard_map/ppermute | solution.py:433
  13.7 3.0 %collective-permute-start = (f32[32,384]{1,0:T(8,128)}, f32[32,384]{1,0:T(8,128)S(1)}, u32[]{:S(2)}, u32[]{:S(2)}) collective-permute-start(f32[32,384]{1,0:T(8,128)} %get-tuple-element.14.right_ref), channel_id=1, source_target_pairs={{0,4},{4,8},{8,12},{1,5},{5,9},{9,13},{2,6},{6,10},{10,14},{3,7},{... | collective-permute-start | bytes 147464 | tf_op jit(solution)/shard_map/ppermute | solution.py:432
  16.7 0.6 and_select_fusion.place_ref
  17.3 0.0 collective-permute-done.1.far_ref
  17.3 0.5 collective-permute-done.west_ref
  17.8 1.0 %collective-permute-done.3.ahead_ref = f32[2,80,256]{2,1,0:T(8,128)S(1)} collective-permute-done((f32[2,80,256]{2,1,0:T(8,128)}, f32[2,80,256]{2,1,0:T(8,128)S(1)}, u32[]{:S(2)}, u32[]{:S(2)}) %collective-permute-start.3) | collective-permute-done | bytes 163872 | tf_op jit(solution)/shard_map/ppermute | solution.py:435
  18.8 0.0 collective-permute-done.2.south_ref
  18.8 0.0 copy-done.6
  18.9 0.6 copy-done.1
  19.5 0.7 copy-done
  20.2 28.8 %step_and_bin.1 = (f32[75,32,256]{2,1,0:T(8,128)}, f32[9,16,128]{2,1,0:T(8,128)}, f32[9,16,128]{2,1,0:T(8,128)}, f32[9,16,128]{2,1,0:T(8,128)}, f32[9,16,128]{2,1,0:T(8,128)}) custom-call(s32[4]{0:T(128)} %and_select_fusion.place_ref, f32[75]{0:T(128)} %thick_ref.1, s32[32,256]{1,0:T(8,128)} %depth_ref.3, s32[32,256]{1,0:T(8,128)} %basin_ref.1, ...), custom_call_target="tpu_custom_call" | custom-call | tf_op jit(solution)/shard_map/step_and_bin/pallas_call | solution.py:354
  49.1 0.5 collective-permute-start.4
  49.6 2.2 %collective-permute-start.5 = (f32[9,16,128]{2,1,0:T(8,128)}, f32[9,16,128]{2,1,0:T(8,128)S(1)}, u32[]{:S(2)}, u32[]{:S(2)}) collective-permute-start(f32[9,16,128]{2,1,0:T(8,128)} %get-tuple-element.21), channel_id=1, source_target_pairs={{0,8},{4,12},{8,0},{12,4},{1,9},{5,13},{9,1},{13,5},{2,10},{6,14},... | collective-permute-start | bytes 221192 | tf_op jit(solution)/shard_map/ppermute | solution.py:447
  51.8 1.4 %collective-permute-start.6 = (f32[9,16,128]{2,1,0:T(8,128)}, f32[9,16,128]{2,1,0:T(8,128)S(1)}, u32[]{:S(2)}, u32[]{:S(2)}) collective-permute-start(f32[9,16,128]{2,1,0:T(8,128)} %get-tuple-element.22), channel_id=1, source_target_pairs={{0,12},{4,0},{8,4},{12,8},{1,13},{5,1},{9,5},{13,9},{2,14},{6,2},{... | collective-permute-start | bytes 221192 | tf_op jit(solution)/shard_map/ppermute | solution.py:447
  53.2 0.0 collective-permute-done.4.refs_1_
  53.2 1.5 %collective-permute-done.5.refs_2_ = f32[9,16,128]{2,1,0:T(8,128)S(1)} collective-permute-done((f32[9,16,128]{2,1,0:T(8,128)}, f32[9,16,128]{2,1,0:T(8,128)S(1)}, u32[]{:S(2)}, u32[]{:S(2)}) %collective-permute-start.5) | collective-permute-done | bytes 73760 | tf_op jit(solution)/shard_map/ppermute | solution.py:447
  54.7 1.0 %collective-permute-done.6.refs_3_ = f32[9,16,128]{2,1,0:T(8,128)S(1)} collective-permute-done((f32[9,16,128]{2,1,0:T(8,128)}, f32[9,16,128]{2,1,0:T(8,128)S(1)}, u32[]{:S(2)}, u32[]{:S(2)}) %collective-permute-start.6) | collective-permute-done | bytes 73760 | tf_op jit(solution)/shard_map/ppermute | solution.py:447
  55.7 0.7 fusion
  56.4 6.5 %collective-permute-start.9 = (f32[16,128]{1,0:T(8,128)S(1)}, f32[16,128]{1,0:T(8,128)S(1)}, u32[]{:S(2)}, u32[]{:S(2)}) collective-permute-start(f32[16,128]{1,0:T(8,128)S(1)} %fusion), channel_id=1, source_target_pairs={{0,3},{4,7},{8,11},{12,15},{16,19},{20,23},{24,27},{28,31}} | collective-permute-start | bytes 24584 | tf_op jit(solution)/shard_map/ppermute | solution.py:451
  62.9 1.3 %collective-permute-start.8 = (f32[16,128]{1,0:T(8,128)S(1)}, f32[16,128]{1,0:T(8,128)S(1)}, u32[]{:S(2)}, u32[]{:S(2)}) collective-permute-start(f32[16,128]{1,0:T(8,128)S(1)} %fusion), channel_id=1, source_target_pairs={{0,2},{1,3},{4,6},{5,7},{8,10},{9,11},{12,14},{13,15},{16,18},{17,... | collective-permute-start | bytes 24584 | tf_op jit(solution)/shard_map/ppermute | solution.py:451
  64.2 2.5 %collective-permute-start.7 = (f32[16,128]{1,0:T(8,128)S(1)}, f32[16,128]{1,0:T(8,128)S(1)}, u32[]{:S(2)}, u32[]{:S(2)}) collective-permute-start(f32[16,128]{1,0:T(8,128)S(1)} %fusion), channel_id=1, source_target_pairs={{0,1},{1,2},{2,3},{4,5},{5,6},{6,7},{8,9},{9,10},{10,11},{12,13},{... | collective-permute-start | bytes 24584 | tf_op jit(solution)/shard_map/ppermute | solution.py:451
  66.7 0.0 collective-permute-done.9.refs_6_
  66.7 0.0 copy-start.7
  66.7 0.0 collective-permute-done.8.refs_5_
  66.8 1.3 %collective-permute-done.7.refs_4_ = f32[16,128]{1,0:T(8,128)S(1)} collective-permute-done((f32[16,128]{1,0:T(8,128)S(1)}, f32[16,128]{1,0:T(8,128)S(1)}, u32[]{:S(2)}, u32[]{:S(2)}) %collective-permute-start.7) | collective-permute-done | bytes 8224 | tf_op jit(solution)/shard_map/ppermute | solution.py:451
  68.1 0.0 copy-done.3
  68.1 0.0 copy-done.7
  68.1 0.6 copy-done.9
  68.7 2.0 %close_sums.1 = (f32[5,8,192]{2,1,0:T(8,128)}, f32[5,8,192]{2,1,0:T(8,128)}) custom-call(f32[9,16,128]{2,1,0:T(8,128)} %get-tuple-element.19.refs_0_, f32[9,16,128]{2,1,0:T(8,128)} %copy-done.2, f32[9,16,128]{2,1,0:T(8,128)} %copy-done.3, f32[9,16,128]{2,1,0:T(8,128)} %copy-done.4, f32[16,128]{1,0:T(8,128)} %copy-done.9, f32[16,128]{1,0:T(8,128)} %copy-done.8, ...), custom_call_target="tpu_custom_call" | custom-call | tf_op jit(solution)/shard_map/close_sums/pallas_call | solution.py:412
  (13 shorter events, 0.0 us)
Async XLA Ops:
  6.1 12.7 %collective-permute-start.2 = (f32[3,80,256]{2,1,0:T(8,128)}, f32[3,80,256]{2,1,0:T(8,128)S(1)}, u32[]{:S(2)}, u32[]{:S(2)}) collective-permute-start(f32[3,80,256]{2,1,0:T(8,128)} %get-tuple-element.16.up_ref), channel_id=1, source_target_pairs={{0,1},{1,2},{2,3},{4,5},{5,6},{6,7},{8,9},{9,10},{10,11},{12,13},{... | collective-permute-start | bytes 737288 | tf_op jit(solution)/shard_map/ppermute | solution.py:434
  11.1 7.8 %collective-permute-start.3 = (f32[2,80,256]{2,1,0:T(8,128)}, f32[2,80,256]{2,1,0:T(8,128)S(1)}, u32[]{:S(2)}, u32[]{:S(2)}) collective-permute-start(f32[2,80,256]{2,1,0:T(8,128)} %get-tuple-element.17.down_ref), channel_id=1, source_target_pairs={{1,0},{2,1},{3,2},{5,4},{6,5},{7,6},{9,8},{10,9},{11,10},{13,12},{... | collective-permute-start | bytes 491528 | tf_op jit(solution)/shard_map/ppermute | solution.py:435
  12.4 4.9 %collective-permute-start.1 = (f32[32,256]{1,0:T(8,128)}, f32[32,256]{1,0:T(8,128)S(1)}, u32[]{:S(2)}, u32[]{:S(2)}) collective-permute-start(f32[32,256]{1,0:T(8,128)} %get-tuple-element.15.left_ref), channel_id=1, source_target_pairs={{4,0},{8,4},{12,8},{5,1},{9,5},{13,9},{6,2},{10,6},{14,10},{7,3},{... | collective-permute-start | bytes 98312 | tf_op jit(solution)/shard_map/ppermute | solution.py:433
  13.7 4.1 %collective-permute-start = (f32[32,384]{1,0:T(8,128)}, f32[32,384]{1,0:T(8,128)S(1)}, u32[]{:S(2)}, u32[]{:S(2)}) collective-permute-start(f32[32,384]{1,0:T(8,128)} %get-tuple-element.14.right_ref), channel_id=1, source_target_pairs={{0,4},{4,8},{8,12},{1,5},{5,9},{9,13},{2,6},{6,10},{10,14},{3,7},{... | collective-permute-start | bytes 147464 | tf_op jit(solution)/shard_map/ppermute | solution.py:432
  17.3 1.5 %copy-start.6 = (f32[32,256]{1,0:T(8,128)}, f32[32,256]{1,0:T(8,128)S(1)}, u32[]{:S(2)}) copy-start(f32[32,256]{1,0:T(8,128)S(1)} %collective-permute-done.1.far_ref) | copy-start | bytes 98308
  17.8 1.1 %copy-start.5 = (f32[32,384]{1,0:T(8,128)}, f32[32,384]{1,0:T(8,128)S(1)}, u32[]{:S(2)}) copy-start(f32[32,384]{1,0:T(8,128)S(1)} %collective-permute-done.west_ref) | copy-start | bytes 147460
  18.8 0.7 copy-start.1
  19.5 0.7 copy-start
  49.1 4.1 %collective-permute-start.4 = (f32[9,16,128]{2,1,0:T(8,128)}, f32[9,16,128]{2,1,0:T(8,128)S(1)}, u32[]{:S(2)}, u32[]{:S(2)}) collective-permute-start(f32[9,16,128]{2,1,0:T(8,128)} %get-tuple-element.20), channel_id=1, source_target_pairs={{0,4},{4,8},{8,12},{12,0},{1,5},{5,9},{9,13},{13,1},{2,6},{6,10},{... | collective-permute-start | bytes 221192 | tf_op jit(solution)/shard_map/ppermute | solution.py:447
  49.6 5.1 %collective-permute-start.5 = (f32[9,16,128]{2,1,0:T(8,128)}, f32[9,16,128]{2,1,0:T(8,128)S(1)}, u32[]{:S(2)}, u32[]{:S(2)}) collective-permute-start(f32[9,16,128]{2,1,0:T(8,128)} %get-tuple-element.21), channel_id=1, source_target_pairs={{0,8},{4,12},{8,0},{12,4},{1,9},{5,13},{9,1},{13,5},{2,10},{6,14},... | collective-permute-start | bytes 221192 | tf_op jit(solution)/shard_map/ppermute | solution.py:447
  51.8 3.9 %collective-permute-start.6 = (f32[9,16,128]{2,1,0:T(8,128)}, f32[9,16,128]{2,1,0:T(8,128)S(1)}, u32[]{:S(2)}, u32[]{:S(2)}) collective-permute-start(f32[9,16,128]{2,1,0:T(8,128)} %get-tuple-element.22), channel_id=1, source_target_pairs={{0,12},{4,0},{8,4},{12,8},{1,13},{5,1},{9,5},{13,9},{2,14},{6,2},{... | collective-permute-start | bytes 221192 | tf_op jit(solution)/shard_map/ppermute | solution.py:447
  53.2 14.9 %copy-start.2 = (f32[9,16,128]{2,1,0:T(8,128)}, f32[9,16,128]{2,1,0:T(8,128)S(1)}, u32[]{:S(2)}) copy-start(f32[9,16,128]{2,1,0:T(8,128)S(1)} %collective-permute-done.4.refs_1_) | copy-start | bytes 221188
  54.7 13.4 %copy-start.3 = (f32[9,16,128]{2,1,0:T(8,128)}, f32[9,16,128]{2,1,0:T(8,128)S(1)}, u32[]{:S(2)}) copy-start(f32[9,16,128]{2,1,0:T(8,128)S(1)} %collective-permute-done.5.refs_2_) | copy-start | bytes 221188
  55.7 12.4 %copy-start.4 = (f32[9,16,128]{2,1,0:T(8,128)}, f32[9,16,128]{2,1,0:T(8,128)S(1)}, u32[]{:S(2)}) copy-start(f32[9,16,128]{2,1,0:T(8,128)S(1)} %collective-permute-done.6.refs_3_) | copy-start | bytes 221188
  56.4 10.3 %collective-permute-start.9 = (f32[16,128]{1,0:T(8,128)S(1)}, f32[16,128]{1,0:T(8,128)S(1)}, u32[]{:S(2)}, u32[]{:S(2)}) collective-permute-start(f32[16,128]{1,0:T(8,128)S(1)} %fusion), channel_id=1, source_target_pairs={{0,3},{4,7},{8,11},{12,15},{16,19},{20,23},{24,27},{28,31}} | collective-permute-start | bytes 24584 | tf_op jit(solution)/shard_map/ppermute | solution.py:451
  62.9 3.8 %collective-permute-start.8 = (f32[16,128]{1,0:T(8,128)S(1)}, f32[16,128]{1,0:T(8,128)S(1)}, u32[]{:S(2)}, u32[]{:S(2)}) collective-permute-start(f32[16,128]{1,0:T(8,128)S(1)} %fusion), channel_id=1, source_target_pairs={{0,2},{1,3},{4,6},{5,7},{8,10},{9,11},{12,14},{13,15},{16,18},{17,... | collective-permute-start | bytes 24584 | tf_op jit(solution)/shard_map/ppermute | solution.py:451
  64.2 3.8 %collective-permute-start.7 = (f32[16,128]{1,0:T(8,128)S(1)}, f32[16,128]{1,0:T(8,128)S(1)}, u32[]{:S(2)}, u32[]{:S(2)}) collective-permute-start(f32[16,128]{1,0:T(8,128)S(1)} %fusion), channel_id=1, source_target_pairs={{0,1},{1,2},{2,3},{4,5},{5,6},{6,7},{8,9},{9,10},{10,11},{12,13},{... | collective-permute-start | bytes 24584 | tf_op jit(solution)/shard_map/ppermute | solution.py:451
  66.7 1.3 %copy-start.7 = (f32[16,128]{1,0:T(8,128)}, f32[16,128]{1,0:T(8,128)S(1)}, u32[]{:S(2)}) copy-start(f32[16,128]{1,0:T(8,128)S(1)} %collective-permute-done.9.refs_6_) | copy-start | bytes 24580
  66.8 1.3 %copy-start.8 = (f32[16,128]{1,0:T(8,128)}, f32[16,128]{1,0:T(8,128)S(1)}, u32[]{:S(2)}) copy-start(f32[16,128]{1,0:T(8,128)S(1)} %collective-permute-done.8.refs_5_) | copy-start | bytes 24580
  68.1 0.6 copy-start.9

commit v3 on v2

v3 whole, which is shorter than its diff:
```python
import functools
import math

import jax
import jax.numpy as jnp
from jax import lax
from jax.experimental import pallas as pl
from jax.experimental.pallas import tpu as pltpu
from jax.sharding import PartitionSpec as P

C = 192
B = 5
DIFFUSION = 0.1

LANES = 128
LOW = 64
HIGH = C // LOW
HEADS = 16
PER = 5
SLOTS = 5
VMEM = 63 << 20
F32 = jnp.float32
BF16 = jnp.bfloat16


def lane_ids(shape):
    return lax.broadcasted_iota(jnp.int32, shape, len(shape) - 1)


def row_ids(shape):
    return lax.broadcasted_iota(jnp.int32, shape, len(shape) - 2)


def flux_of(here, slope, bend, bend_ahead, speed):
    value = here + 0.5 * slope - jnp.where(speed > 0.0, bend, bend_ahead)
    return speed * value - DIFFUSION * slope


def sixth(behind, here, ahead):
    return ((ahead - here) - (here - behind)) * (1.0 / 6.0)


def rows_kernel(south_ref, north_ref, speed_ref, depth_ref, up_ref, down_ref):
    levels = south_ref.shape[0]
    rows = depth_ref.shape[0]

    def level(k, carry):
        here = pl.ds(k, 1)
        lower = jnp.where(k < depth_ref[0:8], south_ref[k], 0.0)
        upper = jnp.where(k < depth_ref[rows - 8 :], north_ref[k], 0.0)
        up_ref[0, here, :] = upper[6:7]
        up_ref[1, here, :] = upper[7:8]
        up_ref[2, here, :] = speed_ref[k, 7:8, :]
        down_ref[0, here, :] = lower[0:1]
        down_ref[1, here, :] = lower[1:2]
        return carry

    lax.fori_loop(0, levels, level, 0, unroll=15)
    up_ref[0, levels : levels + 1, :] = depth_ref[rows - 1 : rows].astype(F32)
    down_ref[0, levels : levels + 1, :] = depth_ref[0:1].astype(F32)


def pack_rows(tracer, v_flow, depth):
    levels, rows, cols = tracer.shape
    tall = (levels + 8) // 8 * 8
    shapes = [(3, tall, cols), (2, tall, cols)]
    return pl.pallas_call(
        rows_kernel,
        grid=(1,),
        in_specs=[
            pl.BlockSpec((levels, 8, cols), lambda i: (0, 0, 0)),
            pl.BlockSpec((levels, 8, cols), lambda i: (0, rows // 8 - 1, 0)),
            pl.BlockSpec((levels, 8, cols), lambda i: (0, rows // 8 - 1, 0)),
            pl.BlockSpec((rows, cols), lambda i: (0, 0)),
        ],
        out_specs=[pl.BlockSpec(s, lambda i: (0, 0, 0)) for s in shapes],
        out_shape=[jax.ShapeDtypeStruct(s, F32) for s in shapes],
        compiler_params=pltpu.CompilerParams(vmem_limit_bytes=VMEM),
        name="pack_rows",
    )(tracer, tracer, v_flow, depth)


def columns_kernel(tracer_ref, east_ref, depth_ref, side_ref):
    per, rows, cols = tracer_ref.shape
    step = pl.program_id(0)
    lanes = lane_ids((rows, LANES))
    owner, slot = (lanes // SLOTS, lanes % SLOTS)
    depth = depth_ref[...]
    near, away = (depth[:, :LANES], depth[:, cols - LANES :])
    deep = jnp.where(lanes < LANES // 2, near, away)
    value = pltpu.roll(deep.astype(F32), SLOTS * per + 2, 1)
    for q in range(per):
        k = step * per + q
        ends = jnp.where(lanes < LANES // 2, tracer_ref[q, :, :LANES], tracer_ref[q, :, cols - LANES :])
        turned = pltpu.roll(jnp.where(k < deep, ends, 0.0), SLOTS * q + 2, 1)
        turned = jnp.where(slot == SLOTS - 1, pltpu.roll(east_ref[q], SLOTS * q + SLOTS, 1), turned)
        value = jnp.where(owner == q, turned, value)
    side_ref[:, pl.ds(pl.multiple_of(step * LANES, LANES), LANES)] = value


def levels_of_tile(levels):
    return next(n for n in range((LANES - 3) // SLOTS, 0, -1) if levels % n == 0)


def pack_columns(tracer, u_flow, depth):
    levels, rows, cols = tracer.shape
    per = levels_of_tile(levels)
    tiles = levels // per
    return pl.pallas_call(
        columns_kernel,
        grid=(tiles,),
        in_specs=[
            pl.BlockSpec((per, rows, cols), lambda i: (i, 0, 0)),
            pl.BlockSpec((per, rows, LANES), lambda i: (i, 0, cols // LANES - 1)),
            pl.BlockSpec((rows, cols), lambda i: (0, 0)),
        ],
        out_specs=pl.BlockSpec((rows, tiles * LANES), lambda i: (0, 0)),
        out_shape=jax.ShapeDtypeStruct((rows, tiles * LANES), F32),
        compiler_params=pltpu.CompilerParams(vmem_limit_bytes=VMEM),
        name="pack_columns",
    )(tracer, u_flow, depth)


def main_kernel(
    thick_ref, depth_ref, basin_ref, side_ref, up_ref, down_ref,
    west_hbm, far_hbm, south_hbm, ahead_hbm, tracer_hbm, east_hbm, north_hbm, class_hbm,
    *refs,
):
    scratch = 26 + 12
    next_hbm, total_ref, *piece_refs = refs[: len(refs) - scratch]
    (
        tracer_ref, east_ref, north_ref, class_ref, next_ref, in_sem, out_sem, halo_sem,
        west_ref, far_ref, south_ref, ahead_ref,
        head_ref, zonal_ref, merid_ref, far_value, far_bend, west_slope, west_flux,
        ahead_value, ahead_bend, south_value, south_flux,
        sums_ref, tall_ref, share_ref,
    ) = refs[len(refs) - scratch : len(refs) - 12]
    stages = refs[len(refs) - 12 :]
    levels, rows, cols = tracer_ref.shape
    halves = cols // LANES
    per = stages[0].shape[0]
    chunks = levels // per
    parts = len(piece_refs)
    share = rows // parts
    place = lax.axis_index("lon")
    lat = lax.axis_index("lat")

    bounds = [(0, per)] + [(per * (2 * i + 1), min(2 * per, levels - per * (2 * i + 1))) for i in range(chunks // 2)]
    size = {n for _, n in bounds[1:]}
    assert len(size) == 1
    size = size.pop()

    def span(piece):
        if isinstance(piece, int) and piece == 0:
            return pl.ds(0, per)
        return pl.ds(per + (piece - 1) * size, size)

    sources = ((tracer_hbm, tracer_ref), (east_hbm, east_ref), (north_hbm, north_ref), (class_hbm, class_ref))
    halos = ((west_hbm, west_ref), (far_hbm, far_ref), (south_hbm, south_ref), (ahead_hbm, ahead_ref))

    def copies_in(piece):
        return [
            pltpu.make_async_copy(src.at[span(piece)], dst.at[span(piece)], in_sem.at[piece, i])
            for i, (src, dst) in enumerate(sources)
        ]

    def copy_out(piece):
        return pltpu.make_async_copy(next_ref.at[span(piece)], next_hbm.at[span(piece)], out_sem.at[piece])

    pieces = len(bounds)
    edges = [pltpu.make_async_copy(src, dst, halo_sem.at[i]) for i, (src, dst) in enumerate(halos)]
    for copy in edges:
        copy.start()
    for piece in range(pieces):
        for copy in copies_in(piece):
            copy.start()
    for copy in edges:
        copy.wait()

    span_of = levels_of_tile(levels)
    tiles = levels // span_of
    lanes = lane_ids((rows, LANES))
    slots = lanes % SLOTS
    depth = depth_ref[...].astype(F32)
    has_west, has_far = (place > 0, place < parts - 1)
    for tile in range(tiles):
        part = slice(tile * LANES, (tile + 1) * LANES)
        own = side_ref[:, part]
        west = jnp.where(has_west, west_ref[:, part], 0.0)
        far = jnp.where(has_far, far_ref[:, part], 0.0)
        speed = pltpu.roll(west, LANES - SLOTS + 2, 1)

        def beside(x):
            return pltpu.roll(x, LANES - 1, 1)

        def curve(x):
            return sixth(pltpu.roll(x, 1, 1), x, beside(x))

        right = jnp.where(slots < 2, own, far)
        far_value[:, part] = right
        far_bend[:, part] = curve(right)
        left = jnp.where(slots < 2, west, own)
        slope = beside(left) - left
        west_slope[:, part] = slope
        bend = curve(left)
        flux = flux_of(left, slope, bend, beside(bend), speed)
        lane = SLOTS * span_of
        faces = jnp.minimum(west[:, lane + 1 : lane + 2], depth[:, :1])
        west_flux[:, part] = jnp.where((lanes // SLOTS + tile * span_of).astype(F32) < faces, flux, 0.0)
        if tile == 0:
            wide = lane_ids((rows, cols))
            after = jnp.where(wide == cols - 1, far[:, lane + 2 : lane + 3], pltpu.roll(depth, cols - 1, 1))
            zonal_ref[...] = jnp.minimum(depth, after).astype(jnp.int32)

    has_south, has_ahead = (lat > 0, lat < lax.axis_size("lat") - 1)
    first, second = (down_ref[0], down_ref[1])
    here = jnp.where(has_south, south_ref[1], 0.0)
    behind = jnp.where(has_south, south_ref[0], 0.0)
    speed = jnp.where(has_south, south_ref[2], 0.0)
    beyond = jnp.where(has_ahead, ahead_ref[0], 0.0)
    south_value[...] = here
    ahead_value[...] = beyond
    ahead_bend[...] = sixth(up_ref[1], beyond, jnp.where(has_ahead, ahead_ref[1], 0.0))
    flux = flux_of(here, first - here, sixth(behind, here, first), sixth(here, first, second), speed)
    faces = jnp.minimum(behind[levels : levels + 1, :], depth[0:1])
    south_flux[...] = jnp.where(row_ids(flux.shape).astype(F32) < faces, flux, 0.0)
    above = pltpu.roll(depth, rows - 1, 0)
    above = jnp.where(row_ids((rows, cols)) == rows - 1, beyond[levels : levels + 1, :], above)
    merid_ref[...] = jnp.minimum(depth, above).astype(jnp.int32)
    head_ref[...] = basin_ref[...] * HIGH

    top = 8
    inner = pl.ds(top, rows)

    def level(chunk, q, stage):
        flow_hi, flow_lo, gain_hi, gain_lo, head_key, low_key = stage
        k = chunk * per + q
        thick = thick_ref[k]
        here = pl.ds(k, 1)
        edge = lane_ids((rows, LANES))
        at_end, at_start = (edge == LANES - 1, edge == 0)

        def split(array):
            return [array[:, h * LANES : (h + 1) * LANES] for h in range(halves)]

        def turn_back(blocks, outside):
            turned = [pltpu.roll(x, LANES - 1, 1) for x in blocks] + [outside]
            return [jnp.where(at_end, turned[h + 1], turned[h]) for h in range(halves)]

        def turn_on(blocks, outside):
            turned = [outside] + [pltpu.roll(x, 1, 1) for x in blocks]
            return [jnp.where(at_start, turned[h], turned[h + 1]) for h in range(halves)]

        tile = pl.ds(pl.multiple_of(k // span_of * LANES, LANES), LANES)
        slot = SLOTS * (k % span_of)

        def to_end(ref):
            return pltpu.roll(ref[:, tile], LANES - 3 - slot, 1)

        def to_start(ref):
            return pltpu.roll(ref[:, tile], LANES - 1 - slot, 1)

        depth = split(depth_ref[...])
        raw = split(tracer_ref[k])
        wet = [k < d for d in depth]
        masked = [jnp.where(w, x, 0.0) for w, x in zip(wet, raw)]

        ahead = turn_back(masked, to_end(far_value))
        slope = [a - x for a, x in zip(ahead, masked)]
        slope_behind = turn_on(slope, to_start(west_slope))
        bend = [(a - b) * (1.0 / 6.0) for a, b in zip(slope, slope_behind)]
        bend_ahead = turn_back(bend, to_end(far_bend))
        speed = split(east_ref[k])
        shut = [k >= d for d in split(zonal_ref[...])]
        flux = [
            jnp.where(s, 0.0, flux_of(*x)) for s, *x in zip(shut, masked, slope, bend, bend_ahead, speed)
        ]
        flux_behind = turn_on(flux, to_start(west_flux))
        left_over = [m - (a - b) for m, a, b in zip(masked, flux, flux_behind)]

        north = split(north_ref[k])
        shut = [k >= d for d in split(merid_ref[...])]
        classes = split(class_ref[k])
        heads = split(head_ref[...])
        below, over = (split(south_value[here, :]), split(ahead_value[here, :]))
        over_bend, below_flux = (split(ahead_bend[here, :]), split(south_flux[here, :]))
        for h in range(halves):
            part = slice(h * LANES, (h + 1) * LANES)
            rows_of = tall_ref.at[q, h]
            rows_of[0, inner, :] = masked[h]
            rows_of[0, top - 1 : top, :] = below[h]
            rows_of[0, top + rows : top + rows + 1, :] = over[h]
            slope = rows_of[0, pl.ds(top + 1, rows), :] - masked[h]
            slope_behind = masked[h] - rows_of[0, pl.ds(top - 1, rows), :]
            bend = (slope - slope_behind) * (1.0 / 6.0)
            rows_of[1, inner, :] = bend
            rows_of[1, top + rows : top + rows + 1, :] = over_bend[h]
            bend_ahead = rows_of[1, pl.ds(top + 1, rows), :]
            flux = jnp.where(shut[h], 0.0, flux_of(masked[h], slope, bend, bend_ahead, north[h]))
            rows_of[2, inner, :] = flux
            rows_of[2, top - 1 : top, :] = below_flux[h]
            flux_behind = rows_of[2, pl.ds(top - 1, rows), :]
            updated = jnp.where(wet[h], left_over[h] - (flux - flux_behind), 0.0)
            next_ref[k, :, part] = updated
            flow = jnp.where(shut[h], 0.0, north[h] * thick)
            gain = (updated - masked[h]) * thick
            upper = flow.astype(BF16).astype(F32)
            flow_hi[q, :, part] = flow
            flow_lo[q, :, part] = flow - upper
            upper = gain.astype(BF16).astype(F32)
            gain_hi[q, :, part] = gain
            gain_lo[q, :, part] = gain - upper
            head_key[q, :, part] = (heads[h] + (classes[h] >> 6)).astype(F32)
            low_key[q, :, part] = (classes[h] & (LOW - 1)).astype(F32)

    half = HEADS // 2
    order = row_ids((HEADS, cols))
    heads = [(order % half + g * half).astype(F32).astype(BF16) for g in range(2)]
    lows = row_ids((LOW, cols)).astype(F32).astype(BF16)
    ones = jnp.ones((LOW, cols), BF16)
    none = jnp.zeros((LOW, cols), BF16)

    def spread(ref, q, r, count):
        return jnp.broadcast_to(ref[q, r : r + 1, :], (count, cols))

    def bin_row(r, stage, fresh):
        *terms, head_key, low_key = stage
        first, second = ([], [])
        for q in range(per):
            key = spread(head_key, q, r, HEADS).astype(BF16)
            hot = [key == g for g in heads]
            tiles = []
            for upper, lower in (terms[:2], terms[2:]):
                value = jnp.concatenate([spread(upper, q, r, half), spread(lower, q, r, half)], 0).astype(BF16)
                tiles += [jnp.where(g, value, none[:HEADS]) for g in hot]
            first.append(jnp.concatenate(tiles, 0))
            second.append(jnp.where(spread(low_key, q, r, LOW).astype(BF16) == lows, ones, none))
        total = lax.dot_general(
            jnp.concatenate(first, 1),
            jnp.concatenate(second, 1),
            (((1,), (1,)), ((), ())),
            preferred_element_type=F32,
        )
        sums_ref[r] = jnp.where(fresh, total, total + sums_ref[r])

    both = (stages[:6], stages[6:])

    def work(chunk, stage_in, stage_out, fresh=None):
        done = 0
        for q in range(per):
            until = (q + 1) * rows // per
            if stage_out is not None:
                for r in range(done, until):
                    bin_row(r, stage_out, fresh)
            if stage_in is not None:
                level(chunk, q, stage_in)
            done = until

    for copy in copies_in(0):
        copy.wait()
    work(0, both[0], None)
    copy_out(0).start()

    def pair(i, carry):
        for copy in copies_in(i + 1):
            copy.wait()
        for j in range(size // per):
            work(2 * i + 1 + j, both[(1 + j) % 2], both[j % 2], 2 * i + j == 0)
        copy_out(i + 1).start()
        return carry

    lax.fori_loop(0, pieces - 1, pair, 0)
    work(0, None, both[(chunks - 1) % 2], place < 0)
    running = jnp.zeros((HEADS, LOW), F32)
    for r in range(rows):
        tiles = [sums_ref[r, pl.ds(i * half, half)] for i in range(8)]
        joined = [tiles[2 * i] + tiles[2 * i + 1] for i in range(4)]
        flow = jnp.concatenate(joined[:2], 0)
        running = running + jnp.concatenate(joined[2:], 0)
        share_ref[r] = jnp.concatenate([flow, running], 1)
    for d in range(parts):
        owner = lax.rem(place + d, parts)
        piece_refs[d][...] = share_ref[pl.ds(owner * share, share)]
    total_ref[...] = share_ref[rows - 1]
    for piece in range(pieces):
        copy_out(piece).wait()


def step_and_bin(parts, thick, depth, basins, edges, fields):
    levels, rows, cols = fields[0].shape
    per = next(n for n in range(PER, 0, -1) if levels % n == 0)
    pieces = 1 + levels // per // 2
    halves = cols // LANES
    tall = edges[1].shape[1]
    share = rows // parts

    def vmem(shape, dtype=F32):
        return pltpu.VMEM(shape, dtype)

    whole = vmem((levels, rows, cols))
    compact = vmem((rows, levels // levels_of_tile(levels) * LANES))
    row = vmem((tall, cols))
    level = vmem((rows, cols), jnp.int32)
    piece = (share, HEADS, 2 * LOW)
    return pl.pallas_call(
        main_kernel,
        in_specs=[pl.BlockSpec(memory_space=pltpu.SMEM)]
        + [pl.BlockSpec(memory_space=pltpu.VMEM)] * 5
        + [pl.BlockSpec(memory_space=pl.ANY)] * 8,
        out_specs=[pl.BlockSpec(memory_space=pl.ANY)] + [pl.BlockSpec(memory_space=pltpu.VMEM)] * (parts + 1),
        out_shape=[jax.ShapeDtypeStruct(s, F32) for s in [(levels, rows, cols), piece[1:]] + [piece] * parts],
        scratch_shapes=[
            whole, whole, whole, vmem((levels, rows, cols), jnp.int32), whole,
            pltpu.SemaphoreType.DMA((pieces, 4)),
            pltpu.SemaphoreType.DMA((pieces,)),
            pltpu.SemaphoreType.DMA((4,)),
        ]
        + [vmem(edge.shape) for edge in edges[3:]]
        + [
            level, level, level,
            compact, compact, compact, compact,
            row, row, row, row,
            vmem((rows, 4 * HEADS, LOW)),
            vmem((per, halves, 3, rows + 16, LANES)),
            vmem((rows, HEADS, 2 * LOW)),
        ]
        + [vmem((per, rows, cols))] * 12,
        compiler_params=pltpu.CompilerParams(vmem_limit_bytes=VMEM),
        name="step_and_bin",
    )(thick, depth, basins, *edges, *fields)


def close_kernel(scales, pieces, carries, *refs):
    count = pieces + carries
    sources, (over_ref, tend_ref), landed = (refs[:count], refs[count : count + 2], refs[count + 2 : 2 * count + 2])
    up_ref, run_ref, sem = refs[2 * count + 2 :]
    copies = [pltpu.make_async_copy(src, dst, sem.at[i]) for i, (src, dst) in enumerate(zip(sources, landed))]
    for copy in copies:
        copy.start()
    source = row_ids((2 * LOW, 2 * LOW))
    target = lane_ids((2 * LOW, 2 * LOW))
    after = ((source < LOW) & ((target >= LOW) | (source >= target))).astype(F32)
    for copy in copies:
        copy.wait()
    piece_refs, carry_refs = (landed[:pieces], landed[pieces:])
    share = piece_refs[0].shape[0]
    total = piece_refs[0][...]
    for ref in piece_refs[1:]:
        total = total + ref[...]
    total = total.reshape(share * HEADS, 2 * LOW)
    up_ref[...] = jnp.dot(total, after, precision=lax.Precision.HIGHEST, preferred_element_type=F32)
    run_ref[...] = total
    carry = jnp.zeros((HEADS, 2 * LOW), F32)
    for ref in carry_refs:
        carry = carry + ref[...]
    for b in range(B):
        above = jnp.zeros((share, LOW), F32)
        for high in reversed(range(HIGH)):
            head = b * HIGH + high
            rows = up_ref[pl.ds(head, share, HEADS), :]
            over_ref[b, :, high * LOW : (high + 1) * LOW] = (rows[:, :LOW] + above) * scales[0]
            above = above + rows[:, LOW:]
            rows = run_ref[pl.ds(head, share, HEADS), :] + carry[head : head + 1]
            tend_ref[b, :, high * LOW : (high + 1) * LOW] = rows[:, LOW:] * scales[1]


def close(pieces, carries, scales):
    share = pieces[0].shape[0]
    out = jax.ShapeDtypeStruct((B, share, C), F32)
    inputs = (*pieces, *carries)
    scratch = pltpu.VMEM((share * HEADS, 2 * LOW), F32)
    return pl.pallas_call(
        functools.partial(close_kernel, scales, len(pieces), len(carries)),
        in_specs=[pl.BlockSpec(memory_space=pl.ANY)] * len(inputs),
        out_shape=[out, out],
        scratch_shapes=[pltpu.VMEM(x.shape, F32) for x in inputs]
        + [scratch, scratch, pltpu.SemaphoreType.DMA((len(inputs),))],
        compiler_params=pltpu.CompilerParams(vmem_limit_bytes=VMEM),
        name="close_sums",
    )(*inputs)


def turn(count, step):
    return [(i, (i + step) % count) for i in range(count)]


def body(tracer, u_flow, v_flow, depth_levels, class_index, basin_index, level_thickness):
    levels, rows, cols = tracer.shape
    lons, lats = (lax.axis_size("lon"), lax.axis_size("lat"))
    up, down = pack_rows(tracer, v_flow, depth_levels)
    south = lax.ppermute(up, "lat", turn(lats, 1))
    ahead = lax.ppermute(down, "lat", turn(lats, -1))
    side = pack_columns(tracer, u_flow, depth_levels)
    west = lax.ppermute(side, "lon", turn(lons, 1))
    far = lax.ppermute(side, "lon", turn(lons, -1))
    tracer_next, block_total, *pieces = step_and_bin(
        lons,
        level_thickness,
        depth_levels,
        basin_index,
        (side, up, down, west, far, south, ahead),
        (tracer, u_flow, v_flow, class_index),
    )
    pieces = pieces[:1] + [lax.ppermute(pieces[d], "lon", turn(lons, d)) for d in range(1, lons)]
    lat = lax.axis_index("lat")
    carry = jnp.zeros((HEADS, 2 * LOW), F32)
    for d in range(1, lats):
        carry = carry + jnp.where(lat >= d, lax.ppermute(block_total, "lat", turn(lats, d)), 0.0)
    carries = [carry] + [lax.ppermute(carry, "lon", turn(lons, d)) for d in range(1, lons)]
    unit = 1.0 / math.sqrt(cols * lons * levels)
    overturning, tendency = close(pieces, carries, (16.0 * unit, 4.0 * unit))
    return (tracer_next, overturning, tendency)


def solution(mesh):
    return jax.shard_map(
        body,
        mesh=mesh,
        in_specs=(
            P("member", "lat", "lon"),
            P("member", "lat", "lon"),
            P("member", "lat", "lon"),
            P(("member", "lat"), "lon"),
            P("member", "lat", "lon"),
            P(("member", "lat"), "lon"),
            P(),
        ),
        out_specs=(
            P("member", "lat", "lon"),
            P("member", ("lat", "lon"), None),
            P("member", ("lat", "lon"), None),
        ),
        check_vma=False,
    )
```

time: 71.1 us -> 65 us (0.914)
  starting transfers between devices: 25 us -> 15.1 us
  Pallas kernels: 36.4 us -> 39.2 us
  waiting for transfers between devices: 5.36 us -> 6.96 us
  other arithmetic: 1.29 us -> 0.01 us
    ppermute x10 -> x13, starting transfers between devices: 25 us -> 15.1 us  [the longest x3 4.15 us: body(): lax.ppermute(block_total, 'lat', turn(lats, d))]
    pallas_call x1, Pallas kernels: 28.8 us -> 31 us  [step_and_bin(): pl.pallas_call(main_kernel, in_specs=[pl.BlockSpec(memory_space=pltpu.SME...]
    ppermute x10 -> x13, waiting for transfers between devices: 5.36 us -> 6.96 us  [the longest x3 3.27 us: body(): lax.ppermute(carry, 'lon', turn(lons, d))]
    pallas_call x2 -> x3, Pallas kernels: 7.51 us -> 8.2 us  [the longest x1 3.71 us: pack_columns(): pl.pallas_call(columns_kernel, grid=(tiles,), in_specs=[pl.BlockSpec((per...]
    unnamed x20 -> x22, local copies, waits for them, and re-layouts: 1.94 us -> 1.99 us
  transfers between devices with their start and end apart: 10 -> 13, of which waited for: 5 -> 6; matrix products, arithmetic and copies ran while one was open for 1% -> 0% of each run, Pallas kernels for 0% -> 6%
where the time goes in v3:
time: 65 us; the launch traced here: 63.9 us
  Pallas kernels  39.2 us (60%)
  starting transfers between devices  15.1 us (23%)
  waiting for transfers between devices  6.96 us (11%)
  local copies, waits for them, and re-layouts  1.99 us (3%)
  between operations  0.74 us (1%)
    pallas_call x1, Pallas kernels, step_and_bin(): pl.pallas_call(main_kernel, in_specs=[pl.BlockSpec(memory_space=pltpu.SME...  31 us
    ppermute x3, starting transfers between devices, body(): lax.ppermute(block_total, 'lat', turn(lats, d))  4.15 us
    pallas_call x1, Pallas kernels, pack_columns(): pl.pallas_call(columns_kernel, grid=(tiles,), in_specs=[pl.BlockSpec((per...  3.71 us
    ppermute x3, waiting for transfers between devices, body(): lax.ppermute(carry, 'lon', turn(lons, d))  3.27 us
    ppermute x1, starting transfers between devices, body(): south = lax.ppermute(up, 'lat', turn(lats, 1))  3.02 us
    ppermute x3, starting transfers between devices, body(): lax.ppermute(pieces[d], 'lon', turn(lons, d))  2.92 us
    pallas_call x1, Pallas kernels, pack_rows(): pl.pallas_call(rows_kernel, grid=(1,), in_specs=[pl.BlockSpec((levels, 8,...  2.5 us
    ppermute x1, starting transfers between devices, body(): ahead = lax.ppermute(down, 'lat', turn(lats, -1))  2.03 us
  transfers between devices with their start and end apart: 13, of which 6 were waited for; matrix products, arithmetic and copies ran while one was open for 0% of the time, Pallas kernels for 6%

profile of v3, /device:TPU:0, one launch (start us, length us, event | category | flops | bytes accessed | tf_op | source)
XLA Modules:
  0.0 63.9 jit_solution(7346420059453055457)
XLA Ops:
  0.6 2.5 %pack_rows.1 = (f32[3,80,256]{2,1,0:T(8,128)}, f32[2,80,256]{2,1,0:T(8,128)}) custom-call(f32[75,32,256]{2,1,0:T(8,128)} %tracer_hbm.1, f32[75,32,256]{2,1,0:T(8,128)} %tracer_hbm.1, f32[75,32,256]{2,1,0:T(8,128)} %north_hbm.1, s32[32,256]{1,0:T(8,128)} %depth_ref.5), custom_call_target="tpu_custom_call" | custom-call | tf_op jit(solution)/shard_map/pack_rows/pallas_call | solution.py:67
  3.1 3.0 %collective-permute-start.2 = (f32[3,80,256]{2,1,0:T(8,128)}, f32[3,80,256]{2,1,0:T(8,128)S(1)}, u32[]{:S(2)}, u32[]{:S(2)}) collective-permute-start(f32[3,80,256]{2,1,0:T(8,128)} %get-tuple-element.13.up_ref), channel_id=1, source_target_pairs={{0,1},{1,2},{2,3},{3,0},{4,5},{5,6},{6,7},{7,4},{8,9},{9,10},{10,1... | collective-permute-start | bytes 737288 | tf_op jit(solution)/shard_map/ppermute | solution.py:491
  6.2 2.0 %collective-permute-start.3 = (f32[2,80,256]{2,1,0:T(8,128)}, f32[2,80,256]{2,1,0:T(8,128)S(1)}, u32[]{:S(2)}, u32[]{:S(2)}) collective-permute-start(f32[2,80,256]{2,1,0:T(8,128)} %get-tuple-element.14.down_ref), channel_id=1, source_target_pairs={{0,3},{1,0},{2,1},{3,2},{4,7},{5,4},{6,5},{7,6},{8,11},{9,8},{10,9... | collective-permute-start | bytes 491528 | tf_op jit(solution)/shard_map/ppermute | solution.py:492
  8.2 3.7 %pack_columns.1.side_ref = f32[32,384]{1,0:T(8,128)} custom-call(f32[75,32,256]{2,1,0:T(8,128)} %tracer_hbm.1, f32[75,32,256]{2,1,0:T(8,128)} %east_hbm.1, s32[32,256]{1,0:T(8,128)} %depth_ref.5), custom_call_target="tpu_custom_call" | custom-call | tf_op jit(solution)/shard_map/pack_columns/pallas_call | solution.py:109
  11.9 0.0 collective-permute-start
  11.9 1.8 %collective-permute-start.1 = (f32[32,384]{1,0:T(8,128)}, f32[32,384]{1,0:T(8,128)S(1)}, u32[]{:S(2)}, u32[]{:S(2)}) collective-permute-start(f32[32,384]{1,0:T(8,128)} %pack_columns.1.side_ref), channel_id=1, source_target_pairs={{0,12},{4,0},{8,4},{12,8},{1,13},{5,1},{9,5},{13,9},{2,14},{6,2},{... | collective-permute-start | bytes 147464 | tf_op jit(solution)/shard_map/ppermute | solution.py:495
  13.7 2.0 %collective-permute-done.west_hbm = f32[32,384]{1,0:T(8,128)S(1)} collective-permute-done((f32[32,384]{1,0:T(8,128)}, f32[32,384]{1,0:T(8,128)S(1)}, u32[]{:S(2)}, u32[]{:S(2)}) %collective-permute-start) | collective-permute-done | bytes 49184 | tf_op jit(solution)/shard_map/ppermute | solution.py:494
  15.6 0.1 collective-permute-done.1.far_hbm
  15.7 1.6 %collective-permute-done.3.ahead_hbm = f32[2,80,256]{2,1,0:T(8,128)S(1)} collective-permute-done((f32[2,80,256]{2,1,0:T(8,128)}, f32[2,80,256]{2,1,0:T(8,128)S(1)}, u32[]{:S(2)}, u32[]{:S(2)}) %collective-permute-start.3) | collective-permute-done | bytes 163872 | tf_op jit(solution)/shard_map/ppermute | solution.py:492
  17.3 0.0 collective-permute-done.2.south_hbm
  17.3 0.6 %copy-done.1 = f32[2,80,256]{2,1,0:T(8,128)} copy-done((f32[2,80,256]{2,1,0:T(8,128)}, f32[2,80,256]{2,1,0:T(8,128)S(1)}, u32[]{:S(2)}) %copy-start.1) | copy-done | bytes 163864
  18.0 0.7 %copy-done = f32[3,80,256]{2,1,0:T(8,128)} copy-done((f32[3,80,256]{2,1,0:T(8,128)}, f32[3,80,256]{2,1,0:T(8,128)S(1)}, u32[]{:S(2)}) %copy-start) | copy-done | bytes 245784
  18.7 31.0 %step_and_bin.1 = (f32[75,32,256]{2,1,0:T(8,128)}, f32[16,128]{1,0:T(8,128)}, f32[8,16,128]{2,1,0:T(8,128)}, f32[8,16,128]{2,1,0:T(8,128)}, f32[8,16,128]{2,1,0:T(8,128)}, /*index=5*/f32[8,16,128]{2,1,0:T(8,128)}) custom-call(f32[75]{0:T(128)} %thick_ref.1, s32[32,256]{1,0:T(8,128)} %depth_ref.5, s32[32,256]{1,0:T(8,128)} %basin_ref.1, ...), custom_call_target="tpu_custom_call" | custom-call | tf_op jit(solution)/shard_map/step_and_bin/pallas_call | solution.py:405
  49.6 1.2 %collective-permute-start.7 = (f32[16,128]{1,0:T(8,128)}, f32[16,128]{1,0:T(8,128)S(1)}, u32[]{:S(2)}, u32[]{:S(2)}) collective-permute-start(f32[16,128]{1,0:T(8,128)} %get-tuple-element.20), channel_id=1, source_target_pairs={{0,1},{1,2},{2,3},{3,0},{4,5},{5,6},{6,7},{7,4},{8,9},{9,10},{10,1... | collective-permute-start | bytes 24584 | tf_op jit(solution)/shard_map/ppermute | solution.py:508
  50.8 1.7 %collective-permute-start.8 = (f32[16,128]{1,0:T(8,128)}, f32[16,128]{1,0:T(8,128)S(1)}, u32[]{:S(2)}, u32[]{:S(2)}) collective-permute-start(f32[16,128]{1,0:T(8,128)} %get-tuple-element.20), channel_id=1, source_target_pairs={{0,2},{1,3},{2,0},{3,1},{4,6},{5,7},{6,4},{7,5},{8,10},{9,11},{10,... | collective-permute-start | bytes 24584 | tf_op jit(solution)/shard_map/ppermute | solution.py:508
  52.5 1.3 %collective-permute-start.9 = (f32[16,128]{1,0:T(8,128)}, f32[16,128]{1,0:T(8,128)S(1)}, u32[]{:S(2)}, u32[]{:S(2)}) collective-permute-start(f32[16,128]{1,0:T(8,128)} %get-tuple-element.20), channel_id=1, source_target_pairs={{0,3},{1,0},{2,1},{3,2},{4,7},{5,4},{6,5},{7,6},{8,11},{9,8},{10,9... | collective-permute-start | bytes 24584 | tf_op jit(solution)/shard_map/ppermute | solution.py:508
  53.8 0.0 collective-permute-start.4
  53.8 1.5 %collective-permute-start.5 = (f32[8,16,128]{2,1,0:T(8,128)}, f32[8,16,128]{2,1,0:T(8,128)S(1)}, u32[]{:S(2)}, u32[]{:S(2)}) collective-permute-start(f32[8,16,128]{2,1,0:T(8,128)} %get-tuple-element.18), channel_id=1, source_target_pairs={{0,8},{4,12},{8,0},{12,4},{1,9},{5,13},{9,1},{13,5},{2,10},{6,14},... | collective-permute-start | bytes 196616 | tf_op jit(solution)/shard_map/ppermute | solution.py:504
  55.3 0.0 collective-permute-done.7
  55.3 1.4 %collective-permute-start.6 = (f32[8,16,128]{2,1,0:T(8,128)}, f32[8,16,128]{2,1,0:T(8,128)S(1)}, u32[]{:S(2)}, u32[]{:S(2)}) collective-permute-start(f32[8,16,128]{2,1,0:T(8,128)} %get-tuple-element.19), channel_id=1, source_target_pairs={{0,12},{4,0},{8,4},{12,8},{1,13},{5,1},{9,5},{13,9},{2,14},{6,2},{... | collective-permute-start | bytes 196616 | tf_op jit(solution)/shard_map/ppermute | solution.py:504
  56.8 0.1 collective-permute-start.10
  56.8 1.2 %collective-permute-start.11 = (f32[16,128]{1,0:T(8,128)S(1)}, f32[16,128]{1,0:T(8,128)S(1)}, u32[]{:S(2)}, u32[]{:S(2)}) collective-permute-start(f32[16,128]{1,0:T(8,128)S(1)} %select_add_fusion.refs_4_), channel_id=1, source_target_pairs={{0,8},{4,12},{8,0},{12,4},{1,9},{5,13},{9,1},{13,5},{2,10},{6,14},... | collective-permute-start | bytes 24584 | tf_op jit(solution)/shard_map/ppermute | solution.py:509
  58.0 1.9 %collective-permute-done.10.refs_5_ = f32[16,128]{1,0:T(8,128)S(1)} collective-permute-done((f32[16,128]{1,0:T(8,128)S(1)}, f32[16,128]{1,0:T(8,128)S(1)}, u32[]{:S(2)}, u32[]{:S(2)}) %collective-permute-start.10) | collective-permute-done | bytes 8224 | tf_op jit(solution)/shard_map/ppermute | solution.py:509
  59.9 0.0 collective-permute-start.12
  59.9 0.6 %collective-permute-done.11.refs_6_ = f32[16,128]{1,0:T(8,128)S(1)} collective-permute-done((f32[16,128]{1,0:T(8,128)S(1)}, f32[16,128]{1,0:T(8,128)S(1)}, u32[]{:S(2)}, u32[]{:S(2)}) %collective-permute-start.11) | collective-permute-done | bytes 8224 | tf_op jit(solution)/shard_map/ppermute | solution.py:509
  60.6 0.7 %collective-permute-done.12.refs_7_ = f32[16,128]{1,0:T(8,128)S(1)} collective-permute-done((f32[16,128]{1,0:T(8,128)S(1)}, f32[16,128]{1,0:T(8,128)S(1)}, u32[]{:S(2)}, u32[]{:S(2)}) %collective-permute-start.12) | collective-permute-done | bytes 8224 | tf_op jit(solution)/shard_map/ppermute | solution.py:509
  61.3 0.0 collective-permute-done.5.refs_2_
  61.3 0.5 copy-done.10
  61.9 0.0 copy-done.2
  61.9 0.0 copy-done.3
  61.9 0.0 copy-done.4
  62.0 2.0 %close_sums.1 = (f32[5,8,192]{2,1,0:T(8,128)}, f32[5,8,192]{2,1,0:T(8,128)}) custom-call(f32[8,16,128]{2,1,0:T(8,128)} %get-tuple-element.16.refs_0_, f32[8,16,128]{2,1,0:T(8,128)} %copy-done.2, f32[8,16,128]{2,1,0:T(8,128)} %copy-done.3, f32[8,16,128]{2,1,0:T(8,128)} %copy-done.4, f32[16,128]{1,0:T(8,128)} %copy-done.7, f32[16,128]{1,0:T(8,128)} %copy-done.8, ...), custom_call_target="tpu_custom_call" | custom-call | tf_op jit(solution)/shard_map/close_sums/pallas_call | solution.py:472
  (21 shorter events, 0.0 us)
Async XLA Ops:
  3.1 14.2 %collective-permute-start.2 = (f32[3,80,256]{2,1,0:T(8,128)}, f32[3,80,256]{2,1,0:T(8,128)S(1)}, u32[]{:S(2)}, u32[]{:S(2)}) collective-permute-start(f32[3,80,256]{2,1,0:T(8,128)} %get-tuple-element.13.up_ref), channel_id=1, source_target_pairs={{0,1},{1,2},{2,3},{3,0},{4,5},{5,6},{6,7},{7,4},{8,9},{9,10},{10,1... | collective-permute-start | bytes 737288 | tf_op jit(solution)/shard_map/ppermute | solution.py:491
  6.2 11.1 %collective-permute-start.3 = (f32[2,80,256]{2,1,0:T(8,128)}, f32[2,80,256]{2,1,0:T(8,128)S(1)}, u32[]{:S(2)}, u32[]{:S(2)}) collective-permute-start(f32[2,80,256]{2,1,0:T(8,128)} %get-tuple-element.14.down_ref), channel_id=1, source_target_pairs={{0,3},{1,0},{2,1},{3,2},{4,7},{5,4},{6,5},{7,6},{8,11},{9,8},{10,9... | collective-permute-start | bytes 491528 | tf_op jit(solution)/shard_map/ppermute | solution.py:492
  11.9 3.7 %collective-permute-start = (f32[32,384]{1,0:T(8,128)}, f32[32,384]{1,0:T(8,128)S(1)}, u32[]{:S(2)}, u32[]{:S(2)}) collective-permute-start(f32[32,384]{1,0:T(8,128)} %pack_columns.1.side_ref), channel_id=1, source_target_pairs={{0,4},{4,8},{8,12},{12,0},{1,5},{5,9},{9,13},{13,1},{2,6},{6,10},{... | collective-permute-start | bytes 147464 | tf_op jit(solution)/shard_map/ppermute | solution.py:494
  11.9 3.8 %collective-permute-start.1 = (f32[32,384]{1,0:T(8,128)}, f32[32,384]{1,0:T(8,128)S(1)}, u32[]{:S(2)}, u32[]{:S(2)}) collective-permute-start(f32[32,384]{1,0:T(8,128)} %pack_columns.1.side_ref), channel_id=1, source_target_pairs={{0,12},{4,0},{8,4},{12,8},{1,13},{5,1},{9,5},{13,9},{2,14},{6,2},{... | collective-permute-start | bytes 147464 | tf_op jit(solution)/shard_map/ppermute | solution.py:495
  15.6 1.7 %copy-start.5 = (f32[32,384]{1,0:T(8,128)}, f32[32,384]{1,0:T(8,128)S(1)}, u32[]{:S(2)}) copy-start(f32[32,384]{1,0:T(8,128)S(1)} %collective-permute-done.west_hbm) | copy-start | bytes 147460
  15.7 1.6 %copy-start.6 = (f32[32,384]{1,0:T(8,128)}, f32[32,384]{1,0:T(8,128)S(1)}, u32[]{:S(2)}) copy-start(f32[32,384]{1,0:T(8,128)S(1)} %collective-permute-done.1.far_hbm) | copy-start | bytes 147460
  17.3 0.7 %copy-start.1 = (f32[2,80,256]{2,1,0:T(8,128)}, f32[2,80,256]{2,1,0:T(8,128)S(1)}, u32[]{:S(2)}) copy-start(f32[2,80,256]{2,1,0:T(8,128)S(1)} %collective-permute-done.3.ahead_hbm) | copy-start | bytes 491524
  18.0 0.7 %copy-start = (f32[3,80,256]{2,1,0:T(8,128)}, f32[3,80,256]{2,1,0:T(8,128)S(1)}, u32[]{:S(2)}) copy-start(f32[3,80,256]{2,1,0:T(8,128)S(1)} %collective-permute-done.2.south_hbm) | copy-start | bytes 737284
  49.6 5.7 %collective-permute-start.7 = (f32[16,128]{1,0:T(8,128)}, f32[16,128]{1,0:T(8,128)S(1)}, u32[]{:S(2)}, u32[]{:S(2)}) collective-permute-start(f32[16,128]{1,0:T(8,128)} %get-tuple-element.20), channel_id=1, source_target_pairs={{0,1},{1,2},{2,3},{3,0},{4,5},{5,6},{6,7},{7,4},{8,9},{9,10},{10,1... | collective-permute-start | bytes 24584 | tf_op jit(solution)/shard_map/ppermute | solution.py:508
  50.8 5.9 %collective-permute-start.8 = (f32[16,128]{1,0:T(8,128)}, f32[16,128]{1,0:T(8,128)S(1)}, u32[]{:S(2)}, u32[]{:S(2)}) collective-permute-start(f32[16,128]{1,0:T(8,128)} %get-tuple-element.20), channel_id=1, source_target_pairs={{0,2},{1,3},{2,0},{3,1},{4,6},{5,7},{6,4},{7,5},{8,10},{9,11},{10,... | collective-permute-start | bytes 24584 | tf_op jit(solution)/shard_map/ppermute | solution.py:508
  52.5 4.3 %collective-permute-start.9 = (f32[16,128]{1,0:T(8,128)}, f32[16,128]{1,0:T(8,128)S(1)}, u32[]{:S(2)}, u32[]{:S(2)}) collective-permute-start(f32[16,128]{1,0:T(8,128)} %get-tuple-element.20), channel_id=1, source_target_pairs={{0,3},{1,0},{2,1},{3,2},{4,7},{5,4},{6,5},{7,6},{8,11},{9,8},{10,9... | collective-permute-start | bytes 24584 | tf_op jit(solution)/shard_map/ppermute | solution.py:508
  53.8 7.5 %collective-permute-start.4 = (f32[8,16,128]{2,1,0:T(8,128)}, f32[8,16,128]{2,1,0:T(8,128)S(1)}, u32[]{:S(2)}, u32[]{:S(2)}) collective-permute-start(f32[8,16,128]{2,1,0:T(8,128)} %get-tuple-element.17), channel_id=1, source_target_pairs={{0,4},{4,8},{8,12},{12,0},{1,5},{5,9},{9,13},{13,1},{2,6},{6,10},{... | collective-permute-start | bytes 196616 | tf_op jit(solution)/shard_map/ppermute | solution.py:504
  53.8 7.5 %collective-permute-start.5 = (f32[8,16,128]{2,1,0:T(8,128)}, f32[8,16,128]{2,1,0:T(8,128)S(1)}, u32[]{:S(2)}, u32[]{:S(2)}) collective-permute-start(f32[8,16,128]{2,1,0:T(8,128)} %get-tuple-element.18), channel_id=1, source_target_pairs={{0,8},{4,12},{8,0},{12,4},{1,9},{5,13},{9,1},{13,5},{2,10},{6,14},... | collective-permute-start | bytes 196616 | tf_op jit(solution)/shard_map/ppermute | solution.py:504
  55.3 6.0 %collective-permute-start.6 = (f32[8,16,128]{2,1,0:T(8,128)}, f32[8,16,128]{2,1,0:T(8,128)S(1)}, u32[]{:S(2)}, u32[]{:S(2)}) collective-permute-start(f32[8,16,128]{2,1,0:T(8,128)} %get-tuple-element.19), channel_id=1, source_target_pairs={{0,12},{4,0},{8,4},{12,8},{1,13},{5,1},{9,5},{13,9},{2,14},{6,2},{... | collective-permute-start | bytes 196616 | tf_op jit(solution)/shard_map/ppermute | solution.py:504
  56.8 4.6 %copy-start.7 = (f32[16,128]{1,0:T(8,128)}, f32[16,128]{1,0:T(8,128)S(1)}, u32[]{:S(2)}) copy-start(f32[16,128]{1,0:T(8,128)S(1)} %select_add_fusion.refs_4_) | copy-start | bytes 24580
  56.8 3.1 %collective-permute-start.10 = (f32[16,128]{1,0:T(8,128)S(1)}, f32[16,128]{1,0:T(8,128)S(1)}, u32[]{:S(2)}, u32[]{:S(2)}) collective-permute-start(f32[16,128]{1,0:T(8,128)S(1)} %select_add_fusion.refs_4_), channel_id=1, source_target_pairs={{0,4},{4,8},{8,12},{12,0},{1,5},{5,9},{9,13},{13,1},{2,6},{6,10},{... | collective-permute-start | bytes 24584 | tf_op jit(solution)/shard_map/ppermute | solution.py:509
  56.8 3.7 %collective-permute-start.11 = (f32[16,128]{1,0:T(8,128)S(1)}, f32[16,128]{1,0:T(8,128)S(1)}, u32[]{:S(2)}, u32[]{:S(2)}) collective-permute-start(f32[16,128]{1,0:T(8,128)S(1)} %select_add_fusion.refs_4_), channel_id=1, source_target_pairs={{0,8},{4,12},{8,0},{12,4},{1,9},{5,13},{9,1},{13,5},{2,10},{6,14},... | collective-permute-start | bytes 24584 | tf_op jit(solution)/shard_map/ppermute | solution.py:509
  59.9 1.4 %copy-start.8 = (f32[16,128]{1,0:T(8,128)}, f32[16,128]{1,0:T(8,128)S(1)}, u32[]{:S(2)}) copy-start(f32[16,128]{1,0:T(8,128)S(1)} %collective-permute-done.10.refs_5_) | copy-start | bytes 24580
  59.9 1.4 %collective-permute-start.12 = (f32[16,128]{1,0:T(8,128)S(1)}, f32[16,128]{1,0:T(8,128)S(1)}, u32[]{:S(2)}, u32[]{:S(2)}) collective-permute-start(f32[16,128]{1,0:T(8,128)S(1)} %select_add_fusion.refs_4_), channel_id=1, source_target_pairs={{0,12},{4,0},{8,4},{12,8},{1,13},{5,1},{9,5},{13,9},{2,14},{6,2},{... | collective-permute-start | bytes 24584 | tf_op jit(solution)/shard_map/ppermute | solution.py:509
  60.6 0.8 %copy-start.9 = (f32[16,128]{1,0:T(8,128)}, f32[16,128]{1,0:T(8,128)S(1)}, u32[]{:S(2)}) copy-start(f32[16,128]{1,0:T(8,128)S(1)} %collective-permute-done.11.refs_6_) | copy-start | bytes 24580
  61.3 0.6 copy-start.10
  61.3 0.6 copy-start.2
  61.3 0.6 %copy-start.3 = (f32[8,16,128]{2,1,0:T(8,128)}, f32[8,16,128]{2,1,0:T(8,128)S(1)}, u32[]{:S(2)}) copy-start(f32[8,16,128]{2,1,0:T(8,128)S(1)} %collective-permute-done.5.refs_2_) | copy-start | bytes 196612
  61.3 0.7 %copy-start.4 = (f32[8,16,128]{2,1,0:T(8,128)}, f32[8,16,128]{2,1,0:T(8,128)S(1)}, u32[]{:S(2)}) copy-start(f32[8,16,128]{2,1,0:T(8,128)S(1)} %collective-permute-done.6.refs_3_) | copy-start | bytes 196612

commit v4 on v3

--- a/solution.py
+++ b/solution.py
@@ -18,7 +18,7 @@
 HEADS = 16
 PER = 5
 SLOTS = 5
-VMEM = 63 << 20
+VMEM = 64 << 20
 F32 = jnp.float32
 BF16 = jnp.bfloat16
 
@@ -171,7 +171,7 @@
     edges = [pltpu.make_async_copy(src, dst, halo_sem.at[i]) for i, (src, dst) in enumerate(halos)]
     for copy in edges:
         copy.start()
-    for piece in range(pieces):
+    for piece in range(2):
         for copy in copies_in(piece):
             copy.start()
     for copy in edges:
@@ -362,6 +362,11 @@
     copy_out(0).start()
 
     def pair(i, carry):
+        @pl.when(i < pieces - 2)
+        def _():
+            for copy in copies_in(i + 2):
+                copy.start()
+
         for copy in copies_in(i + 1):
             copy.wait()
         for j in range(size // per):

time: 65 us -> 61.6 us (0.948)
  Pallas kernels: 39.2 us -> 37 us
  local copies, waits for them, and re-layouts: 1.99 us -> 0.58 us
    pallas_call x1, Pallas kernels: 31 us -> 28.8 us  [step_and_bin(): pl.pallas_call(main_kernel, in_specs=[pl.BlockSpec(memory_space=pltpu.SME...]
    unnamed x22 -> x8, local copies, waits for them, and re-layouts: 1.99 us -> 0.58 us
  transfers between devices with their start and end apart: 13 -> 13, of which waited for: 6 -> 5; matrix products, arithmetic and copies ran while one was open for 0% -> 0% of each run, Pallas kernels for 6% -> 6%
where the time goes in v4:
time: 61.6 us; the launch traced here: 60.6 us
  Pallas kernels  37 us (60%)
  starting transfers between devices  15.2 us (25%)
  waiting for transfers between devices  7.09 us (12%)
  between operations  0.69 us (1%)
    pallas_call x1, Pallas kernels, step_and_bin(): pl.pallas_call(main_kernel, in_specs=[pl.BlockSpec(memory_space=pltpu.SME...  28.8 us
    ppermute x3, starting transfers between devices, body(): lax.ppermute(block_total, 'lat', turn(lats, d))  4.27 us
    pallas_call x1, Pallas kernels, pack_columns(): pl.pallas_call(columns_kernel, grid=(tiles,), in_specs=[pl.BlockSpec((per...  3.71 us
    ppermute x3, waiting for transfers between devices, body(): lax.ppermute(carry, 'lon', turn(lons, d))  3.33 us
    ppermute x1, starting transfers between devices, body(): south = lax.ppermute(up, 'lat', turn(lats, 1))  3.02 us
    ppermute x3, starting transfers between devices, body(): lax.ppermute(pieces[d], 'lon', turn(lons, d))  2.96 us
    pallas_call x1, Pallas kernels, pack_rows(): pl.pallas_call(rows_kernel, grid=(1,), in_specs=[pl.BlockSpec((levels, 8,...  2.53 us
    ppermute x1, waiting for transfers between devices, body(): west = lax.ppermute(side, 'lon', turn(lons, 1))  2.07 us
  transfers between devices with their start and end apart: 13, of which 5 were waited for; matrix products, arithmetic and copies ran while one was open for 0% of the time, Pallas kernels for 6%

profile of v4, /device:TPU:0, one launch (start us, length us, event | category | flops | bytes accessed | tf_op | source)
XLA Modules:
  0.0 60.6 jit_solution(2063956090449036370)
XLA Ops:
  0.6 2.5 %pack_rows.1 = (f32[3,80,256]{2,1,0:T(8,128)}, f32[2,80,256]{2,1,0:T(8,128)}) custom-call(f32[75,32,256]{2,1,0:T(8,128)} %tracer_hbm.1, f32[75,32,256]{2,1,0:T(8,128)} %tracer_hbm.1, f32[75,32,256]{2,1,0:T(8,128)} %north_hbm.1, s32[32,256]{1,0:T(8,128)} %depth_ref.5), custom_call_target="tpu_custom_call" | custom-call | tf_op jit(solution)/shard_map/pack_rows/pallas_call | solution.py:67
  3.2 3.0 %collective-permute-start.2 = (f32[3,80,256]{2,1,0:T(8,128)}, f32[3,80,256]{2,1,0:T(8,128)}, u32[]{:S(2)}, u32[]{:S(2)}) collective-permute-start(f32[3,80,256]{2,1,0:T(8,128)} %get-tuple-element.13.up_ref), channel_id=1, source_target_pairs={{0,1},{1,2},{2,3},{3,0},{4,5},{5,6},{6,7},{7,4},{8,9},{9,10},{10,1... | collective-permute-start | bytes 737288 | tf_op jit(solution)/shard_map/ppermute | solution.py:496
  6.2 2.0 %collective-permute-start.3 = (f32[2,80,256]{2,1,0:T(8,128)}, f32[2,80,256]{2,1,0:T(8,128)}, u32[]{:S(2)}, u32[]{:S(2)}) collective-permute-start(f32[2,80,256]{2,1,0:T(8,128)} %get-tuple-element.14.down_ref), channel_id=1, source_target_pairs={{0,3},{1,0},{2,1},{3,2},{4,7},{5,4},{6,5},{7,6},{8,11},{9,8},{10,9... | collective-permute-start | bytes 491528 | tf_op jit(solution)/shard_map/ppermute | solution.py:497
  8.2 3.7 %pack_columns.1.side_ref = f32[32,384]{1,0:T(8,128)} custom-call(f32[75,32,256]{2,1,0:T(8,128)} %tracer_hbm.1, f32[75,32,256]{2,1,0:T(8,128)} %east_hbm.1, s32[32,256]{1,0:T(8,128)} %depth_ref.5), custom_call_target="tpu_custom_call" | custom-call | tf_op jit(solution)/shard_map/pack_columns/pallas_call | solution.py:109
  11.9 0.0 collective-permute-start
  11.9 1.8 %collective-permute-start.1 = (f32[32,384]{1,0:T(8,128)}, f32[32,384]{1,0:T(8,128)}, u32[]{:S(2)}, u32[]{:S(2)}) collective-permute-start(f32[32,384]{1,0:T(8,128)} %pack_columns.1.side_ref), channel_id=1, source_target_pairs={{0,12},{4,0},{8,4},{12,8},{1,13},{5,1},{9,5},{13,9},{2,14},{6,2},{... | collective-permute-start | bytes 147464 | tf_op jit(solution)/shard_map/ppermute | solution.py:500
  13.7 2.1 %collective-permute-done.west_hbm = f32[32,384]{1,0:T(8,128)} collective-permute-done((f32[32,384]{1,0:T(8,128)}, f32[32,384]{1,0:T(8,128)}, u32[]{:S(2)}, u32[]{:S(2)}) %collective-permute-start) | collective-permute-done | bytes 49184 | tf_op jit(solution)/shard_map/ppermute | solution.py:499
  15.8 0.0 collective-permute-done.1.far_hbm
  15.8 1.7 %collective-permute-done.3.ahead_hbm = f32[2,80,256]{2,1,0:T(8,128)} collective-permute-done((f32[2,80,256]{2,1,0:T(8,128)}, f32[2,80,256]{2,1,0:T(8,128)}, u32[]{:S(2)}, u32[]{:S(2)}) %collective-permute-start.3) | collective-permute-done | bytes 163872 | tf_op jit(solution)/shard_map/ppermute | solution.py:497
  17.4 0.0 collective-permute-done.2.south_hbm
  17.4 28.8 %step_and_bin.1 = (f32[75,32,256]{2,1,0:T(8,128)}, f32[16,128]{1,0:T(8,128)}, f32[8,16,128]{2,1,0:T(8,128)}, f32[8,16,128]{2,1,0:T(8,128)}, f32[8,16,128]{2,1,0:T(8,128)}, /*index=5*/f32[8,16,128]{2,1,0:T(8,128)}) custom-call(f32[75]{0:T(128)} %thick_ref.1, s32[32,256]{1,0:T(8,128)} %depth_ref.5, s32[32,256]{1,0:T(8,128)} %basin_ref.1, ...), custom_call_target="tpu_custom_call" | custom-call | tf_op jit(solution)/shard_map/step_and_bin/pallas_call | solution.py:410
  46.2 1.2 %collective-permute-start.7 = (f32[16,128]{1,0:T(8,128)}, f32[16,128]{1,0:T(8,128)S(1)}, u32[]{:S(2)}, u32[]{:S(2)}) collective-permute-start(f32[16,128]{1,0:T(8,128)} %get-tuple-element.20), channel_id=1, source_target_pairs={{0,1},{1,2},{2,3},{3,0},{4,5},{5,6},{6,7},{7,4},{8,9},{9,10},{10,1... | collective-permute-start | bytes 24584 | tf_op jit(solution)/shard_map/ppermute | solution.py:513
  47.4 1.7 %collective-permute-start.8 = (f32[16,128]{1,0:T(8,128)}, f32[16,128]{1,0:T(8,128)S(1)}, u32[]{:S(2)}, u32[]{:S(2)}) collective-permute-start(f32[16,128]{1,0:T(8,128)} %get-tuple-element.20), channel_id=1, source_target_pairs={{0,2},{1,3},{2,0},{3,1},{4,6},{5,7},{6,4},{7,5},{8,10},{9,11},{10,... | collective-permute-start | bytes 24584 | tf_op jit(solution)/shard_map/ppermute | solution.py:513
  49.1 1.4 %collective-permute-start.9 = (f32[16,128]{1,0:T(8,128)}, f32[16,128]{1,0:T(8,128)S(1)}, u32[]{:S(2)}, u32[]{:S(2)}) collective-permute-start(f32[16,128]{1,0:T(8,128)} %get-tuple-element.20), channel_id=1, source_target_pairs={{0,3},{1,0},{2,1},{3,2},{4,7},{5,4},{6,5},{7,6},{8,11},{9,8},{10,9... | collective-permute-start | bytes 24584 | tf_op jit(solution)/shard_map/ppermute | solution.py:513
  50.5 0.0 collective-permute-start.4
  50.5 1.5 %collective-permute-start.5 = (f32[8,16,128]{2,1,0:T(8,128)}, f32[8,16,128]{2,1,0:T(8,128)}, u32[]{:S(2)}, u32[]{:S(2)}) collective-permute-start(f32[8,16,128]{2,1,0:T(8,128)} %get-tuple-element.18), channel_id=1, source_target_pairs={{0,8},{4,12},{8,0},{12,4},{1,9},{5,13},{9,1},{13,5},{2,10},{6,14},... | collective-permute-start | bytes 196616 | tf_op jit(solution)/shard_map/ppermute | solution.py:509
  52.0 0.0 collective-permute-done.7
  52.0 1.4 %collective-permute-start.6 = (f32[8,16,128]{2,1,0:T(8,128)}, f32[8,16,128]{2,1,0:T(8,128)}, u32[]{:S(2)}, u32[]{:S(2)}) collective-permute-start(f32[8,16,128]{2,1,0:T(8,128)} %get-tuple-element.19), channel_id=1, source_target_pairs={{0,12},{4,0},{8,4},{12,8},{1,13},{5,1},{9,5},{13,9},{2,14},{6,2},{... | collective-permute-start | bytes 196616 | tf_op jit(solution)/shard_map/ppermute | solution.py:509
  53.4 0.0 collective-permute-done.8
  53.4 0.0 collective-permute-done.9
  53.5 0.0 copy-start
  53.5 0.1 collective-permute-start.10
  53.5 1.1 %collective-permute-start.11 = (f32[16,128]{1,0:T(8,128)S(1)}, f32[16,128]{1,0:T(8,128)S(1)}, u32[]{:S(2)}, u32[]{:S(2)}) collective-permute-start(f32[16,128]{1,0:T(8,128)S(1)} %select_add_fusion.refs_4_), channel_id=1, source_target_pairs={{0,8},{4,12},{8,0},{12,4},{1,9},{5,13},{9,1},{13,5},{2,10},{6,14},... | collective-permute-start | bytes 24584 | tf_op jit(solution)/shard_map/ppermute | solution.py:514
  54.6 2.0 %collective-permute-done.10.refs_5_ = f32[16,128]{1,0:T(8,128)S(1)} collective-permute-done((f32[16,128]{1,0:T(8,128)S(1)}, f32[16,128]{1,0:T(8,128)S(1)}, u32[]{:S(2)}, u32[]{:S(2)}) %collective-permute-start.10) | collective-permute-done | bytes 8224 | tf_op jit(solution)/shard_map/ppermute | solution.py:514
  56.6 0.0 collective-permute-start.12
  56.6 0.6 %collective-permute-done.11.refs_6_ = f32[16,128]{1,0:T(8,128)S(1)} collective-permute-done((f32[16,128]{1,0:T(8,128)S(1)}, f32[16,128]{1,0:T(8,128)S(1)}, u32[]{:S(2)}, u32[]{:S(2)}) %collective-permute-start.11) | collective-permute-done | bytes 8224 | tf_op jit(solution)/shard_map/ppermute | solution.py:514
  57.3 0.7 %collective-permute-done.12.refs_7_ = f32[16,128]{1,0:T(8,128)S(1)} collective-permute-done((f32[16,128]{1,0:T(8,128)S(1)}, f32[16,128]{1,0:T(8,128)S(1)}, u32[]{:S(2)}, u32[]{:S(2)}) %collective-permute-start.12) | collective-permute-done | bytes 8224 | tf_op jit(solution)/shard_map/ppermute | solution.py:514
  58.0 0.0 collective-permute-done.4.refs_1_
  58.0 0.0 collective-permute-done.5.refs_2_
  58.0 0.6 copy-done.3
  58.6 0.0 collective-permute-done.6.refs_3_
  58.6 2.0 %close_sums.1 = (f32[5,8,192]{2,1,0:T(8,128)}, f32[5,8,192]{2,1,0:T(8,128)}) custom-call(f32[8,16,128]{2,1,0:T(8,128)} %get-tuple-element.16.refs_0_, f32[8,16,128]{2,1,0:T(8,128)} %collective-permute-done.4.refs_1_, f32[8,16,128]{2,1,0:T(8,128)} %collective-permute-done.5.refs_2_, f32[8,16,128]{2,1,0:T(8,128)} %collective-permute-done.6.refs_3_, ...), custom_call_target="tpu_custom_call" | custom-call | tf_op jit(solution)/shard_map/close_sums/pallas_call | solution.py:477
  (7 shorter events, 0.0 us)
Async XLA Ops:
  3.2 14.3 %collective-permute-start.2 = (f32[3,80,256]{2,1,0:T(8,128)}, f32[3,80,256]{2,1,0:T(8,128)}, u32[]{:S(2)}, u32[]{:S(2)}) collective-permute-start(f32[3,80,256]{2,1,0:T(8,128)} %get-tuple-element.13.up_ref), channel_id=1, source_target_pairs={{0,1},{1,2},{2,3},{3,0},{4,5},{5,6},{6,7},{7,4},{8,9},{9,10},{10,1... | collective-permute-start | bytes 737288 | tf_op jit(solution)/shard_map/ppermute | solution.py:496
  6.2 11.2 %collective-permute-start.3 = (f32[2,80,256]{2,1,0:T(8,128)}, f32[2,80,256]{2,1,0:T(8,128)}, u32[]{:S(2)}, u32[]{:S(2)}) collective-permute-start(f32[2,80,256]{2,1,0:T(8,128)} %get-tuple-element.14.down_ref), channel_id=1, source_target_pairs={{0,3},{1,0},{2,1},{3,2},{4,7},{5,4},{6,5},{7,6},{8,11},{9,8},{10,9... | collective-permute-start | bytes 491528 | tf_op jit(solution)/shard_map/ppermute | solution.py:497
  11.9 3.8 %collective-permute-start = (f32[32,384]{1,0:T(8,128)}, f32[32,384]{1,0:T(8,128)}, u32[]{:S(2)}, u32[]{:S(2)}) collective-permute-start(f32[32,384]{1,0:T(8,128)} %pack_columns.1.side_ref), channel_id=1, source_target_pairs={{0,4},{4,8},{8,12},{12,0},{1,5},{5,9},{9,13},{13,1},{2,6},{6,10},{... | collective-permute-start | bytes 147464 | tf_op jit(solution)/shard_map/ppermute | solution.py:499
  11.9 3.8 %collective-permute-start.1 = (f32[32,384]{1,0:T(8,128)}, f32[32,384]{1,0:T(8,128)}, u32[]{:S(2)}, u32[]{:S(2)}) collective-permute-start(f32[32,384]{1,0:T(8,128)} %pack_columns.1.side_ref), channel_id=1, source_target_pairs={{0,12},{4,0},{8,4},{12,8},{1,13},{5,1},{9,5},{13,9},{2,14},{6,2},{... | collective-permute-start | bytes 147464 | tf_op jit(solution)/shard_map/ppermute | solution.py:500
  46.2 5.8 %collective-permute-start.7 = (f32[16,128]{1,0:T(8,128)}, f32[16,128]{1,0:T(8,128)S(1)}, u32[]{:S(2)}, u32[]{:S(2)}) collective-permute-start(f32[16,128]{1,0:T(8,128)} %get-tuple-element.20), channel_id=1, source_target_pairs={{0,1},{1,2},{2,3},{3,0},{4,5},{5,6},{6,7},{7,4},{8,9},{9,10},{10,1... | collective-permute-start | bytes 24584 | tf_op jit(solution)/shard_map/ppermute | solution.py:513
  47.4 6.1 %collective-permute-start.8 = (f32[16,128]{1,0:T(8,128)}, f32[16,128]{1,0:T(8,128)S(1)}, u32[]{:S(2)}, u32[]{:S(2)}) collective-permute-start(f32[16,128]{1,0:T(8,128)} %get-tuple-element.20), channel_id=1, source_target_pairs={{0,2},{1,3},{2,0},{3,1},{4,6},{5,7},{6,4},{7,5},{8,10},{9,11},{10,... | collective-permute-start | bytes 24584 | tf_op jit(solution)/shard_map/ppermute | solution.py:513
  49.1 4.3 %collective-permute-start.9 = (f32[16,128]{1,0:T(8,128)}, f32[16,128]{1,0:T(8,128)S(1)}, u32[]{:S(2)}, u32[]{:S(2)}) collective-permute-start(f32[16,128]{1,0:T(8,128)} %get-tuple-element.20), channel_id=1, source_target_pairs={{0,3},{1,0},{2,1},{3,2},{4,7},{5,4},{6,5},{7,6},{8,11},{9,8},{10,9... | collective-permute-start | bytes 24584 | tf_op jit(solution)/shard_map/ppermute | solution.py:513
  50.5 7.5 %collective-permute-start.4 = (f32[8,16,128]{2,1,0:T(8,128)}, f32[8,16,128]{2,1,0:T(8,128)}, u32[]{:S(2)}, u32[]{:S(2)}) collective-permute-start(f32[8,16,128]{2,1,0:T(8,128)} %get-tuple-element.17), channel_id=1, source_target_pairs={{0,4},{4,8},{8,12},{12,0},{1,5},{5,9},{9,13},{13,1},{2,6},{6,10},{... | collective-permute-start | bytes 196616 | tf_op jit(solution)/shard_map/ppermute | solution.py:509
  50.5 7.5 %collective-permute-start.5 = (f32[8,16,128]{2,1,0:T(8,128)}, f32[8,16,128]{2,1,0:T(8,128)}, u32[]{:S(2)}, u32[]{:S(2)}) collective-permute-start(f32[8,16,128]{2,1,0:T(8,128)} %get-tuple-element.18), channel_id=1, source_target_pairs={{0,8},{4,12},{8,0},{12,4},{1,9},{5,13},{9,1},{13,5},{2,10},{6,14},... | collective-permute-start | bytes 196616 | tf_op jit(solution)/shard_map/ppermute | solution.py:509
  52.0 6.6 %collective-permute-start.6 = (f32[8,16,128]{2,1,0:T(8,128)}, f32[8,16,128]{2,1,0:T(8,128)}, u32[]{:S(2)}, u32[]{:S(2)}) collective-permute-start(f32[8,16,128]{2,1,0:T(8,128)} %get-tuple-element.19), channel_id=1, source_target_pairs={{0,12},{4,0},{8,4},{12,8},{1,13},{5,1},{9,5},{13,9},{2,14},{6,2},{... | collective-permute-start | bytes 196616 | tf_op jit(solution)/shard_map/ppermute | solution.py:509
  53.5 3.1 %copy-start = (f32[16,128]{1,0:T(8,128)}, f32[16,128]{1,0:T(8,128)S(1)}, u32[]{:S(2)}) copy-start(f32[16,128]{1,0:T(8,128)S(1)} %select_add_fusion.refs_4_) | copy-start | bytes 24580
  53.5 3.1 %collective-permute-start.10 = (f32[16,128]{1,0:T(8,128)S(1)}, f32[16,128]{1,0:T(8,128)S(1)}, u32[]{:S(2)}, u32[]{:S(2)}) collective-permute-start(f32[16,128]{1,0:T(8,128)S(1)} %select_add_fusion.refs_4_), channel_id=1, source_target_pairs={{0,4},{4,8},{8,12},{12,0},{1,5},{5,9},{9,13},{13,1},{2,6},{6,10},{... | collective-permute-start | bytes 24584 | tf_op jit(solution)/shard_map/ppermute | solution.py:514
  53.5 3.7 %collective-permute-start.11 = (f32[16,128]{1,0:T(8,128)S(1)}, f32[16,128]{1,0:T(8,128)S(1)}, u32[]{:S(2)}, u32[]{:S(2)}) collective-permute-start(f32[16,128]{1,0:T(8,128)S(1)} %select_add_fusion.refs_4_), channel_id=1, source_target_pairs={{0,8},{4,12},{8,0},{12,4},{1,9},{5,13},{9,1},{13,5},{2,10},{6,14},... | collective-permute-start | bytes 24584 | tf_op jit(solution)/shard_map/ppermute | solution.py:514
  56.6 1.4 %copy-start.1 = (f32[16,128]{1,0:T(8,128)}, f32[16,128]{1,0:T(8,128)S(1)}, u32[]{:S(2)}) copy-start(f32[16,128]{1,0:T(8,128)S(1)} %collective-permute-done.10.refs_5_) | copy-start | bytes 24580
  56.6 1.4 %collective-permute-start.12 = (f32[16,128]{1,0:T(8,128)S(1)}, f32[16,128]{1,0:T(8,128)S(1)}, u32[]{:S(2)}, u32[]{:S(2)}) collective-permute-start(f32[16,128]{1,0:T(8,128)S(1)} %select_add_fusion.refs_4_), channel_id=1, source_target_pairs={{0,12},{4,0},{8,4},{12,8},{1,13},{5,1},{9,5},{13,9},{2,14},{6,2},{... | collective-permute-start | bytes 24584 | tf_op jit(solution)/shard_map/ppermute | solution.py:514
  57.3 0.7 %copy-start.2 = (f32[16,128]{1,0:T(8,128)}, f32[16,128]{1,0:T(8,128)S(1)}, u32[]{:S(2)}) copy-start(f32[16,128]{1,0:T(8,128)S(1)} %collective-permute-done.11.refs_6_) | copy-start | bytes 24580
  58.0 0.6 copy-start.3

commit v5 on v4

--- a/solution.py
+++ b/solution.py
@@ -511,7 +511,15 @@
     carry = jnp.zeros((HEADS, 2 * LOW), F32)
     for d in range(1, lats):
         carry = carry + jnp.where(lat >= d, lax.ppermute(block_total, "lat", turn(lats, d)), 0.0)
-    carries = [carry] + [lax.ppermute(carry, "lon", turn(lons, d)) for d in range(1, lons)]
+    carries = [carry]
+    if lons & (lons - 1) == 0:
+        bit = 1
+        while bit < lons:
+            carry = sum(carries)
+            carries = [carry, lax.ppermute(carry, "lon", [(i, i ^ bit) for i in range(lons)])]
+            bit *= 2
+    else:
+        carries += [lax.ppermute(carry, "lon", turn(lons, d)) for d in range(1, lons)]
     unit = 1.0 / math.sqrt(cols * lons * levels)
     overturning, tendency = close(pieces, carries, (16.0 * unit, 4.0 * unit))
     return (tracer_next, overturning, tendency)

time: 61.6 us -> 61.8 us (level); the launches traced: 60.6 us -> 61.5 us
    ppermute x3 -> x2, waiting for transfers between devices: 3.33 us -> 3.84 us  [body(): lax.ppermute(carry, 'lon', [(i, i ^ bit) for i in range(lons)])]
  transfers between devices with their start and end apart: 13 -> 12, of which waited for: 5 -> 4; matrix products, arithmetic and copies ran while one was open for 0% -> 0% of each run, Pallas kernels for 6% -> 6%
where the time goes in v5:
time: 61.8 us; the launch traced here: 61.5 us
  Pallas kernels  37 us (60%)
  starting transfers between devices  15.1 us (24%)
  waiting for transfers between devices  7.6 us (12%)
  local copies, waits for them, and re-layouts  1.18 us (2%)
  between operations  0.67 us (1%)
    pallas_call x1, Pallas kernels, step_and_bin(): pl.pallas_call(main_kernel, in_specs=[pl.BlockSpec(memory_space=pltpu.SME...  28.8 us
    ppermute x3, starting transfers between devices, body(): lax.ppermute(block_total, 'lat', turn(lats, d))  4.26 us
    ppermute x2, waiting for transfers between devices, body(): lax.ppermute(carry, 'lon', [(i, i ^ bit) for i in range(lons)])  3.84 us
    pallas_call x1, Pallas kernels, pack_columns(): pl.pallas_call(columns_kernel, grid=(tiles,), in_specs=[pl.BlockSpec((per...  3.71 us
    ppermute x1, starting transfers between devices, body(): south = lax.ppermute(up, 'lat', turn(lats, 1))  3.02 us
    ppermute x3, starting transfers between devices, body(): lax.ppermute(pieces[d], 'lon', turn(lons, d))  2.96 us
    pallas_call x1, Pallas kernels, pack_rows(): pl.pallas_call(rows_kernel, grid=(1,), in_specs=[pl.BlockSpec((levels, 8,...  2.5 us
    ppermute x1, waiting for transfers between devices, body(): west = lax.ppermute(side, 'lon', turn(lons, 1))  2.07 us
  transfers between devices with their start and end apart: 12, of which 4 were waited for; matrix products, arithmetic and copies ran while one was open for 0% of the time, Pallas kernels for 6%

profile of v5, /device:TPU:0, one launch (start us, length us, event | category | flops | bytes accessed | tf_op | source)
XLA Modules:
  0.0 61.5 jit_solution(9640938754583090287)
XLA Ops:
  0.6 2.5 %pack_rows.1 = (f32[3,80,256]{2,1,0:T(8,128)}, f32[2,80,256]{2,1,0:T(8,128)}) custom-call(f32[75,32,256]{2,1,0:T(8,128)} %tracer_hbm.1, f32[75,32,256]{2,1,0:T(8,128)} %tracer_hbm.1, f32[75,32,256]{2,1,0:T(8,128)} %north_hbm.1, s32[32,256]{1,0:T(8,128)} %depth_ref.5), custom_call_target="tpu_custom_call" | custom-call | tf_op jit(solution)/shard_map/pack_rows/pallas_call | solution.py:67
  3.1 3.0 %collective-permute-start.2 = (f32[3,80,256]{2,1,0:T(8,128)}, f32[3,80,256]{2,1,0:T(8,128)}, u32[]{:S(2)}, u32[]{:S(2)}) collective-permute-start(f32[3,80,256]{2,1,0:T(8,128)} %get-tuple-element.13.up_ref), channel_id=1, source_target_pairs={{0,1},{1,2},{2,3},{3,0},{4,5},{5,6},{6,7},{7,4},{8,9},{9,10},{10,1... | collective-permute-start | bytes 737288 | tf_op jit(solution)/shard_map/ppermute | solution.py:496
  6.2 2.0 %collective-permute-start.3 = (f32[2,80,256]{2,1,0:T(8,128)}, f32[2,80,256]{2,1,0:T(8,128)}, u32[]{:S(2)}, u32[]{:S(2)}) collective-permute-start(f32[2,80,256]{2,1,0:T(8,128)} %get-tuple-element.14.down_ref), channel_id=1, source_target_pairs={{0,3},{1,0},{2,1},{3,2},{4,7},{5,4},{6,5},{7,6},{8,11},{9,8},{10,9... | collective-permute-start | bytes 491528 | tf_op jit(solution)/shard_map/ppermute | solution.py:497
  8.2 3.7 %pack_columns.1.side_ref = f32[32,384]{1,0:T(8,128)} custom-call(f32[75,32,256]{2,1,0:T(8,128)} %tracer_hbm.1, f32[75,32,256]{2,1,0:T(8,128)} %east_hbm.1, s32[32,256]{1,0:T(8,128)} %depth_ref.5), custom_call_target="tpu_custom_call" | custom-call | tf_op jit(solution)/shard_map/pack_columns/pallas_call | solution.py:109
  11.9 0.0 collective-permute-start
  11.9 1.8 %collective-permute-start.1 = (f32[32,384]{1,0:T(8,128)}, f32[32,384]{1,0:T(8,128)}, u32[]{:S(2)}, u32[]{:S(2)}) collective-permute-start(f32[32,384]{1,0:T(8,128)} %pack_columns.1.side_ref), channel_id=1, source_target_pairs={{0,12},{4,0},{8,4},{12,8},{1,13},{5,1},{9,5},{13,9},{2,14},{6,2},{... | collective-permute-start | bytes 147464 | tf_op jit(solution)/shard_map/ppermute | solution.py:500
  13.7 2.1 %collective-permute-done.west_hbm = f32[32,384]{1,0:T(8,128)} collective-permute-done((f32[32,384]{1,0:T(8,128)}, f32[32,384]{1,0:T(8,128)}, u32[]{:S(2)}, u32[]{:S(2)}) %collective-permute-start) | collective-permute-done | bytes 49184 | tf_op jit(solution)/shard_map/ppermute | solution.py:499
  15.7 0.0 collective-permute-done.1.far_hbm
  15.7 1.7 %collective-permute-done.3.ahead_hbm = f32[2,80,256]{2,1,0:T(8,128)} collective-permute-done((f32[2,80,256]{2,1,0:T(8,128)}, f32[2,80,256]{2,1,0:T(8,128)}, u32[]{:S(2)}, u32[]{:S(2)}) %collective-permute-start.3) | collective-permute-done | bytes 163872 | tf_op jit(solution)/shard_map/ppermute | solution.py:497
  17.4 0.0 collective-permute-done.2.south_hbm
  17.4 28.8 %step_and_bin.1 = (f32[75,32,256]{2,1,0:T(8,128)}, f32[16,128]{1,0:T(8,128)}, f32[8,16,128]{2,1,0:T(8,128)}, f32[8,16,128]{2,1,0:T(8,128)}, f32[8,16,128]{2,1,0:T(8,128)}, /*index=5*/f32[8,16,128]{2,1,0:T(8,128)}) custom-call(f32[75]{0:T(128)} %thick_ref.1, s32[32,256]{1,0:T(8,128)} %depth_ref.5, s32[32,256]{1,0:T(8,128)} %basin_ref.1, ...), custom_call_target="tpu_custom_call" | custom-call | tf_op jit(solution)/shard_map/step_and_bin/pallas_call | solution.py:410
  46.2 1.2 %collective-permute-start.7 = (f32[16,128]{1,0:T(8,128)}, f32[16,128]{1,0:T(8,128)S(1)}, u32[]{:S(2)}, u32[]{:S(2)}) collective-permute-start(f32[16,128]{1,0:T(8,128)} %get-tuple-element.20), channel_id=1, source_target_pairs={{0,1},{1,2},{2,3},{3,0},{4,5},{5,6},{6,7},{7,4},{8,9},{9,10},{10,1... | collective-permute-start | bytes 24584 | tf_op jit(solution)/shard_map/ppermute | solution.py:513
  47.4 1.7 %collective-permute-start.8 = (f32[16,128]{1,0:T(8,128)}, f32[16,128]{1,0:T(8,128)S(1)}, u32[]{:S(2)}, u32[]{:S(2)}) collective-permute-start(f32[16,128]{1,0:T(8,128)} %get-tuple-element.20), channel_id=1, source_target_pairs={{0,2},{1,3},{2,0},{3,1},{4,6},{5,7},{6,4},{7,5},{8,10},{9,11},{10,... | collective-permute-start | bytes 24584 | tf_op jit(solution)/shard_map/ppermute | solution.py:513
  49.1 1.3 %collective-permute-start.9 = (f32[16,128]{1,0:T(8,128)}, f32[16,128]{1,0:T(8,128)S(1)}, u32[]{:S(2)}, u32[]{:S(2)}) collective-permute-start(f32[16,128]{1,0:T(8,128)} %get-tuple-element.20), channel_id=1, source_target_pairs={{0,3},{1,0},{2,1},{3,2},{4,7},{5,4},{6,5},{7,6},{8,11},{9,8},{10,9... | collective-permute-start | bytes 24584 | tf_op jit(solution)/shard_map/ppermute | solution.py:513
  50.4 0.0 collective-permute-start.4
  50.4 1.5 %collective-permute-start.5 = (f32[8,16,128]{2,1,0:T(8,128)}, f32[8,16,128]{2,1,0:T(8,128)}, u32[]{:S(2)}, u32[]{:S(2)}) collective-permute-start(f32[8,16,128]{2,1,0:T(8,128)} %get-tuple-element.18), channel_id=1, source_target_pairs={{0,8},{4,12},{8,0},{12,4},{1,9},{5,13},{9,1},{13,5},{2,10},{6,14},... | collective-permute-start | bytes 196616 | tf_op jit(solution)/shard_map/ppermute | solution.py:509
  52.0 0.0 collective-permute-done.7
  52.0 1.4 %collective-permute-start.6 = (f32[8,16,128]{2,1,0:T(8,128)}, f32[8,16,128]{2,1,0:T(8,128)}, u32[]{:S(2)}, u32[]{:S(2)}) collective-permute-start(f32[8,16,128]{2,1,0:T(8,128)} %get-tuple-element.19), channel_id=1, source_target_pairs={{0,12},{4,0},{8,4},{12,8},{1,13},{5,1},{9,5},{13,9},{2,14},{6,2},{... | collective-permute-start | bytes 196616 | tf_op jit(solution)/shard_map/ppermute | solution.py:509
  53.4 0.0 collective-permute-done.8
  53.4 0.0 collective-permute-done.9
  53.4 0.1 collective-permute-start.10
  53.5 1.2 %collective-permute-done.10 = f32[16,128]{1,0:T(8,128)S(1)} collective-permute-done((f32[16,128]{1,0:T(8,128)S(1)}, f32[16,128]{1,0:T(8,128)S(1)}, u32[]{:S(2)}, u32[]{:S(2)}) %collective-permute-start.10) | collective-permute-done | bytes 8224 | tf_op jit(solution)/shard_map/ppermute | solution.py:519
  54.7 0.0 copy-start
  54.7 0.6 copy-done
  55.3 1.0 %collective-permute-start.11 = (f32[16,128]{1,0:T(8,128)S(1)}, f32[16,128]{1,0:T(8,128)S(1)}, u32[]{:S(2)}, u32[]{:S(2)}) collective-permute-start(f32[16,128]{1,0:T(8,128)S(1)} %add.11.refs_4_), channel_id=1, source_target_pairs={{0,8},{4,12},{8,0},{12,4},{1,9},{5,13},{9,1},{13,5},{2,10},{6,14},... | collective-permute-start | bytes 24584 | tf_op jit(solution)/shard_map/ppermute | solution.py:519
  56.2 2.7 %collective-permute-done.11.refs_5_ = f32[16,128]{1,0:T(8,128)S(1)} collective-permute-done((f32[16,128]{1,0:T(8,128)S(1)}, f32[16,128]{1,0:T(8,128)S(1)}, u32[]{:S(2)}, u32[]{:S(2)}) %collective-permute-start.11) | collective-permute-done | bytes 8224 | tf_op jit(solution)/shard_map/ppermute | solution.py:519
  58.9 0.0 copy-start.1
  58.9 0.6 copy-done.1
  59.5 0.0 collective-permute-done.4.refs_1_
  59.5 0.0 collective-permute-done.5.refs_2_
  59.5 0.0 collective-permute-done.6.refs_3_
  59.5 2.0 %close_sums.1 = (f32[5,8,192]{2,1,0:T(8,128)}, f32[5,8,192]{2,1,0:T(8,128)}) custom-call(f32[8,16,128]{2,1,0:T(8,128)} %get-tuple-element.16.refs_0_, f32[8,16,128]{2,1,0:T(8,128)} %collective-permute-done.4.refs_1_, f32[8,16,128]{2,1,0:T(8,128)} %collective-permute-done.5.refs_2_, f32[8,16,128]{2,1,0:T(8,128)} %collective-permute-done.6.refs_3_, ...), custom_call_target="tpu_custom_call" | custom-call | tf_op jit(solution)/shard_map/close_sums/pallas_call | solution.py:477
  (2 shorter events, 0.0 us)
Async XLA Ops:
  3.1 14.3 %collective-permute-start.2 = (f32[3,80,256]{2,1,0:T(8,128)}, f32[3,80,256]{2,1,0:T(8,128)}, u32[]{:S(2)}, u32[]{:S(2)}) collective-permute-start(f32[3,80,256]{2,1,0:T(8,128)} %get-tuple-element.13.up_ref), channel_id=1, source_target_pairs={{0,1},{1,2},{2,3},{3,0},{4,5},{5,6},{6,7},{7,4},{8,9},{9,10},{10,1... | collective-permute-start | bytes 737288 | tf_op jit(solution)/shard_map/ppermute | solution.py:496
  6.2 11.2 %collective-permute-start.3 = (f32[2,80,256]{2,1,0:T(8,128)}, f32[2,80,256]{2,1,0:T(8,128)}, u32[]{:S(2)}, u32[]{:S(2)}) collective-permute-start(f32[2,80,256]{2,1,0:T(8,128)} %get-tuple-element.14.down_ref), channel_id=1, source_target_pairs={{0,3},{1,0},{2,1},{3,2},{4,7},{5,4},{6,5},{7,6},{8,11},{9,8},{10,9... | collective-permute-start | bytes 491528 | tf_op jit(solution)/shard_map/ppermute | solution.py:497
  11.9 3.8 %collective-permute-start = (f32[32,384]{1,0:T(8,128)}, f32[32,384]{1,0:T(8,128)}, u32[]{:S(2)}, u32[]{:S(2)}) collective-permute-start(f32[32,384]{1,0:T(8,128)} %pack_columns.1.side_ref), channel_id=1, source_target_pairs={{0,4},{4,8},{8,12},{12,0},{1,5},{5,9},{9,13},{13,1},{2,6},{6,10},{... | collective-permute-start | bytes 147464 | tf_op jit(solution)/shard_map/ppermute | solution.py:499
  11.9 3.8 %collective-permute-start.1 = (f32[32,384]{1,0:T(8,128)}, f32[32,384]{1,0:T(8,128)}, u32[]{:S(2)}, u32[]{:S(2)}) collective-permute-start(f32[32,384]{1,0:T(8,128)} %pack_columns.1.side_ref), channel_id=1, source_target_pairs={{0,12},{4,0},{8,4},{12,8},{1,13},{5,1},{9,5},{13,9},{2,14},{6,2},{... | collective-permute-start | bytes 147464 | tf_op jit(solution)/shard_map/ppermute | solution.py:500
  46.2 5.8 %collective-permute-start.7 = (f32[16,128]{1,0:T(8,128)}, f32[16,128]{1,0:T(8,128)S(1)}, u32[]{:S(2)}, u32[]{:S(2)}) collective-permute-start(f32[16,128]{1,0:T(8,128)} %get-tuple-element.20), channel_id=1, source_target_pairs={{0,1},{1,2},{2,3},{3,0},{4,5},{5,6},{6,7},{7,4},{8,9},{9,10},{10,1... | collective-permute-start | bytes 24584 | tf_op jit(solution)/shard_map/ppermute | solution.py:513
  47.4 6.1 %collective-permute-start.8 = (f32[16,128]{1,0:T(8,128)}, f32[16,128]{1,0:T(8,128)S(1)}, u32[]{:S(2)}, u32[]{:S(2)}) collective-permute-start(f32[16,128]{1,0:T(8,128)} %get-tuple-element.20), channel_id=1, source_target_pairs={{0,2},{1,3},{2,0},{3,1},{4,6},{5,7},{6,4},{7,5},{8,10},{9,11},{10,... | collective-permute-start | bytes 24584 | tf_op jit(solution)/shard_map/ppermute | solution.py:513
  49.1 4.3 %collective-permute-start.9 = (f32[16,128]{1,0:T(8,128)}, f32[16,128]{1,0:T(8,128)S(1)}, u32[]{:S(2)}, u32[]{:S(2)}) collective-permute-start(f32[16,128]{1,0:T(8,128)} %get-tuple-element.20), channel_id=1, source_target_pairs={{0,3},{1,0},{2,1},{3,2},{4,7},{5,4},{6,5},{7,6},{8,11},{9,8},{10,9... | collective-permute-start | bytes 24584 | tf_op jit(solution)/shard_map/ppermute | solution.py:513
  50.4 9.1 %collective-permute-start.4 = (f32[8,16,128]{2,1,0:T(8,128)}, f32[8,16,128]{2,1,0:T(8,128)}, u32[]{:S(2)}, u32[]{:S(2)}) collective-permute-start(f32[8,16,128]{2,1,0:T(8,128)} %get-tuple-element.17), channel_id=1, source_target_pairs={{0,4},{4,8},{8,12},{12,0},{1,5},{5,9},{9,13},{13,1},{2,6},{6,10},{... | collective-permute-start | bytes 196616 | tf_op jit(solution)/shard_map/ppermute | solution.py:509
  50.4 9.1 %collective-permute-start.5 = (f32[8,16,128]{2,1,0:T(8,128)}, f32[8,16,128]{2,1,0:T(8,128)}, u32[]{:S(2)}, u32[]{:S(2)}) collective-permute-start(f32[8,16,128]{2,1,0:T(8,128)} %get-tuple-element.18), channel_id=1, source_target_pairs={{0,8},{4,12},{8,0},{12,4},{1,9},{5,13},{9,1},{13,5},{2,10},{6,14},... | collective-permute-start | bytes 196616 | tf_op jit(solution)/shard_map/ppermute | solution.py:509
  52.0 7.5 %collective-permute-start.6 = (f32[8,16,128]{2,1,0:T(8,128)}, f32[8,16,128]{2,1,0:T(8,128)}, u32[]{:S(2)}, u32[]{:S(2)}) collective-permute-start(f32[8,16,128]{2,1,0:T(8,128)} %get-tuple-element.19), channel_id=1, source_target_pairs={{0,12},{4,0},{8,4},{12,8},{1,13},{5,1},{9,5},{13,9},{2,14},{6,2},{... | collective-permute-start | bytes 196616 | tf_op jit(solution)/shard_map/ppermute | solution.py:509
  53.4 1.2 %collective-permute-start.10 = (f32[16,128]{1,0:T(8,128)S(1)}, f32[16,128]{1,0:T(8,128)S(1)}, u32[]{:S(2)}, u32[]{:S(2)}) collective-permute-start(f32[16,128]{1,0:T(8,128)S(1)} %select_add_fusion), channel_id=1, source_target_pairs={{0,4},{4,0},{8,12},{12,8},{1,5},{5,1},{9,13},{13,9},{2,6},{6,2},{1... | collective-permute-start | bytes 24584 | tf_op jit(solution)/shard_map/ppermute | solution.py:519
  54.7 0.6 copy-start
  55.3 3.7 %collective-permute-start.11 = (f32[16,128]{1,0:T(8,128)S(1)}, f32[16,128]{1,0:T(8,128)S(1)}, u32[]{:S(2)}, u32[]{:S(2)}) collective-permute-start(f32[16,128]{1,0:T(8,128)S(1)} %add.11.refs_4_), channel_id=1, source_target_pairs={{0,8},{4,12},{8,0},{12,4},{1,9},{5,13},{9,1},{13,5},{2,10},{6,14},... | collective-permute-start | bytes 24584 | tf_op jit(solution)/shard_map/ppermute | solution.py:519
  58.9 0.6 copy-start.1
